TPU v7x, 32 devices: a whole 2x2x4 slice. The times are simulated.
32 devices in a mesh: gz: 4 (over z), gy: 2 (over y), gx: 4 (over x, core).
Axes of the slice: x: 2, y: 2, z: 4, core: 2. Of those that a mesh axis runs over, the one named last changes fastest.
Arguments:
- side_field: float32 [2, 192, 64, 512], P(None, 'gz', 'gy', 'gx'), may hold values from -6 to 6
- magnetogram: float32 [64, 512], P('gy', 'gx'), may hold values from -6 to 6
Outputs:
- potential: float32 [3, 192, 64, 512], P(None, 'gz', 'gy', 'gx')
All inputs are finite; a program needn't handle non-finite values.
Results may differ from a plain program's by a relative error of at most 0.000021.
Values sent between devices are 32-bit elements; how exact they have to be, the bound alone decides.
No kernel may reach another device: no remote copies, remote signals or barrier semaphores. Data moves between devices by JAX's collectives and lax.ppermute only.
A program may use at most 64 MiB of HBM per device.

v0:
```python
import jax
import jax.numpy as jnp
from jax import lax
from jax.sharding import PartitionSpec as P

spacing = 0.0625
friction = 0.004


def entering(part, axis, combine, identity):
    place = lax.axis_index(axis)
    gathered = lax.all_gather(part, axis)
    state = jnp.zeros_like(part) + jnp.asarray(identity, part.dtype)

    def one(hop, state):
        return combine(state, lax.dynamic_index_in_dim(gathered, hop, 0, False))

    return lax.fori_loop(0, place, one, state)


def with_halo(block, sides, width):
    for axis, dim in sides:
        count = lax.axis_size(axis)
        forward = [(i, i + 1) for i in range(count - 1)]
        backward = [(target, source) for source, target in forward]
        low = lax.ppermute(
            lax.slice_in_dim(block, block.shape[dim] - width, None, axis=dim), axis, forward
        )
        high = lax.ppermute(lax.slice_in_dim(block, 0, width, axis=dim), axis, backward)
        block = jnp.concatenate([low, block, high], axis=dim)
    return block


def forward_parts(values):
    anchor = values[:-1, :-1, :-1]
    return (
        values[1:, :-1, :-1] - anchor,
        values[:-1, 1:, :-1] - anchor,
        values[:-1, :-1, 1:] - anchor,
    )


def backward_parts(values):
    corner = values[1:, 1:, 1:]
    return (
        corner - values[:-1, 1:, 1:],
        corner - values[1:, :-1, 1:],
        corner - values[1:, 1:, :-1],
    )


def advance(padded):
    along_x = forward_parts(padded[0])
    along_y = forward_parts(padded[1])
    along_z = forward_parts(padded[2])
    field_x = (along_z[1] - along_y[0]) / spacing
    field_y = (along_x[0] - along_z[2]) / spacing
    field_z = (along_y[2] - along_x[1]) / spacing
    back_x = backward_parts(field_x)
    back_y = backward_parts(field_y)
    back_z = backward_parts(field_z)
    current_x = (back_z[1] - back_y[0]) / spacing
    current_y = (back_x[0] - back_z[2]) / spacing
    current_z = (back_y[2] - back_x[1]) / spacing
    cell_x = field_x[1:, 1:, 1:]
    cell_y = field_y[1:, 1:, 1:]
    cell_z = field_z[1:, 1:, 1:]
    denominator = cell_x * cell_x + cell_y * cell_y + cell_z * cell_z + 1.0
    speed_x = (current_y * cell_z - current_z * cell_y) / denominator
    speed_y = (current_z * cell_x - current_x * cell_z) / denominator
    speed_z = (current_x * cell_y - current_y * cell_x) / denominator
    drive_x = speed_y * cell_z - speed_z * cell_y
    drive_y = speed_z * cell_x - speed_x * cell_z
    drive_z = speed_x * cell_y - speed_y * cell_x
    inner = padded[:, 1:-1, 1:-1, 1:-1]
    return inner + friction * jnp.stack([drive_x, drive_y, drive_z])


def add_up(earlier, later):
    return earlier + later


def inside(count, device_index, device_count):
    first = device_index * count - 1
    position = first + jnp.arange(count + 2, dtype=jnp.int32)
    return ((position >= 0) & (position < count * device_count)).astype(jnp.float32)


def local(side_field, magnetogram):
    half = 0.5 * spacing
    rows_sum = jnp.cumsum(magnetogram, axis=1)
    row_totals = rows_sum[:, -1]
    row_carry = entering(row_totals, "gx", add_up, jnp.zeros_like(row_totals))
    base_y = half * (rows_sum + row_carry[:, None])
    columns_sum = jnp.cumsum(magnetogram, axis=0)
    column_totals = columns_sum[-1]
    column_carry = entering(column_totals, "gy", add_up, jnp.zeros_like(column_totals))
    base_x = -half * (columns_sum + column_carry[None, :])
    vertical = jnp.cumsum(side_field, axis=1)
    totals = vertical[:, -1]
    below = entering(totals, "gz", add_up, jnp.zeros_like(totals))
    rising = vertical + below[:, None]
    potential = jnp.stack(
        [
            base_x[None] + spacing * rising[1],
            base_y[None] - spacing * rising[0],
            jnp.zeros_like(rising[0]),
        ]
    )
    depth_z, depth_y, depth_x = (potential.shape[1], potential.shape[2], potential.shape[3])
    width = 2
    padded = with_halo(potential, (("gz", 1), ("gy", 2), ("gx", 3)), width)
    widened = advance(padded)
    mask_z = inside(depth_z, lax.axis_index("gz"), lax.axis_size("gz"))
    mask_y = inside(depth_y, lax.axis_index("gy"), lax.axis_size("gy"))
    mask_x = inside(depth_x, lax.axis_index("gx"), lax.axis_size("gx"))
    valid = mask_z[:, None, None] * mask_y[None, :, None] * mask_x[None, None, :]
    widened = widened * valid[None]
    potential = advance(widened)
    return potential


def solution(mesh):
    return jax.shard_map(
        local,
        mesh=mesh,
        in_specs=(P(None, "gz", "gy", "gx"), P("gy", "gx")),
        out_specs=P(None, "gz", "gy", "gx"),
        check_vma=False,
    )
```

profile of v0, /device:TPU:0, one launch (start us, length us, event | category | flops | bytes accessed | tf_op | source)
XLA Modules:
  0.0 124.5 jit_solution(14785904796519646486)
XLA Ops:
  0.0 1.1 reduce_window_sum.35
  1.1 0.2 slice_reduce_fusion
  1.3 1.3 %dynamic-slice = u32[1]{0:T(128)} dynamic-slice(u32[32]{0:T(128)} %constant.102, u32[]{:T(128)S(6)} %add.158), dynamic_slice_sizes={1} | dynamic-slice | bytes 12
  3.2 0.2 dynamic-update-slice
  3.5 8.3 %all-reduce = f32[128]{0:T(128)S(1)} all-reduce(f32[128]{0:T(128)S(1)} %dynamic-update-slice), channel_id=3, replica_groups=mesh['gz'=4,'gy'=2,'gx'=4] {'gx'}, use_global_device_ids=true, to_apply=%add | all-reduce | flops 128 | bytes 1024
  11.8 0.1 reshape.93
  11.9 0.1 add_multiply_fusion
  12.0 8.3 %fusion.36 = f32[2,48,32,128]{3,2,1,0:T(8,128)S(1)} fusion(f32[2,48,32,128]{3,2,1,0:T(8,128)S(1)} %copy-done), kind=kOutput, calls=%fused_computation.103 | output fusion | flops 18481152 | bytes 3145728 | tf_op jit(solution)/shard_map/jit(cumsum)/reduce_window_sum | solution.py:99
  20.3 0.0 copy-start.4
  20.3 13.6 %all-gather = f32[8,1,32,128]{3,2,1,0:T(8,128)S(1)} all-gather(f32[2,1,32,128]{3,2,1,0:T(8,128)S(1)} %slice.227), channel_id=2, replica_groups=mesh['gz'=4,'gy'=2,'gx'=4] {'gz'}, dimensions={0}, use_global_device_ids=true | all-gather | bytes 163840 | tf_op jit(solution)/shard_map/all_gather | solution.py:12
  34.0 1.3 %broadcast_add_fusion = f32[2,48,32,128]{3,2,1,0:T(8,128)} fusion(f32[2,48,32,128]{3,2,1,0:T(8,128)S(1)} %fusion.36, f32[2,32,128]{2,1,0:T(8,128)S(1)} %get-tuple-element.75), kind=kLoop, calls=%fused_computation.85 | loop fusion | flops 393216 | bytes 3178496 | tf_op jit(solution)/shard_map/add | solution.py:102
  35.3 0.1 reduce_window_sum.33
  35.3 4.2 %all-gather.2 = f32[2,1,128]{2,1,0:T(1,128)S(1)} all-gather(f32[1,1,128]{2,1,0:T(1,128)S(1)} %slice_bitcast_fusion.6), channel_id=1, replica_groups=mesh['gz'=4,'gy'=2,'gx'=4] {'gy'}, dimensions={0}, use_global_device_ids=true | all-gather | bytes 1536 | tf_op jit(solution)/shard_map/all_gather | solution.py:12
  39.6 1.6 %fusion.27 = (f32[1,48,32,128]{3,2,1,0:T(8,128)S(1)}, f32[1,48,32,128]{3,2,1,0:T(8,128)S(1)}) fusion(f32[2,48,32,128]{3,2,1,0:T(8,128)} %broadcast_add_fusion, f32[32,128]{1,0:T(8,128)S(1)} %add_multiply_fusion.1, f32[32,128]{1,0:T(8,128)S(1)} %add_multiply_fusion), kind=kLoop, calls=%fused_computation.76 | loop fusion | flops 786432 | bytes 3178496 | tf_op jit(solution)/shard_map/add | solution.py:105
  41.1 0.1 stack_broadcast_in_dim.3
  41.2 3.5 %collective-permute-start = (f32[3,2,32,128]{3,2,1,0:T(8,128)S(1)}, f32[3,2,32,128]{3,2,1,0:T(8,128)S(1)}, u32[]{:S(2)}, u32[]{:S(2)}) collective-permute-start(f32[3,2,32,128]{3,2,1,0:T(8,128)S(1)} %get-tuple-element.123), channel_id=1, source_target_pairs={{0,8},{8,16},{16,24},{1,9},{9,17},{17,25},{2,10},{10,18},{18,26},{... | collective-permute-start | bytes 294920 | tf_op jit(solution)/shard_map/ppermute | solution.py:26
  44.8 1.3 %collective-permute-start.1 = (f32[3,2,32,128]{3,2,1,0:T(8,128)S(1)}, f32[3,2,32,128]{3,2,1,0:T(8,128)S(1)}, u32[]{:S(2)}, u32[]{:S(2)}) collective-permute-start(f32[3,2,32,128]{3,2,1,0:T(8,128)S(1)} %get-tuple-element.124), channel_id=1, source_target_pairs={{8,0},{16,8},{24,16},{9,1},{17,9},{25,17},{10,2},{18,10},{26,18},{... | collective-permute-start | bytes 294920 | tf_op jit(solution)/shard_map/ppermute | solution.py:29
  46.1 0.9 collective-permute-done
  47.0 4.3 %collective-permute-done.1 = f32[3,2,32,128]{3,2,1,0:T(8,128)S(1)} collective-permute-done((f32[3,2,32,128]{3,2,1,0:T(8,128)S(1)}, f32[3,2,32,128]{3,2,1,0:T(8,128)S(1)}, u32[]{:S(2)}, u32[]{:S(2)}) %collective-permute-start.1) | collective-permute-done | bytes 98336 | tf_op jit(solution)/shard_map/ppermute | solution.py:29
  51.3 0.1 pad_maximum_fusion.6
  51.4 3.5 %collective-permute-start.2 = (f32[3,52,2,128]{3,2,1,0:T(2,128)S(1)}, f32[3,52,2,128]{3,2,1,0:T(2,128)S(1)}, u32[]{:S(2)}, u32[]{:S(2)}) collective-permute-start(f32[3,52,2,128]{3,2,1,0:T(2,128)S(1)} %get-tuple-element.121), channel_id=1, source_target_pairs={{0,4},{1,5},{2,6},{3,7},{8,12},{9,13},{10,14},{11,15},{16,20},{17,... | collective-permute-start | bytes 479240 | tf_op jit(solution)/shard_map/ppermute | solution.py:26
  54.9 1.3 %collective-permute-start.3 = (f32[3,52,2,128]{3,2,1,0:T(2,128)S(1)}, f32[3,52,2,128]{3,2,1,0:T(2,128)S(1)}, u32[]{:S(2)}, u32[]{:S(2)}) collective-permute-start(f32[3,52,2,128]{3,2,1,0:T(2,128)S(1)} %get-tuple-element.122), channel_id=1, source_target_pairs={{4,0},{5,1},{6,2},{7,3},{12,8},{13,9},{14,10},{15,11},{20,16},{21,... | collective-permute-start | bytes 479240 | tf_op jit(solution)/shard_map/ppermute | solution.py:29
  56.2 0.1 broadcast_multiply_fusion.1
  56.3 1.4 %collective-permute-done.2 = f32[3,52,2,128]{3,2,1,0:T(2,128)S(1)} collective-permute-done((f32[3,52,2,128]{3,2,1,0:T(2,128)S(1)}, f32[3,52,2,128]{3,2,1,0:T(2,128)S(1)}, u32[]{:S(2)}, u32[]{:S(2)}) %collective-permute-start.2) | collective-permute-done | bytes 159776 | tf_op jit(solution)/shard_map/ppermute | solution.py:26
  57.6 4.4 %collective-permute-done.3 = f32[3,52,2,128]{3,2,1,0:T(2,128)S(1)} collective-permute-done((f32[3,52,2,128]{3,2,1,0:T(2,128)S(1)}, f32[3,52,2,128]{3,2,1,0:T(2,128)S(1)}, u32[]{:S(2)}, u32[]{:S(2)}) %collective-permute-start.3) | collective-permute-done | bytes 159776 | tf_op jit(solution)/shard_map/ppermute | solution.py:29
  62.0 0.5 pad_maximum_fusion.1
  62.5 3.7 %fusion.35 = (f32[3,52,36,2]{3,2,1,0:T(8,128)}, f32[3,52,36,2]{3,2,1,0:T(8,128)}) fusion(f32[3,52,36,128]{3,2,1,0:T(8,128)S(1)} %pad_maximum_fusion.1), kind=kLoop, calls=%fused_computation.102 | loop fusion | bytes 179712 | tf_op jit(solution)/shard_map/slice | solution.py:27
  66.2 3.1 %copy.3 = f32[3,52,36,2]{1,3,2,0:T(2,128)S(1)} copy(f32[3,52,36,2]{3,2,1,0:T(8,128)} %get-tuple-element.119) | data formatting | bytes 89856 | tf_op jit(solution)/shard_map/slice | solution.py:27
  69.4 1.3 %collective-permute-start.4 = (f32[3,52,36,2]{1,3,2,0:T(2,128)S(1)}, f32[3,52,36,2]{1,3,2,0:T(2,128)S(1)}, u32[]{:S(2)}, u32[]{:S(2)}) collective-permute-start(f32[3,52,36,2]{1,3,2,0:T(2,128)S(1)} %copy.3), channel_id=1, source_target_pairs={{0,1},{1,2},{2,3},{4,5},{5,6},{6,7},{8,9},{9,10},{10,11},{12,13},{... | collective-permute-start | bytes 134792 | tf_op jit(solution)/shard_map/ppermute | solution.py:26
  70.7 3.2 %copy.4 = f32[3,52,36,2]{1,3,2,0:T(2,128)S(1)} copy(f32[3,52,36,2]{3,2,1,0:T(8,128)} %get-tuple-element.120) | data formatting | bytes 89856 | tf_op jit(solution)/shard_map/slice | solution.py:29
  73.9 1.5 %collective-permute-start.5 = (f32[3,52,36,2]{1,3,2,0:T(2,128)S(1)}, f32[3,52,36,2]{1,3,2,0:T(2,128)S(1)}, u32[]{:S(2)}, u32[]{:S(2)}) collective-permute-start(f32[3,52,36,2]{1,3,2,0:T(2,128)S(1)} %copy.4), channel_id=1, source_target_pairs={{1,0},{2,1},{3,2},{5,4},{6,5},{7,6},{9,8},{10,9},{11,10},{13,12},{... | collective-permute-start | bytes 134792 | tf_op jit(solution)/shard_map/ppermute | solution.py:29
  75.3 1.6 %broadcast_multiply_fusion = f32[50,34,130]{2,1,0:T(8,128)} fusion(f32[130]{0:T(256)S(1)} %and_convert_fusion, f32[50,34]{1,0:T(8,128)S(1)} %broadcast_multiply_fusion.1), kind=kLoop, calls=%fused_computation.60 | loop fusion | flops 221000 | bytes 891320 | tf_op jit(solution)/shard_map/mul | solution.py:117
  77.0 2.8 %copy.5 = f32[3,52,36,2]{3,2,1,0:T(8,128)} copy(f32[3,52,36,2]{1,3,2,0:T(2,128)S(1)} %collective-permute-done.4) | data formatting | bytes 89856 | tf_op jit(solution)/shard_map/ppermute | solution.py:26
  79.8 2.9 %copy.6 = f32[3,52,36,2]{3,2,1,0:T(8,128)} copy(f32[3,52,36,2]{1,3,2,0:T(2,128)S(1)} %collective-permute-done.5) | data formatting | bytes 89856 | tf_op jit(solution)/shard_map/ppermute | solution.py:29
  82.7 9.5 %pad_maximum_fusion = f32[3,52,36,132]{3,2,1,0:T(8,128)S(1)} fusion(f32[3,52,36,2]{3,2,1,0:T(8,128)} %copy.6, f32[3,52,2,128]{3,2,1,0:T(2,128)S(1)} %collective-permute-done.3, f32[3,2,32,128]{3,2,1,0:T(8,128)S(1)} %collective-permute-done.1, f32[1,48,32,128]{3,2,1,0:T(8,128)S(1)} %stack_broadcast_in_dim.3, f32[1,48,32,128]{3,2,1,0:T(8,128)S(1)} %get-tuple-element.132, ...), kind=kLoop, calls=%fused_computation.3 | loop fusion | flops 5930496 | bytes 5930496 | tf_op jit(solution)/shard_map/concatenate | solution.py:30
  92.1 0.4 slice_bitcast_fusion.1
  92.6 2.3 %fusion.6 = (f32[51,35,131]{2,1,0:T(8,128)S(1)}, f32[51,35,131]{2,1,0:T(8,128)S(1)}, f32[51,35,131]{2,1,0:T(8,128)S(1)}) fusion(f32[52,36,132]{2,1,0:T(8,128)S(1)} %get-tuple-element.113, f32[52,36,132]{2,1,0:T(8,128)S(1)} %get-tuple-element.115, f32[52,36,132]{2,1,0:T(8,128)S(1)} %get-tuple-element.114), kind=kLoop, calls=%fused_computation.23 | loop fusion | flops 2806020 | bytes 11224080 | tf_op jit(solution)/shard_map/div | solution.py:57
  94.9 4.5 %subtract_bitcast_fusion.2 = (f32[1,50,34,130]{3,2,1,0:T(8,128)S(1)}, f32[50,34,130]{2,1,0:T(8,128)S(1)}, f32[50,34,130]{2,1,0:T(8,128)S(1)}, f32[50,34,130]{2,1,0:T(8,128)S(1)}) fusion(f32[51,35,131]{2,1,0:T(8,128)S(1)} %get-tuple-element.126, f32[51,35,131]{2,1,0:T(8,128)S(1)} %get-tuple-element.127, f32[51,35,131]{2,1,0:T(8,128)S(1)} %get-tuple-element.125), kind=kLoop, calls=%fused_computation.43 | loop fusion | flops 6409000 | bytes 11492000 | tf_op jit(solution)/shard_map/stack | solution.py:76
  99.4 0.0 copy-start.3
  99.4 2.8 %subtract_bitcast_fusion.1 = (f32[1,50,34,130]{3,2,1,0:T(8,128)S(1)}, f32[1,50,34,130]{3,2,1,0:T(8,128)S(1)}) fusion(f32[50,34,130]{2,1,0:T(8,128)S(1)} %get-tuple-element.108, f32[50,34,130]{2,1,0:T(8,128)S(1)} %get-tuple-element.107, f32[50,34,130]{2,1,0:T(8,128)S(1)} %get-tuple-element.106, f32[51,35,131]{2,1,0:T(8,128)S(1)} %get-tuple-element.126, ...), kind=kLoop, calls=%fused_computation.41 | loop fusion | flops 5304000 | bytes 7072000 | tf_op jit(solution)/shard_map/stack | solution.py:76
  102.3 1.9 %fusion = f32[3,50,34,130]{3,2,1,0:T(8,128)S(1)} fusion(f32[3,52,36,132]{3,2,1,0:T(8,128)S(1)} %pad_maximum_fusion, f32[1,50,34,130]{3,2,1,0:T(8,128)S(1)} %get-tuple-element.110, f32[1,50,34,130]{3,2,1,0:T(8,128)S(1)} %get-tuple-element.109, f32[1,50,34,130]{3,2,1,0:T(8,128)S(1)} %get-tuple-element.105, f32[50,34,130]{2,1,0:T(8,128)S(1)} %copy-done.3), kind=kLoop, calls=%fused_computation.5 | loop fusion | flops 3315000 | bytes 8840000 | tf_op jit(solution)/shard_map/mul | solution.py:118
  104.2 0.4 slice_bitcast_fusion.4
  104.6 2.2 %copy-done.2 = f32[3,50,34,130]{3,2,1,0:T(8,128)} copy-done((f32[3,50,34,130]{3,2,1,0:T(8,128)}, f32[3,50,34,130]{3,2,1,0:T(8,128)S(1)}, u32[]{:S(2)}) %copy-start.2) | copy-done | bytes 2652024
  106.7 3.4 %fusion.19 = (f32[49,33,129]{2,1,0:T(8,128)S(1)}, f32[49,33,129]{2,1,0:T(8,128)}, f32[49,33,129]{2,1,0:T(8,128)}) fusion(f32[50,34,130]{2,1,0:T(8,128)S(1)} %get-tuple-element.116, f32[50,34,130]{2,1,0:T(8,128)S(1)} %get-tuple-element.118, f32[50,34,130]{2,1,0:T(8,128)S(1)} %get-tuple-element.117), kind=kLoop, calls=%fused_computation.58 | loop fusion | flops 2503116 | bytes 10012464 | tf_op jit(solution)/shard_map/div | solution.py:57
  110.2 5.9 %subtract_bitcast_fusion.5 = (f32[1,48,32,128]{3,2,1,0:T(8,128)S(1)}, f32[48,32,128]{2,1,0:T(8,128)S(1)}, f32[48,32,128]{2,1,0:T(8,128)S(1)}, f32[48,32,128]{2,1,0:T(8,128)S(1)}) fusion(f32[49,33,129]{2,1,0:T(8,128)} %get-tuple-element.129, f32[49,33,129]{2,1,0:T(8,128)} %get-tuple-element.130, f32[49,33,129]{2,1,0:T(8,128)S(1)} %get-tuple-element.128), kind=kLoop, calls=%fused_computation.80 | loop fusion | flops 5701632 | bytes 10223616 | tf_op jit(solution)/shard_map/stack | solution.py:76
  116.1 3.4 %subtract_bitcast_fusion.4 = (f32[1,48,32,128]{3,2,1,0:T(8,128)S(1)}, f32[1,48,32,128]{3,2,1,0:T(8,128)S(1)}) fusion(f32[48,32,128]{2,1,0:T(8,128)S(1)} %get-tuple-element.104, f32[48,32,128]{2,1,0:T(8,128)S(1)} %get-tuple-element.103, f32[48,32,128]{2,1,0:T(8,128)S(1)} %get-tuple-element.102, f32[49,33,129]{2,1,0:T(8,128)} %get-tuple-element.129, ...), kind=kLoop, calls=%fused_computation.78 | loop fusion | flops 4718592 | bytes 6291456 | tf_op jit(solution)/shard_map/stack | solution.py:76
  119.4 0.0 copy-start.1
  119.5 5.0 %slice_add_fusion.1 = f32[3,48,32,128]{3,2,1,0:T(8,128)} fusion(f32[3,50,34,130]{3,2,1,0:T(8,128)} %copy-done.2, f32[1,48,32,128]{3,2,1,0:T(8,128)S(1)} %get-tuple-element.112, f32[1,48,32,128]{3,2,1,0:T(8,128)S(1)} %get-tuple-element.111, f32[1,48,32,128]{3,2,1,0:T(8,128)S(1)} %get-tuple-element.101), kind=kLoop, calls=%fused_computation.8 | loop fusion | flops 2359296 | bytes 7077888 | tf_op jit(solution)/shard_map/add | solution.py:76
  (22 shorter events, 0.1 us)
Async XLA Ops:
  0.0 12.0 %copy-start = (f32[2,48,32,128]{3,2,1,0:T(8,128)S(1)}, f32[2,48,32,128]{3,2,1,0:T(8,128)}, u32[]{:S(2)}) copy-start(f32[2,48,32,128]{3,2,1,0:T(8,128)} %param.8) | copy-start | bytes 4718596
  20.3 15.0 %copy-start.4 = (f32[32,128]{1,0:T(8,128)S(1)}, f32[32,128]{1,0:T(8,128)}, u32[]{:S(2)}) copy-start(f32[32,128]{1,0:T(8,128)} %param.9) | copy-start | bytes 49156
  41.2 5.7 %collective-permute-start = (f32[3,2,32,128]{3,2,1,0:T(8,128)S(1)}, f32[3,2,32,128]{3,2,1,0:T(8,128)S(1)}, u32[]{:S(2)}, u32[]{:S(2)}) collective-permute-start(f32[3,2,32,128]{3,2,1,0:T(8,128)S(1)} %get-tuple-element.123), channel_id=1, source_target_pairs={{0,8},{8,16},{16,24},{1,9},{9,17},{17,25},{2,10},{10,18},{18,26},{... | collective-permute-start | bytes 294920 | tf_op jit(solution)/shard_map/ppermute | solution.py:26
  44.8 6.5 %collective-permute-start.1 = (f32[3,2,32,128]{3,2,1,0:T(8,128)S(1)}, f32[3,2,32,128]{3,2,1,0:T(8,128)S(1)}, u32[]{:S(2)}, u32[]{:S(2)}) collective-permute-start(f32[3,2,32,128]{3,2,1,0:T(8,128)S(1)} %get-tuple-element.124), channel_id=1, source_target_pairs={{8,0},{16,8},{24,16},{9,1},{17,9},{25,17},{10,2},{18,10},{26,18},{... | collective-permute-start | bytes 294920 | tf_op jit(solution)/shard_map/ppermute | solution.py:29
  51.4 6.2 %collective-permute-start.2 = (f32[3,52,2,128]{3,2,1,0:T(2,128)S(1)}, f32[3,52,2,128]{3,2,1,0:T(2,128)S(1)}, u32[]{:S(2)}, u32[]{:S(2)}) collective-permute-start(f32[3,52,2,128]{3,2,1,0:T(2,128)S(1)} %get-tuple-element.121), channel_id=1, source_target_pairs={{0,4},{1,5},{2,6},{3,7},{8,12},{9,13},{10,14},{11,15},{16,20},{17,... | collective-permute-start | bytes 479240 | tf_op jit(solution)/shard_map/ppermute | solution.py:26
  54.9 7.2 %collective-permute-start.3 = (f32[3,52,2,128]{3,2,1,0:T(2,128)S(1)}, f32[3,52,2,128]{3,2,1,0:T(2,128)S(1)}, u32[]{:S(2)}, u32[]{:S(2)}) collective-permute-start(f32[3,52,2,128]{3,2,1,0:T(2,128)S(1)} %get-tuple-element.122), channel_id=1, source_target_pairs={{4,0},{5,1},{6,2},{7,3},{12,8},{13,9},{14,10},{15,11},{20,16},{21,... | collective-permute-start | bytes 479240 | tf_op jit(solution)/shard_map/ppermute | solution.py:29
  69.4 7.6 %collective-permute-start.4 = (f32[3,52,36,2]{1,3,2,0:T(2,128)S(1)}, f32[3,52,36,2]{1,3,2,0:T(2,128)S(1)}, u32[]{:S(2)}, u32[]{:S(2)}) collective-permute-start(f32[3,52,36,2]{1,3,2,0:T(2,128)S(1)} %copy.3), channel_id=1, source_target_pairs={{0,1},{1,2},{2,3},{4,5},{5,6},{6,7},{8,9},{9,10},{10,11},{12,13},{... | collective-permute-start | bytes 134792 | tf_op jit(solution)/shard_map/ppermute | solution.py:26
  73.9 5.9 %collective-permute-start.5 = (f32[3,52,36,2]{1,3,2,0:T(2,128)S(1)}, f32[3,52,36,2]{1,3,2,0:T(2,128)S(1)}, u32[]{:S(2)}, u32[]{:S(2)}) collective-permute-start(f32[3,52,36,2]{1,3,2,0:T(2,128)S(1)} %copy.4), channel_id=1, source_target_pairs={{1,0},{2,1},{3,2},{5,4},{6,5},{7,6},{9,8},{10,9},{11,10},{13,12},{... | collective-permute-start | bytes 134792 | tf_op jit(solution)/shard_map/ppermute | solution.py:29
  99.4 2.8 %copy-start.3 = (f32[50,34,130]{2,1,0:T(8,128)S(1)}, f32[50,34,130]{2,1,0:T(8,128)}, u32[]{:S(2)}) copy-start(f32[50,34,130]{2,1,0:T(8,128)} %broadcast_multiply_fusion) | copy-start | bytes 2652004
  104.1 2.6 %copy-start.2 = (f32[3,50,34,130]{3,2,1,0:T(8,128)}, f32[3,50,34,130]{3,2,1,0:T(8,128)S(1)}, u32[]{:S(2)}) copy-start(f32[3,50,34,130]{3,2,1,0:T(8,128)S(1)} %fusion) | copy-start | bytes 7956004
  119.4 5.0 %copy-start.1 = (f32[2,48,32,128]{3,2,1,0:T(8,128)S(1)}, f32[2,48,32,128]{3,2,1,0:T(8,128)}, u32[]{:S(2)}) copy-start(f32[2,48,32,128]{3,2,1,0:T(8,128)} %param.8) | copy-start | bytes 4718596
where the time goes:
time: 126 us; the launch traced here: 124 us
  other arithmetic  53.5 us (42%)
  blocking collectives  26.2 us (21%)
  local copies, waits for them, and re-layouts  20.6 us (16%)
  starting transfers between devices  12.3 us (10%)
  waiting for transfers between devices  11 us (9%)
    all_gather x2, blocking collectives, entering(): gathered = lax.all_gather(part, axis)  17.8 us
    another operation x4, other arithmetic, advance(): return inner + friction * jnp.stack([drive_x, drive_y, drive_z])  16.6 us
    concatenate x2, other arithmetic, with_halo(): block = jnp.concatenate([low, block, high], axis=dim)  9.95 us
    ppermute x3, waiting for transfers between devices, with_halo(): lax.ppermute(lax.slice_in_dim(block, 0, width, axis=dim), axis, backward)  8.72 us
    another operation x1, other arithmetic, local(): vertical = jnp.cumsum(side_field, axis=1)  8.34 us
    unnamed x1, blocking collectives  8.31 us
    ppermute x3, starting transfers between devices, with_halo(): lax.ppermute(lax.slice_in_dim(block, block.shape[dim] - width, None, axis...  8.28 us
    slice x2, local copies, waits for them, and re-layouts, with_halo(): lax.slice_in_dim(block, block.shape[dim] - width, None, axis=dim)  6.84 us
  transfers between devices with their start and end apart: 6, of which 4 were waited for; matrix products, arithmetic and copies ran while one was open for 6% of the time, Pallas kernels for 0%

commit v1 on v0

v1 whole, which is shorter than its diff:
```python
import functools

import jax
import jax.numpy as jnp
from jax import lax
from jax.experimental import pallas as pl
from jax.experimental.pallas import tpu as pltpu
from jax.sharding import PartitionSpec as P

spacing = 0.0625
friction = 0.004
gain = friction / (spacing * spacing)
LANES = 128
PAD = 8
GROUP = LANES // 4


def near(index, count):
    return (index + 1) % count if index % 2 else (index - 1) % count


def swap(part, axis, partner):
    count = lax.axis_size(axis)
    return lax.ppermute(part, axis, [(i, partner(i)) for i in range(count)])


def swap_first(part, axis):
    return swap(part, axis, lambda i: i ^ 1)


def swap_second(part, axis):
    count = lax.axis_size(axis)
    return swap(part, axis, lambda i: near(i, count))


def far_steps(count):
    return [2] if count == 4 else list(range(2, count))


def lane_index(shape):
    return lax.broadcasted_iota(jnp.int32, shape, len(shape) - 1)


def row_index(shape):
    return lax.broadcasted_iota(jnp.int32, shape, len(shape) - 2)


def columns_at(values, slot):
    first = 4 * (slot % GROUP)
    rolled = pltpu.roll(values, (first + 2) % LANES, 1)
    lane = lane_index(values.shape)
    return jnp.where((lane >= first) & (lane < first + 4), rolled, 0.0)


def spread(values, first):
    lane = lane_index(values.shape)
    moved = pltpu.roll(values, (LANES - first) % LANES, 1) if first else values
    result = jnp.where(lane < 4, moved, 0.0)
    step = 4
    while step < LANES:
        result = result + pltpu.roll(result, step, 1)
        step *= 2
    return result


def totals_kernel(place, side, mag, first_out, second_out, total_out, rows_out, columns_out):
    depth = side.shape[1]
    z = place[0]
    for c in range(2):
        low0 = side[c, 0]
        low1 = low0 + side[c, 1]
        before = low1
        for layer in range(2, depth - 1):
            before = before + side[c, layer]
        total = before + side[c, depth - 1]
        odd = z % 2 == 1
        first_out[c, 0] = jnp.where(odd, low0, before)
        first_out[c, 1] = jnp.where(odd, low1, total)
        upward = odd | (z == 0)
        second_out[c, 0] = jnp.where(upward, before, low0)
        second_out[c, 1] = jnp.where(upward, total, low1)
        total_out[c] = total
    rows = mag[...]
    lane = lane_index(rows.shape)
    step = 1
    while step < LANES:
        rows = rows + jnp.where(lane >= step, pltpu.roll(rows, step, 1), 0.0)
        step *= 2
    rows_out[...] = rows
    columns = mag[...]
    row = row_index(columns.shape)
    step = 1
    while step < columns.shape[0]:
        columns = columns + jnp.where(row >= step, pltpu.roll(columns, step, 0), 0.0)
        step *= 2
    columns_out[...] = columns


def pack_kernel(side, packed_out, rows_out, running):
    depth, height = side.shape[1], side.shape[2]
    for c in range(2):
        total = jnp.zeros(side.shape[2:], jnp.float32)
        packed = [jnp.zeros(side.shape[2:], jnp.float32) for _ in range(2)]
        for layer in range(depth):
            total = total + side[c, layer]
            running[c, pl.ds(layer * height, height), :] = total
            slot = layer + 2
            packed[slot // GROUP] += columns_at(total, slot)
        for tile in range(2):
            packed_out[c, :, pl.ds(tile * LANES, LANES)] = packed[tile]
        for k, row in enumerate((0, 1, height - 2, height - 1)):
            rows_out[c, k] = running[c, pl.ds(row, depth, stride=height), :]


def z_kernel(
    count, depth, far, place, first, second, total, columns, column_carry, rows, packed, *rest
):
    others, (x_out, ext_out, base_out) = rest[:far], rest[far:]
    z, y = place[0], place[1]
    odd = z % 2 == 1
    for c in range(2):
        near_a, near_b = (first[c, 0], first[c, 1]), (second[c, 0], second[c, 1])
        low = [jnp.where(odd, a, b) for a, b in zip(near_a, near_b)]
        high = [jnp.where(odd, b, a) for a, b in zip(near_a, near_b)]
        carry = jnp.where(odd, near_a[1], 0.0)
        if count == 4:
            carry = carry + jnp.where((z == 2) | (z == 3), near_b[1], 0.0)
        for step, other in zip(far_steps(count), others):
            carry = carry + jnp.where((z ^ step) < z, other[c], 0.0)
        above = carry + total[c]
        layers = (carry - (low[1] - low[0]), carry, above + high[0], above + high[1])
        for k in range(4):
            ext_out[c, k] = layers[k]
        if c == 0:
            base = rows[...]
        else:
            base = -0.5 * (columns[...] + jnp.where(y > 0, column_carry[7:8, :], 0.0))
            base_out[...] = base
        lane = lane_index(carry.shape)
        everywhere = spread(pltpu.roll(carry, 2, 1), 0)
        for tile in range(2):
            slot = lane // 4 + tile * GROUP
            values = packed[c, :, pl.ds(tile * LANES, LANES)]
            inside = (slot >= 2) & (slot < depth + 2)
            values = values + jnp.where(inside, everywhere, 0.0)
            for k, at in enumerate((0, 1, depth + 2, depth + 3)):
                if at // GROUP == tile:
                    values = values + columns_at(layers[k], at)
            if (depth + 4) // GROUP == tile:
                values = values + columns_at(base, depth + 4)
            x_out[c, :, pl.ds(tile * LANES, LANES)] = values


def x_kernel(
    counts, depth, place, packed, first, second, far_rows, rows, base, ext, edges,
    strips_out, flat_out, ext_out, y_out,
):
    count_z, count_y, count_x = counts
    height = packed.shape[1]
    z, y, x = place[0], place[1], place[2]
    odd = x % 2 == 1
    base_tile, base_lane = (depth + 4) // GROUP, 4 * ((depth + 4) % GROUP)

    def tile_of(ref, c, tile):
        return ref[c, :, pl.ds(tile * LANES, LANES)]

    def row_totals(ref):
        return tile_of(ref, 0, base_tile)[:, base_lane + 1 : base_lane + 2]

    own_total = rows[...][:, LANES - 1 :]
    total_a, total_b = row_totals(first), row_totals(second)
    far_total = far_rows[...][:, LANES - 1 :]
    if count_x == 2:
        row_carry = jnp.where(odd, total_a, 0.0)
    elif count_x == 4:
        row_carry = jnp.where(odd, total_a, 0.0) + jnp.where(x >= 2, total_b + far_total, 0.0)
    else:
        row_carry = far_total
    left_total = jnp.where(odd, total_a, total_b)

    lane = lane_index((height, LANES))
    q = lane % 4
    for part in range(2):
        merged = []
        for c in range(2):
            tiles = []
            for tile in range(2):
                own, a, b = (tile_of(ref, c, tile) for ref in (packed, first, second))
                if part == 0:
                    tiles.append(jnp.where(q < 2, jnp.where(odd, a, b), own))
                else:
                    tiles.append(jnp.where(q < 2, own, jnp.where(odd, b, a)))
            merged.append(tiles)
        if part == 0:
            carry = jnp.where(q < 2, row_carry - left_total, row_carry)
        else:
            carry = jnp.where(q < 2, row_carry, row_carry + own_total)
        base_y = 0.5 * (spread(merged[0][base_tile], base_lane) + carry)
        base_x = spread(merged[1][base_tile], base_lane)
        for tile in range(2):
            slot = lane // 4 + tile * GROUP
            inside = (slot < depth + 4) & ((slot >= 2) | (z > 0))
            inside = inside & ((slot < depth + 2) | (z < count_z - 1))
            if part == 0:
                inside = inside & ((q >= 2) | (x > 0))
            else:
                inside = inside & ((q < 2) | (x < count_x - 1))
            place_at = pl.ds((part * 2 + tile) * LANES, LANES)
            strips_out[0, :, place_at] = jnp.where(inside, base_x + merged[1][tile], 0.0)
            strips_out[1, :, place_at] = jnp.where(inside, base_y - merged[0][tile], 0.0)

    base_x = base[...]
    base_y = 0.5 * (rows[...] + row_carry)
    flat_out[0] = base_x + ext[1, 1]
    flat_out[1] = base_y - ext[0, 1]
    for k in range(4):
        inside = (z > 0) if k < 2 else (z < count_z - 1)
        ext_out[0, k] = jnp.where(inside, base_x + ext[1, k], 0.0)
        ext_out[1, k] = jnp.where(inside, base_y - ext[0, k], 0.0)

    slots = slot_rows(depth)
    for message in range(y_out.shape[0]):
        downward = (y % 2 == 1) if message == 0 else (y % 2 == 0)
        for c in range(2):
            for r in range(2):
                start = (c * 2 + r) * slots
                low, high = pl.ds(r, 1), pl.ds(height - 2 + r, 1)
                flat = jnp.where(downward, flat_out[c, low, :], flat_out[c, high, :])
                edge = jnp.where(downward, edges[1 - c, r], edges[1 - c, 2 + r])
                edge = edge if c == 0 else -edge
                y_out[message, pl.ds(start + 2, depth), :] = flat + edge
                for k, at in enumerate((0, 1, depth + 2, depth + 3)):
                    y_out[message, pl.ds(start + at, 1), :] = jnp.where(
                        downward, ext_out[c, k, low, :], ext_out[c, k, high, :]
                    )
            for tile in range(4):
                start = 4 * slots + (c * 4 + tile) * 2
                lanes = pl.ds(tile * LANES, LANES)
                y_out[message, pl.ds(start, 2), :] = jnp.where(
                    downward,
                    strips_out[c, pl.ds(0, 2), lanes],
                    strips_out[c, pl.ds(height - 2, 2), lanes],
                )


def slot_rows(depth):
    return (depth + 4 + 7) // 8 * 8


def following(values, axis, step=1):
    return pltpu.roll(values, values.shape[axis] - step, axis)


def preceding(values, axis, step=1):
    return pltpu.roll(values, step, axis)


def push(a, field, current):
    square = field[0] * field[0] + field[1] * field[1] + field[2] * field[2]
    along = current[0] * field[0] + current[1] * field[1] + current[2] * field[2]
    factor = gain / (square + 1.0)
    p, q = along * factor, square * factor
    return [a[c] + (field[c] * p - current[c] * q) for c in range(3)]


def strip_field(a):
    x, y, z = a
    field_x = following(z, 0) - z - (following(y, 1, 4) - y)
    field_y = following(x, 1, 4) - x - (following(z, 1) - z)
    field_z = following(y, 1) - y - (following(x, 0) - x)
    return field_x, field_y, field_z


def strip_current(b):
    x, y, z = b
    current_x = z - preceding(z, 0) - (y - preceding(y, 1, 4))
    current_y = x - preceding(x, 1, 4) - (z - preceding(z, 1))
    current_z = y - preceding(y, 1) - (x - preceding(x, 0))
    return current_x, current_y, current_z


def step_kernel(
    counts, place, side, flat, ext, strips, first, second, out, state, field, later, halo, wide
):
    count_z, count_y, count_x = counts
    depth, height = side.shape[1], side.shape[2]
    z, y, x = place[0], place[1], place[2]
    slots = slot_rows(depth)
    layers = depth + 4
    padded = state.shape[2]
    odd = y % 2 == 1

    sums = [jnp.zeros((height, LANES), jnp.float32) for _ in range(2)]
    rows = pl.ds(PAD, height)
    for c in range(2):
        for k, at in enumerate((0, 1, depth + 2, depth + 3)):
            state[c, at, rows, :] = ext[c, k]

    def fill(layer, sums):
        sums = [total + side[c, layer] for c, total in enumerate(sums)]
        state[0, layer + 2, rows, :] = flat[0] + sums[1]
        state[1, layer + 2, rows, :] = flat[1] - sums[0]
        return sums

    lax.fori_loop(0, depth, fill, sums)

    for low in (True, False):
        exists = (y > 0) if low else (y < count_y - 1)
        row = PAD - 2 if low else PAD + height
        for c in range(2):
            flat_state = state.at[c].reshape(layers * padded, LANES)
            for r in range(2):
                take = pl.ds((c * 2 + r) * slots, layers)
                a, b = first[take, :], second[take, :]
                value = jnp.where(odd, a, b) if low else jnp.where(odd, b, a)
                flat_state[pl.ds(row + r, layers, stride=padded), :] = jnp.where(exists, value, 0.0)
            for tile in range(4):
                take = pl.ds(4 * slots + (c * 4 + tile) * 2, 2)
                a, b = first[take, :], second[take, :]
                value = jnp.where(odd, a, b) if low else jnp.where(odd, b, a)
                wide[c, pl.ds(row, 2), pl.ds(tile * LANES, LANES)] = jnp.where(exists, value, 0.0)
    wide[0, rows, :] = strips[0]
    wide[1, rows, :] = strips[1]

    half = 2 * LANES
    lane = lane_index((padded, 2 * half))
    row = row_index((padded, 2 * half))
    q = lane % 4
    slot = (lane % half) // 4
    right = lane >= half
    inside = (row >= PAD - 2) & (row < PAD + height + 2) & (slot < layers)
    inside = inside & ((row >= PAD) | (y > 0)) & ((row < PAD + height) | (y < count_y - 1))
    inside = inside & ((slot >= 2) | (z > 0)) & ((slot < depth + 2) | (z < count_z - 1))
    inside = inside & (right | (q >= 2) | (x > 0))
    inside = inside & (~right | (q < 2) | (x < count_x - 1))
    a = [jnp.where(inside, wide[c], 0.0) for c in range(2)]
    a.append(jnp.zeros_like(a[0]))
    b = strip_field(a)
    pick = (lane_index((padded, half)) % 4) == 2

    def keep(at, upper, lower):
        value = jnp.where(pick, upper[:, half:], lower[:, :half])
        halo[at, 0] = value[:, :LANES]
        halo[at, 1] = value[:, LANES:]

    keep(0, a[1], b[1])
    keep(1, a[2], b[2])
    a = [jnp.where(inside, value, 0.0) for value in push(a, b, strip_current(b))]
    b = strip_field(a)
    keep(2, a[1], b[1])
    keep(3, a[2], b[2])

    lane = lane_index((8, LANES))
    last, start = lane == LANES - 1, lane == 0

    def beside(at, layer, row):
        shift = LANES - 2 - 4 * (layer % GROUP)
        return pltpu.roll(halo[at, layer // GROUP, pl.ds(row, 8), :], shift, 1)

    def right_of(value, edge):
        return following(jnp.where(start, edge, value), 1)

    def left_of(value, edge):
        return preceding(jnp.where(last, edge, value), 1)

    def load(ref, c, layer, row):
        return ref[c, layer, pl.ds(row, 8), :]

    def first_field(layer, _):
        for tile in range(5):
            r = PAD - 2 + 8 * tile
            ax, ay = load(state, 0, layer, r), load(state, 1, layer, r)
            ay_right = right_of(ay, beside(0, layer, r))
            to = pl.ds(r, 8)
            field[0, layer, to, :] = ay - load(state, 1, layer + 1, r)
            field[1, layer, to, :] = load(state, 0, layer + 1, r) - ax
            field[2, layer, to, :] = ay_right - ay - (load(state, 0, layer, r + 1) - ax)
        return 0

    def currents(layer, r, at):
        bx, by, bz = (load(field, c, layer, r) for c in range(3))
        by_left = left_of(by, beside(at, layer, r))
        bz_left = left_of(bz, beside(at + 1, layer, r))
        jx = bz - load(field, 2, layer, r - 1) - (by - load(field, 1, layer - 1, r))
        jy = bx - load(field, 0, layer - 1, r) - (bz - bz_left)
        jz = by - by_left - (bx - load(field, 0, layer, r - 1))
        return (bx, by, bz), (jx, jy, jz)

    def first_push(layer, _):
        for tile in range(5):
            r = PAD - 1 + 8 * tile
            b, j = currents(layer, r, 0)
            a = [load(state, c, layer, r) for c in range(2)]
            a.append(jnp.zeros_like(a[0]))
            for c, value in enumerate(push(a, b, j)):
                later[c, layer, pl.ds(r, 8), :] = value
        return 0

    def second_field(layer, _):
        for tile in range(5):
            r = PAD - 1 + 8 * tile
            ax, ay, az = (load(later, c, layer, r) for c in range(3))
            ay_right = right_of(ay, beside(2, layer, r))
            az_right = right_of(az, beside(3, layer, r))
            to = pl.ds(r, 8)
            field[0, layer, to, :] = (
                load(later, 2, layer, r + 1) - az - (load(later, 1, layer + 1, r) - ay)
            )
            field[1, layer, to, :] = load(later, 0, layer + 1, r) - ax - (az_right - az)
            field[2, layer, to, :] = ay_right - ay - (load(later, 0, layer, r + 1) - ax)
        return 0

    def second_push(layer, _):
        for tile in range(height // 8):
            r = PAD + 8 * tile
            b, j = currents(layer, r, 2)
            a = [load(later, c, layer, r) for c in range(3)]
            for c, value in enumerate(push(a, b, j)):
                out[c, layer - 2, pl.ds(8 * tile, 8), :] = spacing * value
        return 0

    lax.fori_loop(0, depth + 3, first_field, 0)
    lax.fori_loop(1, depth + 3, first_push, 0)

    zeros = jnp.zeros((height + 8, LANES), jnp.float32)
    line = jnp.zeros((layers, LANES), jnp.float32)
    for c in range(3):
        for exists, layer in ((z > 0, 1), (z < count_z - 1, depth + 2)):

            @pl.when(jnp.logical_not(exists))
            def _():
                later[c, layer, pl.ds(PAD - 1, height + 8), :] = zeros

        for exists, row in ((y > 0, PAD - 1), (y < count_y - 1, PAD + height)):

            @pl.when(jnp.logical_not(exists))
            def _():
                flat_later = later.at[c].reshape(layers * padded, LANES)
                flat_later[pl.ds(row, layers, stride=padded), :] = line

    lax.fori_loop(1, depth + 2, second_field, 0)
    lax.fori_loop(2, depth + 2, second_push, 0)


def call(kernel, shapes, args, scratch=(), limit=16):
    vmem = pl.BlockSpec(memory_space=pltpu.VMEM)
    return pl.pallas_call(
        kernel,
        out_shape=[jax.ShapeDtypeStruct(shape, jnp.float32) for shape in shapes],
        in_specs=[pl.BlockSpec(memory_space=pltpu.SMEM)] + [vmem] * (len(args) - 1),
        out_specs=[vmem] * len(shapes),
        scratch_shapes=[pltpu.VMEM(shape, jnp.float32) for shape in scratch],
        compiler_params=pltpu.CompilerParams(vmem_limit_bytes=limit * 2**20),
    )(*args)


def gathered_carries(rows, columns):
    height, width = rows.shape
    x, y = lax.axis_index("gx"), lax.axis_index("gy")
    row_totals = lax.all_gather(rows[:, -1], "gx")
    before = (jnp.arange(row_totals.shape[0]) < x)[:, None]
    row_carry = jnp.sum(jnp.where(before, row_totals, 0.0), axis=0)
    column_totals = lax.all_gather(columns[-1], "gy")
    before = (jnp.arange(column_totals.shape[0]) < y)[:, None]
    column_carry = jnp.sum(jnp.where(before, column_totals, 0.0), axis=0)
    return (
        jnp.broadcast_to(row_carry[:, None], (height, width)),
        jnp.broadcast_to(column_carry[None], (8, width)),
    )


def local(side, mag):
    counts = tuple(lax.axis_size(axis) for axis in ("gz", "gy", "gx"))
    count_z, count_y, count_x = counts
    _, depth, height, width = side.shape
    place = jnp.stack([lax.axis_index(axis) for axis in ("gz", "gy", "gx")]).astype(jnp.int32)
    plane, block = (height, width), (2, height, width)

    first, second, total, rows, columns = call(
        totals_kernel, [(2, 2) + plane, (2, 2) + plane, block, plane, plane], [place, side, mag]
    )
    first = swap_first(first, "gz")
    second = swap_second(second, "gz") if count_z > 2 else first
    others = [
        swap(total, "gz", functools.partial(lambda step, i: i ^ step, step))
        for step in far_steps(count_z)
    ]
    direct = count_y == 2 and count_x in (2, 4)
    if direct:
        column_carry = swap_first(columns[-8:], "gy")
    else:
        row_carry, column_carry = gathered_carries(rows, columns)
    packed, edges = call(
        lambda _, *refs: pack_kernel(*refs),
        [(2, height, 2 * LANES), (2, 4, depth, width)],
        [place, side],
        [(2, depth * height, width)],
    )
    far = len(others)
    packed, ext, base = call(
        functools.partial(z_kernel, count_z, depth, far),
        [(2, height, 2 * LANES), (2, 4) + plane, plane],
        [place, first, second, total, columns, column_carry, rows, packed, *others],
    )
    first = swap_first(packed, "gx")
    second = swap_second(packed, "gx") if count_x > 2 else first
    if not direct:
        far_rows = row_carry
    elif count_x == 4:
        far_rows = swap(rows, "gx", lambda i: i ^ 2)
    else:
        far_rows = rows
    messages = 1 if count_y == 2 else 2
    message_rows = 4 * slot_rows(depth) + 16
    strips, flat, ext, edge_rows = call(
        functools.partial(x_kernel, counts, depth),
        [(2, height, 4 * LANES), block, (2, 4) + plane, (messages, message_rows, width)],
        [place, packed, first, second, far_rows, rows, base, ext, edges],
    )
    first = swap_first(edge_rows[0], "gy")
    second = swap_second(edge_rows[1], "gy") if count_y > 2 else first
    layers, padded = depth + 4, height + 2 * PAD
    (result,) = call(
        functools.partial(step_kernel, counts),
        [(3, depth) + plane],
        [place, side, flat, ext, strips, first, second],
        [
            (2, layers, padded, width),
            (3, layers, padded, width),
            (3, layers, padded, width),
            (4, 2, padded, LANES),
            (2, padded, 4 * LANES),
        ],
        limit=24,
    )
    return result


def solution(mesh):
    return jax.shard_map(
        local,
        mesh=mesh,
        in_specs=(P(None, "gz", "gy", "gx"), P("gy", "gx")),
        out_specs=P(None, "gz", "gy", "gx"),
        check_vma=False,
    )
```

time: 126 us -> 60.9 us (0.48)
  other arithmetic: 53.5 us -> 0.08 us
  Pallas kernels: 0 us -> 38.4 us
  blocking collectives: 26.2 us -> 0 us
  local copies, waits for them, and re-layouts: 20.6 us -> 2.13 us
  waiting for transfers between devices: 11 us -> 8.99 us
  starting transfers between devices: 12.3 us -> 11 us
    pallas_call x0 -> x5, Pallas kernels: none -> 38.4 us  [call(): pl.pallas_call(kernel, out_shape=[jax.ShapeDtypeStruct(shape, jnp.float32...]
    another operation x7 -> x1, other arithmetic: 26.1 us -> 0.08 us  [local(): jnp.stack([lax.axis_index(axis) for axis in ('gz', 'gy', 'gx')])]
    all_gather x2 -> x0, blocking collectives: 17.8 us -> none  [entering(): gathered = lax.all_gather(part, axis)]
    slice x5 -> x1, local copies, waits for them, and re-layouts: 10.2 us -> 0.01 us  [local(): column_carry = swap_first(columns[-8:], 'gy')]
    concatenate x2 -> x0, other arithmetic: 9.95 us -> none  [with_halo(): block = jnp.concatenate([low, block, high], axis=dim)]
    unnamed x1 -> x0, blocking collectives: 8.31 us -> none
    add x3 -> x0, other arithmetic: 7.88 us -> none  [the longest x1 5.01 us: advance(): return inner + friction * jnp.stack([drive_x, drive_y, drive_z])]
    div x2 -> x0, other arithmetic: 5.71 us -> none  [advance(): field_y = (along_x[0] - along_z[2]) / spacing]
  transfers between devices with their start and end apart: 6 -> 8, of which waited for: 4 -> 4; matrix products, arithmetic and copies ran while one was open for 6% -> 0% of each run, Pallas kernels for 0% -> 2%
where the time goes in v1:
time: 60.9 us; the launch traced here: 60.6 us
  Pallas kernels  38.4 us (63%)
  starting transfers between devices  11 us (18%)
  waiting for transfers between devices  8.99 us (15%)
  local copies, waits for them, and re-layouts  2.13 us (3%)
    pallas_call x5, Pallas kernels, call(): pl.pallas_call(kernel, out_shape=[jax.ShapeDtypeStruct(shape, jnp.float32...  38.4 us
    ppermute x8, starting transfers between devices, swap(): return lax.ppermute(part, axis, [(i, partner(i)) for i in range(count)])  11 us
    ppermute x8, waiting for transfers between devices, swap(): return lax.ppermute(part, axis, [(i, partner(i)) for i in range(count)])  8.99 us
    unnamed x6, local copies, waits for them, and re-layouts  2.13 us
  transfers between devices with their start and end apart: 8, of which 4 were waited for; matrix products, arithmetic and copies ran while one was open for 0% of the time, Pallas kernels for 2%

profile of v1, /device:TPU:0, one launch (start us, length us, event | category | flops | bytes accessed | tf_op | source)
XLA Modules:
  0.0 60.6 jit_solution(11744963614800000696)
XLA Ops:
  0.0 0.1 pad_add_fusion.place._
  0.1 0.0 copy-start
  0.1 1.4 %copy-done = f32[2,48,32,128]{3,2,1,0:T(8,128)S(1)} copy-done((f32[2,48,32,128]{3,2,1,0:T(8,128)S(1)}, f32[2,48,32,128]{3,2,1,0:T(8,128)}, u32[]{:S(2)}) %copy-start) | copy-done | bytes 1572888
  1.5 0.0 copy-start.2
  1.5 0.7 %copy-done.2 = f32[32,128]{1,0:T(8,128)S(1)} copy-done((f32[32,128]{1,0:T(8,128)S(1)}, f32[32,128]{1,0:T(8,128)}, u32[]{:S(2)}) %copy-start.2) | copy-done | bytes 16408
  2.2 0.0 copy-start.1
  2.2 1.0 %shard_map.28 = (f32[2,2,32,128]{3,2,1,0:T(8,128)S(1)}, f32[2,2,32,128]{3,2,1,0:T(8,128)S(1)}, f32[2,32,128]{2,1,0:T(8,128)S(1)}, f32[32,128]{1,0:T(8,128)S(1)}, f32[32,128]{1,0:T(8,128)S(1)}) custom-call(s32[3]{0:T(128)S(1)} %pad_add_fusion.place._, f32[2,48,32,128]{3,2,1,0:T(8,128)S(1)} %copy-done, f32[32,128]{1,0:T(8,128)S(1)} %copy-done.2), custom_call_target="tpu_custom_call" | custom-call | tf_op jit(solution)/shard_map/pallas_call | solution.py:447
  3.2 3.1 %collective-permute-start = (f32[2,2,32,128]{3,2,1,0:T(8,128)S(1)}, f32[2,2,32,128]{3,2,1,0:T(8,128)S(1)}, u32[]{:S(2)}, u32[]{:S(2)}) collective-permute-start(f32[2,2,32,128]{3,2,1,0:T(8,128)S(1)} %get-tuple-element.19), channel_id=1, source_target_pairs={{0,8},{8,0},{16,24},{24,16},{1,9},{9,1},{17,25},{25,17},{2,10},{10... | collective-permute-start | bytes 196616 | tf_op jit(solution)/shard_map/ppermute | solution.py:24
  6.3 2.5 %collective-permute-start.1 = (f32[2,2,32,128]{3,2,1,0:T(8,128)S(1)}, f32[2,2,32,128]{3,2,1,0:T(8,128)S(1)}, u32[]{:S(2)}, u32[]{:S(2)}) collective-permute-start(f32[2,2,32,128]{3,2,1,0:T(8,128)S(1)} %get-tuple-element.20), channel_id=1, source_target_pairs={{0,24},{8,16},{16,8},{24,0},{1,25},{9,17},{17,9},{25,1},{2,26},{10... | collective-permute-start | bytes 196616 | tf_op jit(solution)/shard_map/ppermute | solution.py:24
  8.8 0.1 collective-permute-start.3
  8.9 1.5 %collective-permute-start.2 = (f32[8,128]{1,0:T(8,128)S(1)}, f32[8,128]{1,0:T(8,128)S(1)}, u32[]{:S(2)}, u32[]{:S(2)}) collective-permute-start(f32[8,128]{1,0:T(8,128)S(1)} %slice.3), channel_id=1, source_target_pairs={{0,4},{4,0},{1,5},{5,1},{2,6},{6,2},{3,7},{7,3},{8,12},{12,8},{9,1... | collective-permute-start | bytes 12296 | tf_op jit(solution)/shard_map/ppermute | solution.py:24
  10.4 1.1 %shard_map.29 = (f32[2,32,256]{2,1,0:T(8,128)S(1)}, f32[2,4,48,128]{3,2,1,0:T(8,128)S(1)}) custom-call(s32[3]{0:T(128)S(1)} %pad_add_fusion.place._, f32[2,48,32,128]{3,2,1,0:T(8,128)S(1)} %copy-done), custom_call_target="tpu_custom_call" | custom-call | tf_op jit(solution)/shard_map/pallas_call | solution.py:447
  11.5 1.0 %collective-permute-done.2.column_carry = f32[8,128]{1,0:T(8,128)S(1)} collective-permute-done((f32[8,128]{1,0:T(8,128)S(1)}, f32[8,128]{1,0:T(8,128)S(1)}, u32[]{:S(2)}, u32[]{:S(2)}) %collective-permute-start.2) | collective-permute-done | bytes 4128 | tf_op jit(solution)/shard_map/ppermute | solution.py:24
  12.5 1.4 %collective-permute-done.3.rest_0_ = f32[2,32,128]{2,1,0:T(8,128)S(1)} collective-permute-done((f32[2,32,128]{2,1,0:T(8,128)S(1)}, f32[2,32,128]{2,1,0:T(8,128)S(1)}, u32[]{:S(2)}, u32[]{:S(2)}) %collective-permute-start.3) | collective-permute-done | bytes 32800 | tf_op jit(solution)/shard_map/ppermute | solution.py:24
  13.9 0.0 collective-permute-done.first
  13.9 0.0 collective-permute-done.1.second
  13.9 1.0 %shard_map.30 = (f32[2,32,256]{2,1,0:T(8,128)S(1)}, f32[2,4,32,128]{3,2,1,0:T(8,128)S(1)}, f32[32,128]{1,0:T(8,128)S(1)}) custom-call(s32[3]{0:T(128)S(1)} %pad_add_fusion.place._, f32[2,2,32,128]{3,2,1,0:T(8,128)S(1)} %collective-permute-done.first, f32[2,2,32,128]{3,2,1,0:T(8,128)S(1)} %collective-permute-done.1.second, ...), custom_call_target="tpu_custom_call" | custom-call | tf_op jit(solution)/shard_map/pallas_call | solution.py:447
  14.9 0.2 collective-permute-start.5
  15.1 1.5 %collective-permute-start.4 = (f32[2,32,256]{2,1,0:T(8,128)S(1)}, f32[2,32,256]{2,1,0:T(8,128)S(1)}, u32[]{:S(2)}, u32[]{:S(2)}) collective-permute-start(f32[2,32,256]{2,1,0:T(8,128)S(1)} %get-tuple-element.25.packed), channel_id=1, source_target_pairs={{0,1},{1,0},{2,3},{3,2},{4,5},{5,4},{6,7},{7,6},{8,9},{9,8},{10,11... | collective-permute-start | bytes 196616 | tf_op jit(solution)/shard_map/ppermute | solution.py:24
  16.6 0.5 collective-permute-start.6
  17.1 3.2 %collective-permute-done.6.far_rows = f32[32,128]{1,0:T(8,128)S(1)} collective-permute-done((f32[32,128]{1,0:T(8,128)S(1)}, f32[32,128]{1,0:T(8,128)S(1)}, u32[]{:S(2)}, u32[]{:S(2)}) %collective-permute-start.6) | collective-permute-done | bytes 16416 | tf_op jit(solution)/shard_map/ppermute | solution.py:24
  20.3 0.0 collective-permute-done.5.second
  20.3 0.0 collective-permute-done.4.first
  20.3 1.0 %shard_map.31 = (f32[2,32,512]{2,1,0:T(8,128)S(1)}, f32[2,32,128]{2,1,0:T(8,128)S(1)}, f32[2,4,32,128]{3,2,1,0:T(8,128)S(1)}, f32[1,240,128]{2,1,0:T(8,128)S(1)}) custom-call(s32[3]{0:T(128)S(1)} %pad_add_fusion.place._, f32[2,32,256]{2,1,0:T(8,128)S(1)} %get-tuple-element.25.packed, f32[2,32,256]{2,1,0:T(8,128)S(1)} %collective-permute-done.4.first, ...), custom_call_target="tpu_custom_call" | custom-call | tf_op jit(solution)/shard_map/pallas_call | solution.py:447
  21.3 1.6 %collective-permute-start.7 = (f32[240,128]{1,0:T(8,128)S(1)}, f32[240,128]{1,0:T(8,128)S(1)}, u32[]{:S(2)}, u32[]{:S(2)}) collective-permute-start(f32[240,128]{1,0:T(8,128)S(1)} %bitcast.4), channel_id=1, source_target_pairs={{0,4},{4,0},{1,5},{5,1},{2,6},{6,2},{3,7},{7,3},{8,12},{12,8},{9,1... | collective-permute-start | bytes 368648 | tf_op jit(solution)/shard_map/ppermute | solution.py:24
  22.9 3.4 %collective-permute-done.7.first.second = f32[240,128]{1,0:T(8,128)S(1)} collective-permute-done((f32[240,128]{1,0:T(8,128)S(1)}, f32[240,128]{1,0:T(8,128)S(1)}, u32[]{:S(2)}, u32[]{:S(2)}) %collective-permute-start.7) | collective-permute-done | bytes 122912 | tf_op jit(solution)/shard_map/ppermute | solution.py:24
  26.3 0.0 copy-done.1
  26.3 34.3 %shard_map.32 = f32[3,48,32,128]{3,2,1,0:T(8,128)} custom-call(s32[3]{0:T(128)S(1)} %pad_add_fusion.place._, f32[2,48,32,128]{3,2,1,0:T(8,128)S(1)} %copy-done.1, f32[2,32,128]{2,1,0:T(8,128)S(1)} %get-tuple-element.29.flat, f32[2,4,32,128]{3,2,1,0:T(8,128)S(1)} %get-tuple-element.30.ext, f32[2,32,512]{2,1,0:T(8,128)S(1)} %get-tuple-element.31.strips, ...), custom_call_target="tpu_custom_call" | custom-call | tf_op jit(solution)/shard_map/pallas_call | solution.py:447
  (1 shorter events, 0.0 us)
Async XLA Ops:
  0.1 1.4 %copy-start = (f32[2,48,32,128]{3,2,1,0:T(8,128)S(1)}, f32[2,48,32,128]{3,2,1,0:T(8,128)}, u32[]{:S(2)}) copy-start(f32[2,48,32,128]{3,2,1,0:T(8,128)} %side.3) | copy-start | bytes 4718596
  1.5 0.7 %copy-start.2 = (f32[32,128]{1,0:T(8,128)S(1)}, f32[32,128]{1,0:T(8,128)}, u32[]{:S(2)}) copy-start(f32[32,128]{1,0:T(8,128)} %mag.1) | copy-start | bytes 49156
  2.2 24.1 %copy-start.1 = (f32[2,48,32,128]{3,2,1,0:T(8,128)S(1)}, f32[2,48,32,128]{3,2,1,0:T(8,128)}, u32[]{:S(2)}) copy-start(f32[2,48,32,128]{3,2,1,0:T(8,128)} %side.3) | copy-start | bytes 4718596
  3.2 10.7 %collective-permute-start = (f32[2,2,32,128]{3,2,1,0:T(8,128)S(1)}, f32[2,2,32,128]{3,2,1,0:T(8,128)S(1)}, u32[]{:S(2)}, u32[]{:S(2)}) collective-permute-start(f32[2,2,32,128]{3,2,1,0:T(8,128)S(1)} %get-tuple-element.19), channel_id=1, source_target_pairs={{0,8},{8,0},{16,24},{24,16},{1,9},{9,1},{17,25},{25,17},{2,10},{10... | collective-permute-start | bytes 196616 | tf_op jit(solution)/shard_map/ppermute | solution.py:24
  6.3 7.6 %collective-permute-start.1 = (f32[2,2,32,128]{3,2,1,0:T(8,128)S(1)}, f32[2,2,32,128]{3,2,1,0:T(8,128)S(1)}, u32[]{:S(2)}, u32[]{:S(2)}) collective-permute-start(f32[2,2,32,128]{3,2,1,0:T(8,128)S(1)} %get-tuple-element.20), channel_id=1, source_target_pairs={{0,24},{8,16},{16,8},{24,0},{1,25},{9,17},{17,9},{25,1},{2,26},{10... | collective-permute-start | bytes 196616 | tf_op jit(solution)/shard_map/ppermute | solution.py:24
  8.8 5.2 %collective-permute-start.3 = (f32[2,32,128]{2,1,0:T(8,128)S(1)}, f32[2,32,128]{2,1,0:T(8,128)S(1)}, u32[]{:S(2)}, u32[]{:S(2)}) collective-permute-start(f32[2,32,128]{2,1,0:T(8,128)S(1)} %get-tuple-element.21.total), channel_id=1, source_target_pairs={{0,16},{8,24},{16,0},{24,8},{1,17},{9,25},{17,1},{25,9},{2,18},{10... | collective-permute-start | bytes 98312 | tf_op jit(solution)/shard_map/ppermute | solution.py:24
  8.9 3.6 %collective-permute-start.2 = (f32[8,128]{1,0:T(8,128)S(1)}, f32[8,128]{1,0:T(8,128)S(1)}, u32[]{:S(2)}, u32[]{:S(2)}) collective-permute-start(f32[8,128]{1,0:T(8,128)S(1)} %slice.3), channel_id=1, source_target_pairs={{0,4},{4,0},{1,5},{5,1},{2,6},{6,2},{3,7},{7,3},{8,12},{12,8},{9,1... | collective-permute-start | bytes 12296 | tf_op jit(solution)/shard_map/ppermute | solution.py:24
  14.9 5.4 %collective-permute-start.5 = (f32[2,32,256]{2,1,0:T(8,128)S(1)}, f32[2,32,256]{2,1,0:T(8,128)S(1)}, u32[]{:S(2)}, u32[]{:S(2)}) collective-permute-start(f32[2,32,256]{2,1,0:T(8,128)S(1)} %get-tuple-element.25.packed), channel_id=1, source_target_pairs={{0,3},{1,2},{2,1},{3,0},{4,7},{5,6},{6,5},{7,4},{8,11},{9,10},{10,... | collective-permute-start | bytes 196616 | tf_op jit(solution)/shard_map/ppermute | solution.py:24
  15.1 5.3 %collective-permute-start.4 = (f32[2,32,256]{2,1,0:T(8,128)S(1)}, f32[2,32,256]{2,1,0:T(8,128)S(1)}, u32[]{:S(2)}, u32[]{:S(2)}) collective-permute-start(f32[2,32,256]{2,1,0:T(8,128)S(1)} %get-tuple-element.25.packed), channel_id=1, source_target_pairs={{0,1},{1,0},{2,3},{3,2},{4,5},{5,4},{6,7},{7,6},{8,9},{9,8},{10,11... | collective-permute-start | bytes 196616 | tf_op jit(solution)/shard_map/ppermute | solution.py:24
  16.6 3.7 %collective-permute-start.6 = (f32[32,128]{1,0:T(8,128)S(1)}, f32[32,128]{1,0:T(8,128)S(1)}, u32[]{:S(2)}, u32[]{:S(2)}) collective-permute-start(f32[32,128]{1,0:T(8,128)S(1)} %get-tuple-element.23.rows), channel_id=1, source_target_pairs={{0,2},{1,3},{2,0},{3,1},{4,6},{5,7},{6,4},{7,5},{8,10},{9,11},{10,... | collective-permute-start | bytes 49160 | tf_op jit(solution)/shard_map/ppermute | solution.py:24
  21.3 4.9 %collective-permute-start.7 = (f32[240,128]{1,0:T(8,128)S(1)}, f32[240,128]{1,0:T(8,128)S(1)}, u32[]{:S(2)}, u32[]{:S(2)}) collective-permute-start(f32[240,128]{1,0:T(8,128)S(1)} %bitcast.4), channel_id=1, source_target_pairs={{0,4},{4,0},{1,5},{5,1},{2,6},{6,2},{3,7},{7,3},{8,12},{12,8},{9,1... | collective-permute-start | bytes 368648 | tf_op jit(solution)/shard_map/ppermute | solution.py:24

commit v2 on v1

--- a/solution.py
+++ b/solution.py
@@ -296,13 +296,10 @@
         for k, at in enumerate((0, 1, depth + 2, depth + 3)):
             state[c, at, rows, :] = ext[c, k]
 
-    def fill(layer, sums):
+    for layer in range(depth):
         sums = [total + side[c, layer] for c, total in enumerate(sums)]
         state[0, layer + 2, rows, :] = flat[0] + sums[1]
         state[1, layer + 2, rows, :] = flat[1] - sums[0]
-        return sums
-
-    lax.fori_loop(0, depth, fill, sums)
 
     for low in (True, False):
         exists = (y > 0) if low else (y < count_y - 1)
@@ -366,7 +363,7 @@
     def load(ref, c, layer, row):
         return ref[c, layer, pl.ds(row, 8), :]
 
-    def first_field(layer, _):
+    def first_field(layer):
         for tile in range(5):
             r = PAD - 2 + 8 * tile
             ax, ay = load(state, 0, layer, r), load(state, 1, layer, r)
@@ -375,7 +372,6 @@
             field[0, layer, to, :] = ay - load(state, 1, layer + 1, r)
             field[1, layer, to, :] = load(state, 0, layer + 1, r) - ax
             field[2, layer, to, :] = ay_right - ay - (load(state, 0, layer, r + 1) - ax)
-        return 0
 
     def currents(layer, r, at):
         bx, by, bz = (load(field, c, layer, r) for c in range(3))
@@ -386,7 +382,7 @@
         jz = by - by_left - (bx - load(field, 0, layer, r - 1))
         return (bx, by, bz), (jx, jy, jz)
 
-    def first_push(layer, _):
+    def first_push(layer):
         for tile in range(5):
             r = PAD - 1 + 8 * tile
             b, j = currents(layer, r, 0)
@@ -394,9 +390,8 @@
             a.append(jnp.zeros_like(a[0]))
             for c, value in enumerate(push(a, b, j)):
                 later[c, layer, pl.ds(r, 8), :] = value
-        return 0
-
-    def second_field(layer, _):
+
+    def second_field(layer):
         for tile in range(5):
             r = PAD - 1 + 8 * tile
             ax, ay, az = (load(later, c, layer, r) for c in range(3))
@@ -408,19 +403,19 @@
             )
             field[1, layer, to, :] = load(later, 0, layer + 1, r) - ax - (az_right - az)
             field[2, layer, to, :] = ay_right - ay - (load(later, 0, layer, r + 1) - ax)
-        return 0
-
-    def second_push(layer, _):
+
+    def second_push(layer):
         for tile in range(height // 8):
             r = PAD + 8 * tile
             b, j = currents(layer, r, 2)
             a = [load(later, c, layer, r) for c in range(3)]
             for c, value in enumerate(push(a, b, j)):
                 out[c, layer - 2, pl.ds(8 * tile, 8), :] = spacing * value
-        return 0
-
-    lax.fori_loop(0, depth + 3, first_field, 0)
-    lax.fori_loop(1, depth + 3, first_push, 0)
+
+    for layer in range(0, depth + 3):
+        first_field(layer)
+    for layer in range(1, depth + 3):
+        first_push(layer)
 
     zeros = jnp.zeros((height + 8, LANES), jnp.float32)
     line = jnp.zeros((layers, LANES), jnp.float32)
@@ -438,8 +433,10 @@
                 flat_later = later.at[c].reshape(layers * padded, LANES)
                 flat_later[pl.ds(row, layers, stride=padded), :] = line
 
-    lax.fori_loop(1, depth + 2, second_field, 0)
-    lax.fori_loop(2, depth + 2, second_push, 0)
+    for layer in range(1, depth + 2):
+        second_field(layer)
+    for layer in range(2, depth + 2):
+        second_push(layer)
 
 
 def call(kernel, shapes, args, scratch=(), limit=16):

time: 60.9 us -> 33.5 us (0.55)
  Pallas kernels: 38.4 us -> 11 us
    pallas_call x5, Pallas kernels: 38.4 us -> 11 us  [call(): pl.pallas_call(kernel, out_shape=[jax.ShapeDtypeStruct(shape, jnp.float32...]
  transfers between devices with their start and end apart: 8 -> 8, of which waited for: 4 -> 4; matrix products, arithmetic and copies ran while one was open for 0% -> 0% of each run, Pallas kernels for 2% -> 3%
where the time goes in v2:
time: 33.5 us; the launch traced here: 33.2 us
  Pallas kernels  11 us (33%)
  starting transfers between devices  11 us (33%)
  waiting for transfers between devices  8.99 us (27%)
  local copies, waits for them, and re-layouts  2.13 us (6%)
    pallas_call x5, Pallas kernels, call(): pl.pallas_call(kernel, out_shape=[jax.ShapeDtypeStruct(shape, jnp.float32...  11 us
    ppermute x8, starting transfers between devices, swap(): return lax.ppermute(part, axis, [(i, partner(i)) for i in range(count)])  11 us
    ppermute x8, waiting for transfers between devices, swap(): return lax.ppermute(part, axis, [(i, partner(i)) for i in range(count)])  8.99 us
    unnamed x6, local copies, waits for them, and re-layouts  2.13 us
  transfers between devices with their start and end apart: 8, of which 4 were waited for; matrix products, arithmetic and copies ran while one was open for 0% of the time, Pallas kernels for 3%

profile of v2, /device:TPU:0, one launch (start us, length us, event | category | flops | bytes accessed | tf_op | source)
XLA Modules:
  0.0 33.2 jit_solution(10834522882929202196)
XLA Ops:
  0.0 0.1 pad_add_fusion.place._
  0.1 0.0 copy-start
  0.1 1.4 %copy-done = f32[2,48,32,128]{3,2,1,0:T(8,128)S(1)} copy-done((f32[2,48,32,128]{3,2,1,0:T(8,128)S(1)}, f32[2,48,32,128]{3,2,1,0:T(8,128)}, u32[]{:S(2)}) %copy-start) | copy-done | bytes 1572888
  1.5 0.0 copy-start.2
  1.5 0.7 %copy-done.2 = f32[32,128]{1,0:T(8,128)S(1)} copy-done((f32[32,128]{1,0:T(8,128)S(1)}, f32[32,128]{1,0:T(8,128)}, u32[]{:S(2)}) %copy-start.2) | copy-done | bytes 16408
  2.2 0.0 copy-start.1
  2.2 1.0 %shard_map.28 = (f32[2,2,32,128]{3,2,1,0:T(8,128)S(1)}, f32[2,2,32,128]{3,2,1,0:T(8,128)S(1)}, f32[2,32,128]{2,1,0:T(8,128)S(1)}, f32[32,128]{1,0:T(8,128)S(1)}, f32[32,128]{1,0:T(8,128)S(1)}) custom-call(s32[3]{0:T(128)S(1)} %pad_add_fusion.place._, f32[2,48,32,128]{3,2,1,0:T(8,128)S(1)} %copy-done, f32[32,128]{1,0:T(8,128)S(1)} %copy-done.2), custom_call_target="tpu_custom_call" | custom-call | tf_op jit(solution)/shard_map/pallas_call | solution.py:444
  3.2 3.1 %collective-permute-start = (f32[2,2,32,128]{3,2,1,0:T(8,128)S(1)}, f32[2,2,32,128]{3,2,1,0:T(8,128)S(1)}, u32[]{:S(2)}, u32[]{:S(2)}) collective-permute-start(f32[2,2,32,128]{3,2,1,0:T(8,128)S(1)} %get-tuple-element.19), channel_id=1, source_target_pairs={{0,8},{8,0},{16,24},{24,16},{1,9},{9,1},{17,25},{25,17},{2,10},{10... | collective-permute-start | bytes 196616 | tf_op jit(solution)/shard_map/ppermute | solution.py:24
  6.3 2.5 %collective-permute-start.1 = (f32[2,2,32,128]{3,2,1,0:T(8,128)S(1)}, f32[2,2,32,128]{3,2,1,0:T(8,128)S(1)}, u32[]{:S(2)}, u32[]{:S(2)}) collective-permute-start(f32[2,2,32,128]{3,2,1,0:T(8,128)S(1)} %get-tuple-element.20), channel_id=1, source_target_pairs={{0,24},{8,16},{16,8},{24,0},{1,25},{9,17},{17,9},{25,1},{2,26},{10... | collective-permute-start | bytes 196616 | tf_op jit(solution)/shard_map/ppermute | solution.py:24
  8.8 0.1 collective-permute-start.3
  8.9 1.5 %collective-permute-start.2 = (f32[8,128]{1,0:T(8,128)S(1)}, f32[8,128]{1,0:T(8,128)S(1)}, u32[]{:S(2)}, u32[]{:S(2)}) collective-permute-start(f32[8,128]{1,0:T(8,128)S(1)} %slice.3), channel_id=1, source_target_pairs={{0,4},{4,0},{1,5},{5,1},{2,6},{6,2},{3,7},{7,3},{8,12},{12,8},{9,1... | collective-permute-start | bytes 12296 | tf_op jit(solution)/shard_map/ppermute | solution.py:24
  10.4 1.1 %shard_map.29 = (f32[2,32,256]{2,1,0:T(8,128)S(1)}, f32[2,4,48,128]{3,2,1,0:T(8,128)S(1)}) custom-call(s32[3]{0:T(128)S(1)} %pad_add_fusion.place._, f32[2,48,32,128]{3,2,1,0:T(8,128)S(1)} %copy-done), custom_call_target="tpu_custom_call" | custom-call | tf_op jit(solution)/shard_map/pallas_call | solution.py:444
  11.5 1.0 %collective-permute-done.2.column_carry = f32[8,128]{1,0:T(8,128)S(1)} collective-permute-done((f32[8,128]{1,0:T(8,128)S(1)}, f32[8,128]{1,0:T(8,128)S(1)}, u32[]{:S(2)}, u32[]{:S(2)}) %collective-permute-start.2) | collective-permute-done | bytes 4128 | tf_op jit(solution)/shard_map/ppermute | solution.py:24
  12.5 1.4 %collective-permute-done.3.rest_0_ = f32[2,32,128]{2,1,0:T(8,128)S(1)} collective-permute-done((f32[2,32,128]{2,1,0:T(8,128)S(1)}, f32[2,32,128]{2,1,0:T(8,128)S(1)}, u32[]{:S(2)}, u32[]{:S(2)}) %collective-permute-start.3) | collective-permute-done | bytes 32800 | tf_op jit(solution)/shard_map/ppermute | solution.py:24
  13.9 0.0 collective-permute-done.first
  13.9 0.0 collective-permute-done.1.second
  13.9 1.0 %shard_map.30 = (f32[2,32,256]{2,1,0:T(8,128)S(1)}, f32[2,4,32,128]{3,2,1,0:T(8,128)S(1)}, f32[32,128]{1,0:T(8,128)S(1)}) custom-call(s32[3]{0:T(128)S(1)} %pad_add_fusion.place._, f32[2,2,32,128]{3,2,1,0:T(8,128)S(1)} %collective-permute-done.first, f32[2,2,32,128]{3,2,1,0:T(8,128)S(1)} %collective-permute-done.1.second, ...), custom_call_target="tpu_custom_call" | custom-call | tf_op jit(solution)/shard_map/pallas_call | solution.py:444
  14.9 0.2 collective-permute-start.5
  15.1 1.5 %collective-permute-start.4 = (f32[2,32,256]{2,1,0:T(8,128)S(1)}, f32[2,32,256]{2,1,0:T(8,128)S(1)}, u32[]{:S(2)}, u32[]{:S(2)}) collective-permute-start(f32[2,32,256]{2,1,0:T(8,128)S(1)} %get-tuple-element.25.packed), channel_id=1, source_target_pairs={{0,1},{1,0},{2,3},{3,2},{4,5},{5,4},{6,7},{7,6},{8,9},{9,8},{10,11... | collective-permute-start | bytes 196616 | tf_op jit(solution)/shard_map/ppermute | solution.py:24
  16.6 0.5 %collective-permute-start.6 = (f32[32,128]{1,0:T(8,128)S(1)}, f32[32,128]{1,0:T(8,128)S(1)}, u32[]{:S(2)}, u32[]{:S(2)}) collective-permute-start(f32[32,128]{1,0:T(8,128)S(1)} %get-tuple-element.23.rows), channel_id=1, source_target_pairs={{0,2},{1,3},{2,0},{3,1},{4,6},{5,7},{6,4},{7,5},{8,10},{9,11},{10,... | collective-permute-start | bytes 49160 | tf_op jit(solution)/shard_map/ppermute | solution.py:24
  17.1 3.2 %collective-permute-done.6.far_rows = f32[32,128]{1,0:T(8,128)S(1)} collective-permute-done((f32[32,128]{1,0:T(8,128)S(1)}, f32[32,128]{1,0:T(8,128)S(1)}, u32[]{:S(2)}, u32[]{:S(2)}) %collective-permute-start.6) | collective-permute-done | bytes 16416 | tf_op jit(solution)/shard_map/ppermute | solution.py:24
  20.3 0.0 collective-permute-done.5.second
  20.3 0.0 collective-permute-done.4.first
  20.3 1.0 %shard_map.31 = (f32[2,32,512]{2,1,0:T(8,128)S(1)}, f32[2,32,128]{2,1,0:T(8,128)S(1)}, f32[2,4,32,128]{3,2,1,0:T(8,128)S(1)}, f32[1,240,128]{2,1,0:T(8,128)S(1)}) custom-call(s32[3]{0:T(128)S(1)} %pad_add_fusion.place._, f32[2,32,256]{2,1,0:T(8,128)S(1)} %get-tuple-element.25.packed, f32[2,32,256]{2,1,0:T(8,128)S(1)} %collective-permute-done.4.first, ...), custom_call_target="tpu_custom_call" | custom-call | tf_op jit(solution)/shard_map/pallas_call | solution.py:444
  21.3 1.6 %collective-permute-start.7 = (f32[240,128]{1,0:T(8,128)S(1)}, f32[240,128]{1,0:T(8,128)S(1)}, u32[]{:S(2)}, u32[]{:S(2)}) collective-permute-start(f32[240,128]{1,0:T(8,128)S(1)} %bitcast.4), channel_id=1, source_target_pairs={{0,4},{4,0},{1,5},{5,1},{2,6},{6,2},{3,7},{7,3},{8,12},{12,8},{9,1... | collective-permute-start | bytes 368648 | tf_op jit(solution)/shard_map/ppermute | solution.py:24
  22.9 3.4 %collective-permute-done.7.first.second = f32[240,128]{1,0:T(8,128)S(1)} collective-permute-done((f32[240,128]{1,0:T(8,128)S(1)}, f32[240,128]{1,0:T(8,128)S(1)}, u32[]{:S(2)}, u32[]{:S(2)}) %collective-permute-start.7) | collective-permute-done | bytes 122912 | tf_op jit(solution)/shard_map/ppermute | solution.py:24
  26.3 0.0 copy-done.1
  26.3 6.9 %shard_map.32 = f32[3,48,32,128]{3,2,1,0:T(8,128)} custom-call(s32[3]{0:T(128)S(1)} %pad_add_fusion.place._, f32[2,48,32,128]{3,2,1,0:T(8,128)S(1)} %copy-done.1, f32[2,32,128]{2,1,0:T(8,128)S(1)} %get-tuple-element.29.flat, f32[2,4,32,128]{3,2,1,0:T(8,128)S(1)} %get-tuple-element.30.ext, f32[2,32,512]{2,1,0:T(8,128)S(1)} %get-tuple-element.31.strips, ...), custom_call_target="tpu_custom_call" | custom-call | tf_op jit(solution)/shard_map/pallas_call | solution.py:444
  (1 shorter events, 0.0 us)
Async XLA Ops:
  0.1 1.4 %copy-start = (f32[2,48,32,128]{3,2,1,0:T(8,128)S(1)}, f32[2,48,32,128]{3,2,1,0:T(8,128)}, u32[]{:S(2)}) copy-start(f32[2,48,32,128]{3,2,1,0:T(8,128)} %side.3) | copy-start | bytes 4718596
  1.5 0.7 %copy-start.2 = (f32[32,128]{1,0:T(8,128)S(1)}, f32[32,128]{1,0:T(8,128)}, u32[]{:S(2)}) copy-start(f32[32,128]{1,0:T(8,128)} %mag.1) | copy-start | bytes 49156
  2.2 24.1 %copy-start.1 = (f32[2,48,32,128]{3,2,1,0:T(8,128)S(1)}, f32[2,48,32,128]{3,2,1,0:T(8,128)}, u32[]{:S(2)}) copy-start(f32[2,48,32,128]{3,2,1,0:T(8,128)} %side.3) | copy-start | bytes 4718596
  3.2 10.7 %collective-permute-start = (f32[2,2,32,128]{3,2,1,0:T(8,128)S(1)}, f32[2,2,32,128]{3,2,1,0:T(8,128)S(1)}, u32[]{:S(2)}, u32[]{:S(2)}) collective-permute-start(f32[2,2,32,128]{3,2,1,0:T(8,128)S(1)} %get-tuple-element.19), channel_id=1, source_target_pairs={{0,8},{8,0},{16,24},{24,16},{1,9},{9,1},{17,25},{25,17},{2,10},{10... | collective-permute-start | bytes 196616 | tf_op jit(solution)/shard_map/ppermute | solution.py:24
  6.3 7.6 %collective-permute-start.1 = (f32[2,2,32,128]{3,2,1,0:T(8,128)S(1)}, f32[2,2,32,128]{3,2,1,0:T(8,128)S(1)}, u32[]{:S(2)}, u32[]{:S(2)}) collective-permute-start(f32[2,2,32,128]{3,2,1,0:T(8,128)S(1)} %get-tuple-element.20), channel_id=1, source_target_pairs={{0,24},{8,16},{16,8},{24,0},{1,25},{9,17},{17,9},{25,1},{2,26},{10... | collective-permute-start | bytes 196616 | tf_op jit(solution)/shard_map/ppermute | solution.py:24
  8.8 5.2 %collective-permute-start.3 = (f32[2,32,128]{2,1,0:T(8,128)S(1)}, f32[2,32,128]{2,1,0:T(8,128)S(1)}, u32[]{:S(2)}, u32[]{:S(2)}) collective-permute-start(f32[2,32,128]{2,1,0:T(8,128)S(1)} %get-tuple-element.21.total), channel_id=1, source_target_pairs={{0,16},{8,24},{16,0},{24,8},{1,17},{9,25},{17,1},{25,9},{2,18},{10... | collective-permute-start | bytes 98312 | tf_op jit(solution)/shard_map/ppermute | solution.py:24
  8.9 3.6 %collective-permute-start.2 = (f32[8,128]{1,0:T(8,128)S(1)}, f32[8,128]{1,0:T(8,128)S(1)}, u32[]{:S(2)}, u32[]{:S(2)}) collective-permute-start(f32[8,128]{1,0:T(8,128)S(1)} %slice.3), channel_id=1, source_target_pairs={{0,4},{4,0},{1,5},{5,1},{2,6},{6,2},{3,7},{7,3},{8,12},{12,8},{9,1... | collective-permute-start | bytes 12296 | tf_op jit(solution)/shard_map/ppermute | solution.py:24
  14.9 5.4 %collective-permute-start.5 = (f32[2,32,256]{2,1,0:T(8,128)S(1)}, f32[2,32,256]{2,1,0:T(8,128)S(1)}, u32[]{:S(2)}, u32[]{:S(2)}) collective-permute-start(f32[2,32,256]{2,1,0:T(8,128)S(1)} %get-tuple-element.25.packed), channel_id=1, source_target_pairs={{0,3},{1,2},{2,1},{3,0},{4,7},{5,6},{6,5},{7,4},{8,11},{9,10},{10,... | collective-permute-start | bytes 196616 | tf_op jit(solution)/shard_map/ppermute | solution.py:24
  15.1 5.3 %collective-permute-start.4 = (f32[2,32,256]{2,1,0:T(8,128)S(1)}, f32[2,32,256]{2,1,0:T(8,128)S(1)}, u32[]{:S(2)}, u32[]{:S(2)}) collective-permute-start(f32[2,32,256]{2,1,0:T(8,128)S(1)} %get-tuple-element.25.packed), channel_id=1, source_target_pairs={{0,1},{1,0},{2,3},{3,2},{4,5},{5,4},{6,7},{7,6},{8,9},{9,8},{10,11... | collective-permute-start | bytes 196616 | tf_op jit(solution)/shard_map/ppermute | solution.py:24
  16.6 3.7 %collective-permute-start.6 = (f32[32,128]{1,0:T(8,128)S(1)}, f32[32,128]{1,0:T(8,128)S(1)}, u32[]{:S(2)}, u32[]{:S(2)}) collective-permute-start(f32[32,128]{1,0:T(8,128)S(1)} %get-tuple-element.23.rows), channel_id=1, source_target_pairs={{0,2},{1,3},{2,0},{3,1},{4,6},{5,7},{6,4},{7,5},{8,10},{9,11},{10,... | collective-permute-start | bytes 49160 | tf_op jit(solution)/shard_map/ppermute | solution.py:24
  21.3 4.9 %collective-permute-start.7 = (f32[240,128]{1,0:T(8,128)S(1)}, f32[240,128]{1,0:T(8,128)S(1)}, u32[]{:S(2)}, u32[]{:S(2)}) collective-permute-start(f32[240,128]{1,0:T(8,128)S(1)} %bitcast.4), channel_id=1, source_target_pairs={{0,4},{4,0},{1,5},{5,1},{2,6},{6,2},{3,7},{7,3},{8,12},{12,8},{9,1... | collective-permute-start | bytes 368648 | tf_op jit(solution)/shard_map/ppermute | solution.py:24

commit v3 on v2

--- a/solution.py
+++ b/solution.py
@@ -279,174 +279,247 @@
     return current_x, current_y, current_z
 
 
-def step_kernel(
-    counts, place, side, flat, ext, strips, first, second, out, state, field, later, halo, wide
+class Stepper:
+    def __init__(self, counts, place, state, field, later, halo, depth, height):
+        self.counts = counts
+        self.z, self.y, self.x = place[0], place[1], place[2]
+        self.state, self.field, self.later, self.halo = state, field, later, halo
+        self.depth, self.height = depth, height
+        self.padded = state.shape[2]
+        lane = lane_index((8, LANES))
+        self.last, self.start = lane == LANES - 1, lane == 0
+
+    def load(self, ref, c, layer, row):
+        return ref[c, layer, pl.ds(row, 8), :]
+
+    def strips(self, wide):
+        depth, height = self.depth, self.height
+        count_z, count_y, count_x = self.counts
+        half = 2 * LANES
+        shape = (self.padded, 2 * half)
+        lane, row = lane_index(shape), row_index(shape)
+        q = lane % 4
+        slot = (lane % half) // 4
+        right = lane >= half
+        inside = (row >= PAD - 2) & (row < PAD + height + 2) & (slot < depth + 4)
+        inside = inside & ((row >= PAD) | (self.y > 0))
+        inside = inside & ((row < PAD + height) | (self.y < count_y - 1))
+        inside = inside & ((slot >= 2) | (self.z > 0))
+        inside = inside & ((slot < depth + 2) | (self.z < count_z - 1))
+        inside = inside & (right | (q >= 2) | (self.x > 0))
+        inside = inside & (~right | (q < 2) | (self.x < count_x - 1))
+        a = [jnp.where(inside, wide[c], 0.0) for c in range(2)]
+        a.append(jnp.zeros_like(a[0]))
+        b = strip_field(a)
+        pick = (lane_index((self.padded, half)) % 4) == 2
+
+        def keep(at, upper, lower):
+            value = jnp.where(pick, upper[:, half:], lower[:, :half])
+            self.halo[at, 0] = value[:, :LANES]
+            self.halo[at, 1] = value[:, LANES:]
+
+        keep(0, a[1], b[1])
+        keep(1, a[2], b[2])
+        a = [jnp.where(inside, value, 0.0) for value in push(a, b, strip_current(b))]
+        b = strip_field(a)
+        keep(2, a[1], b[1])
+        keep(3, a[2], b[2])
+
+    def beside(self, at, layer, row):
+        shift = LANES - 2 - 4 * (layer % GROUP)
+        return pltpu.roll(self.halo[at, layer // GROUP, pl.ds(row, 8), :], shift, 1)
+
+    def right_of(self, value, edge):
+        return following(jnp.where(self.start, edge, value), 1)
+
+    def left_of(self, value, edge):
+        return preceding(jnp.where(self.last, edge, value), 1)
+
+    def first_field(self, layer, r):
+        load, state = self.load, self.state
+        ax, ay = load(state, 0, layer, r), load(state, 1, layer, r)
+        ay_right = self.right_of(ay, self.beside(0, layer, r))
+        to = pl.ds(r, 8)
+        self.field[0, layer, to, :] = ay - load(state, 1, layer + 1, r)
+        self.field[1, layer, to, :] = load(state, 0, layer + 1, r) - ax
+        self.field[2, layer, to, :] = ay_right - ay - (load(state, 0, layer, r + 1) - ax)
+
+    def currents(self, layer, r, at):
+        load, field = self.load, self.field
+        bx, by, bz = (load(field, c, layer, r) for c in range(3))
+        by_left = self.left_of(by, self.beside(at, layer, r))
+        bz_left = self.left_of(bz, self.beside(at + 1, layer, r))
+        jx = bz - load(field, 2, layer, r - 1) - (by - load(field, 1, layer - 1, r))
+        jy = bx - load(field, 0, layer - 1, r) - (bz - bz_left)
+        jz = by - by_left - (bx - load(field, 0, layer, r - 1))
+        return (bx, by, bz), (jx, jy, jz)
+
+    def first_push(self, layer, r):
+        b, j = self.currents(layer, r, 0)
+        a = [self.load(self.state, c, layer, r) for c in range(2)]
+        a.append(jnp.zeros_like(a[0]))
+        for c, value in enumerate(push(a, b, j)):
+            self.later[c, layer, pl.ds(r, 8), :] = value
+
+    def second_field(self, layer, r):
+        load, later = self.load, self.later
+        ax, ay, az = (load(later, c, layer, r) for c in range(3))
+        ay_right = self.right_of(ay, self.beside(2, layer, r))
+        az_right = self.right_of(az, self.beside(3, layer, r))
+        to = pl.ds(r, 8)
+        self.field[0, layer, to, :] = (
+            load(later, 2, layer, r + 1) - az - (load(later, 1, layer + 1, r) - ay)
+        )
+        self.field[1, layer, to, :] = load(later, 0, layer + 1, r) - ax - (az_right - az)
+        self.field[2, layer, to, :] = ay_right - ay - (load(later, 0, layer, r + 1) - ax)
+
+    def second_push(self, layer, r):
+        b, j = self.currents(layer, r, 2)
+        a = [self.load(self.later, c, layer, r) for c in range(3)]
+        return [spacing * value for value in push(a, b, j)]
+
+    def clear(self, rows):
+        depth, height = self.depth, self.height
+        count_z, count_y, _ = self.counts
+        zeros = jnp.zeros((height + 8, LANES), jnp.float32)
+        line = jnp.zeros((depth + 4, LANES), jnp.float32)
+        for exists, layer in ((self.z > 0, 1), (self.z < count_z - 1, depth + 2)):
+
+            @pl.when(jnp.logical_not(exists))
+            def _():
+                for c in range(3):
+                    self.later[c, layer, pl.ds(PAD - 1, height + 8), :] = zeros
+
+        if not rows:
+            return
+        for exists, row in ((self.y > 0, PAD - 1), (self.y < count_y - 1, PAD + height)):
+
+            @pl.when(jnp.logical_not(exists))
+            def _():
+                for c in range(3):
+                    flat_later = self.later.at[c].reshape((depth + 4) * self.padded, LANES)
+                    flat_later[pl.ds(row, depth + 4, stride=self.padded), :] = line
+
+    def run(self, tiles, rows, out, block, sems, pieces=6):
+        depth = self.depth
+        for layer in range(depth + 3):
+            for r in tiles[0]:
+                self.first_field(layer, r)
+        for layer in range(1, depth + 3):
+            for r in tiles[1]:
+                self.first_push(layer, r)
+        self.clear(rows)
+        for layer in range(1, depth + 2):
+            for r in tiles[2]:
+                self.second_field(layer, r)
+        copies = []
+        size = depth // pieces
+        for piece in range(pieces):
+            layers = pl.ds(piece * size, size)
+            for layer in range(piece * size, (piece + 1) * size):
+                for k, r in enumerate(tiles[3]):
+                    for c, value in enumerate(self.second_push(layer + 2, r)):
+                        block[c, layer, pl.ds(8 * k, 8), :] = value
+            k = 0
+            while k < len(tiles[3]):
+                run = 1
+                while k + run < len(tiles[3]) and tiles[3][k + run] == tiles[3][k] + 8 * run:
+                    run += 1
+                copies.append(
+                    pltpu.make_async_copy(
+                        block.at[:, layers, pl.ds(8 * k, 8 * run), :],
+                        out.at[:, layers, pl.ds(tiles[3][k] - PAD, 8 * run), :],
+                        sems.at[piece, k],
+                    )
+                )
+                copies[-1].start()
+                k += run
+        for copy in copies:
+            copy.wait()
+
+
+def inner_tiles(height):
+    whole = [PAD + r for r in range(0, height, 8)]
+    inner = whole[1:-1]
+    return whole, whole, [r - 1 for r in inner] + [inner[-1]], inner
+
+
+def outer_tiles(height):
+    top = PAD + height - 8
+    return (PAD - 2, top + 1), (PAD - 1, top + 1), (PAD - 1, top), (PAD, top)
+
+
+def inner_kernel(
+    counts, place, side, flat, ext, strips, state, field, later, out, halo, wide, block, sems
 ):
-    count_z, count_y, count_x = counts
     depth, height = side.shape[1], side.shape[2]
-    z, y, x = place[0], place[1], place[2]
-    slots = slot_rows(depth)
-    layers = depth + 4
-    padded = state.shape[2]
-    odd = y % 2 == 1
-
-    sums = [jnp.zeros((height, LANES), jnp.float32) for _ in range(2)]
     rows = pl.ds(PAD, height)
     for c in range(2):
         for k, at in enumerate((0, 1, depth + 2, depth + 3)):
             state[c, at, rows, :] = ext[c, k]
-
+    sums = [jnp.zeros((height, LANES), jnp.float32) for _ in range(2)]
     for layer in range(depth):
         sums = [total + side[c, layer] for c, total in enumerate(sums)]
         state[0, layer + 2, rows, :] = flat[0] + sums[1]
         state[1, layer + 2, rows, :] = flat[1] - sums[0]
-
+    for c in range(2):
+        wide[c, rows, :] = strips[c]
+        wide[c, pl.ds(0, PAD), :] = jnp.zeros((PAD, wide.shape[2]), jnp.float32)
+        wide[c, pl.ds(PAD + height, PAD), :] = jnp.zeros((PAD, wide.shape[2]), jnp.float32)
+    stepper = Stepper(counts, place, state, field, later, halo, depth, height)
+    stepper.strips(wide)
+    stepper.run(inner_tiles(height), False, out, block, sems)
+
+
+def outer_kernel(
+    counts, depth, place, strips, first, second, _s, _f, _l, _o,
+    state, field, later, out, halo, wide, block, sems,
+):
+    _, count_y, _ = counts
+    height, padded = strips.shape[1], state.shape[2]
+    y = place[1]
+    slots = slot_rows(depth)
+    layers = depth + 4
+    odd = y % 2 == 1
     for low in (True, False):
         exists = (y > 0) if low else (y < count_y - 1)
         row = PAD - 2 if low else PAD + height
+
+        def received(take):
+            a, b = first[take, :], second[take, :]
+            value = jnp.where(odd, a, b) if low else jnp.where(odd, b, a)
+            return jnp.where(exists, value, 0.0)
+
         for c in range(2):
             flat_state = state.at[c].reshape(layers * padded, LANES)
             for r in range(2):
-                take = pl.ds((c * 2 + r) * slots, layers)
-                a, b = first[take, :], second[take, :]
-                value = jnp.where(odd, a, b) if low else jnp.where(odd, b, a)
-                flat_state[pl.ds(row + r, layers, stride=padded), :] = jnp.where(exists, value, 0.0)
+                flat_state[pl.ds(row + r, layers, stride=padded), :] = received(
+                    pl.ds((c * 2 + r) * slots, layers)
+                )
             for tile in range(4):
-                take = pl.ds(4 * slots + (c * 4 + tile) * 2, 2)
-                a, b = first[take, :], second[take, :]
-                value = jnp.where(odd, a, b) if low else jnp.where(odd, b, a)
-                wide[c, pl.ds(row, 2), pl.ds(tile * LANES, LANES)] = jnp.where(exists, value, 0.0)
-    wide[0, rows, :] = strips[0]
-    wide[1, rows, :] = strips[1]
-
-    half = 2 * LANES
-    lane = lane_index((padded, 2 * half))
-    row = row_index((padded, 2 * half))
-    q = lane % 4
-    slot = (lane % half) // 4
-    right = lane >= half
-    inside = (row >= PAD - 2) & (row < PAD + height + 2) & (slot < layers)
-    inside = inside & ((row >= PAD) | (y > 0)) & ((row < PAD + height) | (y < count_y - 1))
-    inside = inside & ((slot >= 2) | (z > 0)) & ((slot < depth + 2) | (z < count_z - 1))
-    inside = inside & (right | (q >= 2) | (x > 0))
-    inside = inside & (~right | (q < 2) | (x < count_x - 1))
-    a = [jnp.where(inside, wide[c], 0.0) for c in range(2)]
-    a.append(jnp.zeros_like(a[0]))
-    b = strip_field(a)
-    pick = (lane_index((padded, half)) % 4) == 2
-
-    def keep(at, upper, lower):
-        value = jnp.where(pick, upper[:, half:], lower[:, :half])
-        halo[at, 0] = value[:, :LANES]
-        halo[at, 1] = value[:, LANES:]
-
-    keep(0, a[1], b[1])
-    keep(1, a[2], b[2])
-    a = [jnp.where(inside, value, 0.0) for value in push(a, b, strip_current(b))]
-    b = strip_field(a)
-    keep(2, a[1], b[1])
-    keep(3, a[2], b[2])
-
-    lane = lane_index((8, LANES))
-    last, start = lane == LANES - 1, lane == 0
-
-    def beside(at, layer, row):
-        shift = LANES - 2 - 4 * (layer % GROUP)
-        return pltpu.roll(halo[at, layer // GROUP, pl.ds(row, 8), :], shift, 1)
-
-    def right_of(value, edge):
-        return following(jnp.where(start, edge, value), 1)
-
-    def left_of(value, edge):
-        return preceding(jnp.where(last, edge, value), 1)
-
-    def load(ref, c, layer, row):
-        return ref[c, layer, pl.ds(row, 8), :]
-
-    def first_field(layer):
-        for tile in range(5):
-            r = PAD - 2 + 8 * tile
-            ax, ay = load(state, 0, layer, r), load(state, 1, layer, r)
-            ay_right = right_of(ay, beside(0, layer, r))
-            to = pl.ds(r, 8)
-            field[0, layer, to, :] = ay - load(state, 1, layer + 1, r)
-            field[1, layer, to, :] = load(state, 0, layer + 1, r) - ax
-            field[2, layer, to, :] = ay_right - ay - (load(state, 0, layer, r + 1) - ax)
-
-    def currents(layer, r, at):
-        bx, by, bz = (load(field, c, layer, r) for c in range(3))
-        by_left = left_of(by, beside(at, layer, r))
-        bz_left = left_of(bz, beside(at + 1, layer, r))
-        jx = bz - load(field, 2, layer, r - 1) - (by - load(field, 1, layer - 1, r))
-        jy = bx - load(field, 0, layer - 1, r) - (bz - bz_left)
-        jz = by - by_left - (bx - load(field, 0, layer, r - 1))
-        return (bx, by, bz), (jx, jy, jz)
-
-    def first_push(layer):
-        for tile in range(5):
-            r = PAD - 1 + 8 * tile
-            b, j = currents(layer, r, 0)
-            a = [load(state, c, layer, r) for c in range(2)]
-            a.append(jnp.zeros_like(a[0]))
-            for c, value in enumerate(push(a, b, j)):
-                later[c, layer, pl.ds(r, 8), :] = value
-
-    def second_field(layer):
-        for tile in range(5):
-            r = PAD - 1 + 8 * tile
-            ax, ay, az = (load(later, c, layer, r) for c in range(3))
-            ay_right = right_of(ay, beside(2, layer, r))
-            az_right = right_of(az, beside(3, layer, r))
-            to = pl.ds(r, 8)
-            field[0, layer, to, :] = (
-                load(later, 2, layer, r + 1) - az - (load(later, 1, layer + 1, r) - ay)
-            )
-            field[1, layer, to, :] = load(later, 0, layer + 1, r) - ax - (az_right - az)
-            field[2, layer, to, :] = ay_right - ay - (load(later, 0, layer, r + 1) - ax)
-
-    def second_push(layer):
-        for tile in range(height // 8):
-            r = PAD + 8 * tile
-            b, j = currents(layer, r, 2)
-            a = [load(later, c, layer, r) for c in range(3)]
-            for c, value in enumerate(push(a, b, j)):
-                out[c, layer - 2, pl.ds(8 * tile, 8), :] = spacing * value
-
-    for layer in range(0, depth + 3):
-        first_field(layer)
-    for layer in range(1, depth + 3):
-        first_push(layer)
-
-    zeros = jnp.zeros((height + 8, LANES), jnp.float32)
-    line = jnp.zeros((layers, LANES), jnp.float32)
-    for c in range(3):
-        for exists, layer in ((z > 0, 1), (z < count_z - 1, depth + 2)):
-
-            @pl.when(jnp.logical_not(exists))
-            def _():
-                later[c, layer, pl.ds(PAD - 1, height + 8), :] = zeros
-
-        for exists, row in ((y > 0, PAD - 1), (y < count_y - 1, PAD + height)):
-
-            @pl.when(jnp.logical_not(exists))
-            def _():
-                flat_later = later.at[c].reshape(layers * padded, LANES)
-                flat_later[pl.ds(row, layers, stride=padded), :] = line
-
-    for layer in range(1, depth + 2):
-        second_field(layer)
-    for layer in range(2, depth + 2):
-        second_push(layer)
-
-
-def call(kernel, shapes, args, scratch=(), limit=16):
-    vmem = pl.BlockSpec(memory_space=pltpu.VMEM)
+                wide[c, pl.ds(row, 2), pl.ds(tile * LANES, LANES)] = received(
+                    pl.ds(4 * slots + (c * 4 + tile) * 2, 2)
+                )
+    for c in range(2):
+        wide[c, pl.ds(PAD, height), :] = strips[c]
+    stepper = Stepper(counts, place, state, field, later, halo, depth, height)
+    stepper.strips(wide)
+    stepper.run(outer_tiles(height), True, out, block, sems)
+
+
+def call(kernel, shapes, args, scratch=(), limit=16, far_out=0, far_in=(), aliases={}):
+    vmem, far = pl.BlockSpec(memory_space=pltpu.VMEM), pl.BlockSpec(memory_space=pl.ANY)
+    specs = [far if k in far_in else vmem for k in range(1, len(args))]
     return pl.pallas_call(
         kernel,
         out_shape=[jax.ShapeDtypeStruct(shape, jnp.float32) for shape in shapes],
-        in_specs=[pl.BlockSpec(memory_space=pltpu.SMEM)] + [vmem] * (len(args) - 1),
-        out_specs=[vmem] * len(shapes),
-        scratch_shapes=[pltpu.VMEM(shape, jnp.float32) for shape in scratch],
+        in_specs=[pl.BlockSpec(memory_space=pltpu.SMEM)] + specs,
+        out_specs=[vmem] * (len(shapes) - far_out) + [far] * far_out,
+        scratch_shapes=[
+            pltpu.VMEM(shape, jnp.float32) if isinstance(shape, tuple) else shape
+            for shape in scratch
+        ],
+        input_output_aliases=aliases,
         compiler_params=pltpu.CompilerParams(vmem_limit_bytes=limit * 2**20),
     )(*args)
 
@@ -516,21 +589,44 @@
     )
     first = swap_first(edge_rows[0], "gy")
     second = swap_second(edge_rows[1], "gy") if count_y > 2 else first
-    layers, padded = depth + 4, height + 2 * PAD
-    (result,) = call(
-        functools.partial(step_kernel, counts),
-        [(3, depth) + plane],
-        [place, side, flat, ext, strips, first, second],
+    grids = inner_steps(counts, place, side, flat, ext, strips)
+    return outer_steps(counts, depth, place, strips, first, second, grids)
+
+
+def inner_steps(counts, place, side, flat, ext, strips):
+    _, depth, height, width = side.shape
+    grid = (depth + 4, height + 2 * PAD, width)
+    return call(
+        functools.partial(inner_kernel, counts),
+        [(2,) + grid, (3,) + grid, (3,) + grid, (3, depth, height, width)],
+        [place, side, flat, ext, strips],
         [
-            (2, layers, padded, width),
-            (3, layers, padded, width),
-            (3, layers, padded, width),
-            (4, 2, padded, LANES),
-            (2, padded, 4 * LANES),
+            (4, 2, height + 2 * PAD, LANES),
+            (2, height + 2 * PAD, 4 * LANES),
+            (3, depth, height - 16, width),
+            pltpu.SemaphoreType.DMA((6, 4)),
         ],
-        limit=24,
-    )
-    return result
+        far_out=1,
+    )
+
+
+def outer_steps(counts, depth, place, strips, first, second, grids):
+    height, width = strips.shape[1], first.shape[1]
+    result = call(
+        functools.partial(outer_kernel, counts, depth),
+        [grid.shape for grid in grids],
+        [place, strips, first, second, *grids],
+        [
+            (4, 2, height + 2 * PAD, LANES),
+            (2, height + 2 * PAD, 4 * LANES),
+            (3, depth, 16, width),
+            pltpu.SemaphoreType.DMA((6, 4)),
+        ],
+        far_out=1,
+        far_in=(7,),
+        aliases={4 + k: k for k in range(4)},
+    )
+    return result[3]
 
 
 def solution(mesh):

time: 33.5 us -> 33.2 us (level)
  waiting for transfers between devices: 8.99 us -> 5.63 us
  Pallas kernels: 11 us -> 14.1 us
    ppermute x8, waiting for transfers between devices: 8.99 us -> 5.63 us  [swap(): return lax.ppermute(part, axis, [(i, partner(i)) for i in range(count)])]
    pallas_call x5 -> x6, Pallas kernels: 11 us -> 14.1 us  [call(): pl.pallas_call(kernel, out_shape=[jax.ShapeDtypeStruct(shape, jnp.float32...]
  transfers between devices with their start and end apart: 8 -> 8, of which waited for: 4 -> 3; matrix products, arithmetic and copies ran while one was open for 0% -> 0% of each run, Pallas kernels for 3% -> 20%
where the time goes in v3:
time: 33.2 us; the launch traced here: 33 us
  Pallas kernels  14.1 us (42%)
  starting transfers between devices  11 us (33%)
  waiting for transfers between devices  5.63 us (17%)
  local copies, waits for them, and re-layouts  2.13 us (6%)
    pallas_call x6, Pallas kernels, call(): pl.pallas_call(kernel, out_shape=[jax.ShapeDtypeStruct(shape, jnp.float32...  14.1 us
    ppermute x8, starting transfers between devices, swap(): return lax.ppermute(part, axis, [(i, partner(i)) for i in range(count)])  11 us
    ppermute x8, waiting for transfers between devices, swap(): return lax.ppermute(part, axis, [(i, partner(i)) for i in range(count)])  5.63 us
    unnamed x6, local copies, waits for them, and re-layouts  2.13 us
  transfers between devices with their start and end apart: 8, of which 3 were waited for; matrix products, arithmetic and copies ran while one was open for 0% of the time, Pallas kernels for 20%

profile of v3, /device:TPU:0, one launch (start us, length us, event | category | flops | bytes accessed | tf_op | source)
XLA Modules:
  0.0 33.0 jit_solution(2328066082595680749)
XLA Ops:
  0.0 0.1 pad_add_fusion.place._
  0.1 0.0 copy-start
  0.1 1.4 %copy-done = f32[2,48,32,128]{3,2,1,0:T(8,128)S(1)} copy-done((f32[2,48,32,128]{3,2,1,0:T(8,128)S(1)}, f32[2,48,32,128]{3,2,1,0:T(8,128)}, u32[]{:S(2)}) %copy-start) | copy-done | bytes 1572888
  1.5 0.0 copy-start.2
  1.5 0.7 %copy-done.2 = f32[32,128]{1,0:T(8,128)S(1)} copy-done((f32[32,128]{1,0:T(8,128)S(1)}, f32[32,128]{1,0:T(8,128)}, u32[]{:S(2)}) %copy-start.2) | copy-done | bytes 16408
  2.2 0.0 copy-start.1
  2.2 1.0 %shard_map.28 = (f32[2,2,32,128]{3,2,1,0:T(8,128)S(1)}, f32[2,2,32,128]{3,2,1,0:T(8,128)S(1)}, f32[2,32,128]{2,1,0:T(8,128)S(1)}, f32[32,128]{1,0:T(8,128)S(1)}, f32[32,128]{1,0:T(8,128)S(1)}) custom-call(s32[3]{0:T(128)S(1)} %pad_add_fusion.place._, f32[2,48,32,128]{3,2,1,0:T(8,128)S(1)} %copy-done, f32[32,128]{1,0:T(8,128)S(1)} %copy-done.2), custom_call_target="tpu_custom_call" | custom-call | tf_op jit(solution)/shard_map/pallas_call | solution.py:513
  3.2 3.1 %collective-permute-start = (f32[2,2,32,128]{3,2,1,0:T(8,128)S(1)}, f32[2,2,32,128]{3,2,1,0:T(8,128)S(1)}, u32[]{:S(2)}, u32[]{:S(2)}) collective-permute-start(f32[2,2,32,128]{3,2,1,0:T(8,128)S(1)} %get-tuple-element.24), channel_id=1, source_target_pairs={{0,8},{8,0},{16,24},{24,16},{1,9},{9,1},{17,25},{25,17},{2,10},{10... | collective-permute-start | bytes 196616 | tf_op jit(solution)/shard_map/ppermute | solution.py:24
  6.3 2.5 %collective-permute-start.1 = (f32[2,2,32,128]{3,2,1,0:T(8,128)S(1)}, f32[2,2,32,128]{3,2,1,0:T(8,128)S(1)}, u32[]{:S(2)}, u32[]{:S(2)}) collective-permute-start(f32[2,2,32,128]{3,2,1,0:T(8,128)S(1)} %get-tuple-element.25), channel_id=1, source_target_pairs={{0,24},{8,16},{16,8},{24,0},{1,25},{9,17},{17,9},{25,1},{2,26},{10... | collective-permute-start | bytes 196616 | tf_op jit(solution)/shard_map/ppermute | solution.py:24
  8.8 0.1 collective-permute-start.3
  8.9 1.5 %collective-permute-start.2 = (f32[8,128]{1,0:T(8,128)S(1)}, f32[8,128]{1,0:T(8,128)S(1)}, u32[]{:S(2)}, u32[]{:S(2)}) collective-permute-start(f32[8,128]{1,0:T(8,128)S(1)} %slice.3), channel_id=1, source_target_pairs={{0,4},{4,0},{1,5},{5,1},{2,6},{6,2},{3,7},{7,3},{8,12},{12,8},{9,1... | collective-permute-start | bytes 12296 | tf_op jit(solution)/shard_map/ppermute | solution.py:24
  10.4 1.1 %shard_map.29 = (f32[2,32,256]{2,1,0:T(8,128)S(1)}, f32[2,4,48,128]{3,2,1,0:T(8,128)S(1)}) custom-call(s32[3]{0:T(128)S(1)} %pad_add_fusion.place._, f32[2,48,32,128]{3,2,1,0:T(8,128)S(1)} %copy-done), custom_call_target="tpu_custom_call" | custom-call | tf_op jit(solution)/shard_map/pallas_call | solution.py:513
  11.5 1.0 %collective-permute-done.2.column_carry = f32[8,128]{1,0:T(8,128)S(1)} collective-permute-done((f32[8,128]{1,0:T(8,128)S(1)}, f32[8,128]{1,0:T(8,128)S(1)}, u32[]{:S(2)}, u32[]{:S(2)}) %collective-permute-start.2) | collective-permute-done | bytes 4128 | tf_op jit(solution)/shard_map/ppermute | solution.py:24
  12.5 1.4 %collective-permute-done.3.rest_0_ = f32[2,32,128]{2,1,0:T(8,128)S(1)} collective-permute-done((f32[2,32,128]{2,1,0:T(8,128)S(1)}, f32[2,32,128]{2,1,0:T(8,128)S(1)}, u32[]{:S(2)}, u32[]{:S(2)}) %collective-permute-start.3) | collective-permute-done | bytes 32800 | tf_op jit(solution)/shard_map/ppermute | solution.py:24
  13.9 0.0 collective-permute-done.first
  13.9 0.0 collective-permute-done.1.second
  13.9 1.0 %shard_map.30 = (f32[2,32,256]{2,1,0:T(8,128)S(1)}, f32[2,4,32,128]{3,2,1,0:T(8,128)S(1)}, f32[32,128]{1,0:T(8,128)S(1)}) custom-call(s32[3]{0:T(128)S(1)} %pad_add_fusion.place._, f32[2,2,32,128]{3,2,1,0:T(8,128)S(1)} %collective-permute-done.first, f32[2,2,32,128]{3,2,1,0:T(8,128)S(1)} %collective-permute-done.1.second, ...), custom_call_target="tpu_custom_call" | custom-call | tf_op jit(solution)/shard_map/pallas_call | solution.py:513
  14.9 0.2 collective-permute-start.5
  15.1 1.5 %collective-permute-start.4 = (f32[2,32,256]{2,1,0:T(8,128)S(1)}, f32[2,32,256]{2,1,0:T(8,128)S(1)}, u32[]{:S(2)}, u32[]{:S(2)}) collective-permute-start(f32[2,32,256]{2,1,0:T(8,128)S(1)} %get-tuple-element.30.packed), channel_id=1, source_target_pairs={{0,1},{1,0},{2,3},{3,2},{4,5},{5,4},{6,7},{7,6},{8,9},{9,8},{10,11... | collective-permute-start | bytes 196616 | tf_op jit(solution)/shard_map/ppermute | solution.py:24
  16.6 0.5 %collective-permute-start.6 = (f32[32,128]{1,0:T(8,128)S(1)}, f32[32,128]{1,0:T(8,128)S(1)}, u32[]{:S(2)}, u32[]{:S(2)}) collective-permute-start(f32[32,128]{1,0:T(8,128)S(1)} %get-tuple-element.28.rows), channel_id=1, source_target_pairs={{0,2},{1,3},{2,0},{3,1},{4,6},{5,7},{6,4},{7,5},{8,10},{9,11},{10,... | collective-permute-start | bytes 49160 | tf_op jit(solution)/shard_map/ppermute | solution.py:24
  17.1 3.2 %collective-permute-done.6.far_rows = f32[32,128]{1,0:T(8,128)S(1)} collective-permute-done((f32[32,128]{1,0:T(8,128)S(1)}, f32[32,128]{1,0:T(8,128)S(1)}, u32[]{:S(2)}, u32[]{:S(2)}) %collective-permute-start.6) | collective-permute-done | bytes 16416 | tf_op jit(solution)/shard_map/ppermute | solution.py:24
  20.3 0.0 collective-permute-done.5.second
  20.3 0.0 collective-permute-done.4.first
  20.3 1.0 %shard_map.31 = (f32[2,32,512]{2,1,0:T(8,128)S(1)}, f32[2,32,128]{2,1,0:T(8,128)S(1)}, f32[2,4,32,128]{3,2,1,0:T(8,128)S(1)}, f32[1,240,128]{2,1,0:T(8,128)S(1)}) custom-call(s32[3]{0:T(128)S(1)} %pad_add_fusion.place._, f32[2,32,256]{2,1,0:T(8,128)S(1)} %get-tuple-element.30.packed, f32[2,32,256]{2,1,0:T(8,128)S(1)} %collective-permute-done.4.first, ...), custom_call_target="tpu_custom_call" | custom-call | tf_op jit(solution)/shard_map/pallas_call | solution.py:513
  21.3 1.6 %collective-permute-start.7 = (f32[240,128]{1,0:T(8,128)S(1)}, f32[240,128]{1,0:T(8,128)S(1)}, u32[]{:S(2)}, u32[]{:S(2)}) collective-permute-start(f32[240,128]{1,0:T(8,128)S(1)} %bitcast.4), channel_id=1, source_target_pairs={{0,4},{4,0},{1,5},{5,1},{2,6},{6,2},{3,7},{7,3},{8,12},{12,8},{9,1... | collective-permute-start | bytes 368648 | tf_op jit(solution)/shard_map/ppermute | solution.py:24
  22.9 0.0 copy-done.1
  22.9 5.5 %shard_map.32 = (f32[2,52,48,128]{3,2,1,0:T(8,128)S(1)}, f32[3,52,48,128]{3,2,1,0:T(8,128)S(1)}, f32[3,52,48,128]{3,2,1,0:T(8,128)S(1)}, f32[3,48,32,128]{3,2,1,0:T(8,128)}) custom-call(s32[3]{0:T(128)S(1)} %pad_add_fusion.place._, f32[2,48,32,128]{3,2,1,0:T(8,128)S(1)} %copy-done.1, f32[2,32,128]{2,1,0:T(8,128)S(1)} %get-tuple-element.36.flat, ...), custom_call_target="tpu_custom_call" | custom-call | tf_op jit(solution)/shard_map/pallas_call | solution.py:513
  28.4 0.0 collective-permute-done.7.first.second
  28.4 4.6 %shard_map.33 = (f32[2,52,48,128]{3,2,1,0:T(8,128)S(1)}, f32[3,52,48,128]{3,2,1,0:T(8,128)S(1)}, f32[3,52,48,128]{3,2,1,0:T(8,128)S(1)}, f32[3,48,32,128]{3,2,1,0:T(8,128)}) custom-call(s32[3]{0:T(128)S(1)} %pad_add_fusion.place._, ...), custom_call_target="tpu_custom_call", output_to_operand_aliasing={{0}: (4, {}), {1}: (5, {}), {2}: (6, {}), {3}: (7, {})} | custom-call | tf_op jit(solution)/shard_map/pallas_call | solution.py:513
  (1 shorter events, 0.0 us)
Async XLA Ops:
  0.1 1.4 %copy-start = (f32[2,48,32,128]{3,2,1,0:T(8,128)S(1)}, f32[2,48,32,128]{3,2,1,0:T(8,128)}, u32[]{:S(2)}) copy-start(f32[2,48,32,128]{3,2,1,0:T(8,128)} %side.3) | copy-start | bytes 4718596
  1.5 0.7 %copy-start.2 = (f32[32,128]{1,0:T(8,128)S(1)}, f32[32,128]{1,0:T(8,128)}, u32[]{:S(2)}) copy-start(f32[32,128]{1,0:T(8,128)} %mag.1) | copy-start | bytes 49156
  2.2 20.7 %copy-start.1 = (f32[2,48,32,128]{3,2,1,0:T(8,128)S(1)}, f32[2,48,32,128]{3,2,1,0:T(8,128)}, u32[]{:S(2)}) copy-start(f32[2,48,32,128]{3,2,1,0:T(8,128)} %side.3) | copy-start | bytes 4718596
  3.2 10.7 %collective-permute-start = (f32[2,2,32,128]{3,2,1,0:T(8,128)S(1)}, f32[2,2,32,128]{3,2,1,0:T(8,128)S(1)}, u32[]{:S(2)}, u32[]{:S(2)}) collective-permute-start(f32[2,2,32,128]{3,2,1,0:T(8,128)S(1)} %get-tuple-element.24), channel_id=1, source_target_pairs={{0,8},{8,0},{16,24},{24,16},{1,9},{9,1},{17,25},{25,17},{2,10},{10... | collective-permute-start | bytes 196616 | tf_op jit(solution)/shard_map/ppermute | solution.py:24
  6.3 7.6 %collective-permute-start.1 = (f32[2,2,32,128]{3,2,1,0:T(8,128)S(1)}, f32[2,2,32,128]{3,2,1,0:T(8,128)S(1)}, u32[]{:S(2)}, u32[]{:S(2)}) collective-permute-start(f32[2,2,32,128]{3,2,1,0:T(8,128)S(1)} %get-tuple-element.25), channel_id=1, source_target_pairs={{0,24},{8,16},{16,8},{24,0},{1,25},{9,17},{17,9},{25,1},{2,26},{10... | collective-permute-start | bytes 196616 | tf_op jit(solution)/shard_map/ppermute | solution.py:24
  8.8 5.2 %collective-permute-start.3 = (f32[2,32,128]{2,1,0:T(8,128)S(1)}, f32[2,32,128]{2,1,0:T(8,128)S(1)}, u32[]{:S(2)}, u32[]{:S(2)}) collective-permute-start(f32[2,32,128]{2,1,0:T(8,128)S(1)} %get-tuple-element.26.total), channel_id=1, source_target_pairs={{0,16},{8,24},{16,0},{24,8},{1,17},{9,25},{17,1},{25,9},{2,18},{10... | collective-permute-start | bytes 98312 | tf_op jit(solution)/shard_map/ppermute | solution.py:24
  8.9 3.6 %collective-permute-start.2 = (f32[8,128]{1,0:T(8,128)S(1)}, f32[8,128]{1,0:T(8,128)S(1)}, u32[]{:S(2)}, u32[]{:S(2)}) collective-permute-start(f32[8,128]{1,0:T(8,128)S(1)} %slice.3), channel_id=1, source_target_pairs={{0,4},{4,0},{1,5},{5,1},{2,6},{6,2},{3,7},{7,3},{8,12},{12,8},{9,1... | collective-permute-start | bytes 12296 | tf_op jit(solution)/shard_map/ppermute | solution.py:24
  14.9 5.4 %collective-permute-start.5 = (f32[2,32,256]{2,1,0:T(8,128)S(1)}, f32[2,32,256]{2,1,0:T(8,128)S(1)}, u32[]{:S(2)}, u32[]{:S(2)}) collective-permute-start(f32[2,32,256]{2,1,0:T(8,128)S(1)} %get-tuple-element.30.packed), channel_id=1, source_target_pairs={{0,3},{1,2},{2,1},{3,0},{4,7},{5,6},{6,5},{7,4},{8,11},{9,10},{10,... | collective-permute-start | bytes 196616 | tf_op jit(solution)/shard_map/ppermute | solution.py:24
  15.1 5.3 %collective-permute-start.4 = (f32[2,32,256]{2,1,0:T(8,128)S(1)}, f32[2,32,256]{2,1,0:T(8,128)S(1)}, u32[]{:S(2)}, u32[]{:S(2)}) collective-permute-start(f32[2,32,256]{2,1,0:T(8,128)S(1)} %get-tuple-element.30.packed), channel_id=1, source_target_pairs={{0,1},{1,0},{2,3},{3,2},{4,5},{5,4},{6,7},{7,6},{8,9},{9,8},{10,11... | collective-permute-start | bytes 196616 | tf_op jit(solution)/shard_map/ppermute | solution.py:24
  16.6 3.7 %collective-permute-start.6 = (f32[32,128]{1,0:T(8,128)S(1)}, f32[32,128]{1,0:T(8,128)S(1)}, u32[]{:S(2)}, u32[]{:S(2)}) collective-permute-start(f32[32,128]{1,0:T(8,128)S(1)} %get-tuple-element.28.rows), channel_id=1, source_target_pairs={{0,2},{1,3},{2,0},{3,1},{4,6},{5,7},{6,4},{7,5},{8,10},{9,11},{10,... | collective-permute-start | bytes 49160 | tf_op jit(solution)/shard_map/ppermute | solution.py:24
  21.3 7.1 %collective-permute-start.7 = (f32[240,128]{1,0:T(8,128)S(1)}, f32[240,128]{1,0:T(8,128)S(1)}, u32[]{:S(2)}, u32[]{:S(2)}) collective-permute-start(f32[240,128]{1,0:T(8,128)S(1)} %bitcast.4), channel_id=1, source_target_pairs={{0,4},{4,0},{1,5},{5,1},{2,6},{6,2},{3,7},{7,3},{8,12},{12,8},{9,1... | collective-permute-start | bytes 368648 | tf_op jit(solution)/shard_map/ppermute | solution.py:24

commit v4 on v3

--- a/solution.py
+++ b/solution.py
@@ -55,45 +55,70 @@
 def spread(values, first):
     lane = lane_index(values.shape)
     moved = pltpu.roll(values, (LANES - first) % LANES, 1) if first else values
-    result = jnp.where(lane < 4, moved, 0.0)
-    step = 4
-    while step < LANES:
-        result = result + pltpu.roll(result, step, 1)
-        step *= 2
-    return result
-
-
-def totals_kernel(place, side, mag, first_out, second_out, total_out, rows_out, columns_out):
+    alone = jnp.where(lane < 4, moved, 0.0)
+    four = (alone + pltpu.roll(alone, 4, 1)) + (pltpu.roll(alone, 8, 1) + pltpu.roll(alone, 12, 1))
+    parts = [four] + [pltpu.roll(four, step, 1) for step in range(16, LANES, 16)]
+    while len(parts) > 1:
+        parts = [a + b for a, b in zip(parts[::2], parts[1::2])]
+    return parts[0]
+
+
+def totals_kernel(
+    place, side, mag, first_out, second_out, total_out, rows_out, columns_out, held, plane, sems
+):
     depth = side.shape[1]
     z = place[0]
-    for c in range(2):
-        low0 = side[c, 0]
-        low1 = low0 + side[c, 1]
-        before = low1
-        for layer in range(2, depth - 1):
-            before = before + side[c, layer]
-        total = before + side[c, depth - 1]
-        odd = z % 2 == 1
-        first_out[c, 0] = jnp.where(odd, low0, before)
-        first_out[c, 1] = jnp.where(odd, low1, total)
-        upward = odd | (z == 0)
-        second_out[c, 0] = jnp.where(upward, before, low0)
-        second_out[c, 1] = jnp.where(upward, total, low1)
-        total_out[c] = total
-    rows = mag[...]
-    lane = lane_index(rows.shape)
+    size = depth // 4
+    fetch_plane = pltpu.make_async_copy(mag, plane, sems.at[8])
+    fetch_plane.start()
+    fetches = []
+    for piece in range(4):
+        for c in range(2):
+            layers = pl.ds(piece * size, size)
+            fetches.append(
+                pltpu.make_async_copy(
+                    side.at[c, layers], held.at[c, layers], sems.at[piece * 2 + c]
+                )
+            )
+            fetches[-1].start()
+    fetch_plane.wait()
+    rows = columns = plane[...]
+    lane, row = lane_index(rows.shape), row_index(rows.shape)
     step = 1
     while step < LANES:
         rows = rows + jnp.where(lane >= step, pltpu.roll(rows, step, 1), 0.0)
         step *= 2
     rows_out[...] = rows
-    columns = mag[...]
-    row = row_index(columns.shape)
     step = 1
     while step < columns.shape[0]:
         columns = columns + jnp.where(row >= step, pltpu.roll(columns, step, 0), 0.0)
         step *= 2
     columns_out[...] = columns
+
+    odd = z % 2 == 1
+    upward = odd | (z == 0)
+    low = [None, None]
+    sums = [None, None]
+    for piece in range(4):
+        for c in range(2):
+            fetches[piece * 2 + c].wait()
+            total = sums[c]
+            for layer in range(piece * size, (piece + 1) * size):
+                if layer == depth - 1:
+                    before = total
+                total = held[c, layer] if layer == 0 else total + held[c, layer]
+                if layer == 0:
+                    low0 = total
+                if layer == 1:
+                    low[c] = (low0, total)
+            sums[c] = total
+            if piece == 3:
+                low0, low1 = low[c]
+                first_out[c, 0] = jnp.where(odd, low0, before)
+                first_out[c, 1] = jnp.where(odd, low1, total)
+                second_out[c, 0] = jnp.where(upward, before, low0)
+                second_out[c, 1] = jnp.where(upward, total, low1)
+                total_out[c] = total
 
 
 def pack_kernel(side, packed_out, rows_out, running):
@@ -115,7 +140,7 @@
 def z_kernel(
     count, depth, far, place, first, second, total, columns, column_carry, rows, packed, *rest
 ):
-    others, (x_out, ext_out, base_out) = rest[:far], rest[far:]
+    others, (x_out, ext_out, flat_out) = rest[:far], rest[far:]
     z, y = place[0], place[1]
     odd = z % 2 == 1
     for c in range(2):
@@ -127,32 +152,27 @@
             carry = carry + jnp.where((z == 2) | (z == 3), near_b[1], 0.0)
         for step, other in zip(far_steps(count), others):
             carry = carry + jnp.where((z ^ step) < z, other[c], 0.0)
-        above = carry + total[c]
-        layers = (carry - (low[1] - low[0]), carry, above + high[0], above + high[1])
-        for k in range(4):
+        if c == 0:
+            shared = 0.5 * rows[...] - carry
+        else:
+            before = jnp.where(y > 0, column_carry[7:8, :], 0.0)
+            shared = carry - 0.5 * (columns[...] + before)
+        layers = (low[0] - low[1], None, total[c] + high[0], total[c] + high[1])
+        flat_out[c] = shared
+        for k in (0, 2, 3):
             ext_out[c, k] = layers[k]
-        if c == 0:
-            base = rows[...]
-        else:
-            base = -0.5 * (columns[...] + jnp.where(y > 0, column_carry[7:8, :], 0.0))
-            base_out[...] = base
-        lane = lane_index(carry.shape)
-        everywhere = spread(pltpu.roll(carry, 2, 1), 0)
+        ext_out[c, 1] = jnp.zeros_like(carry)
         for tile in range(2):
-            slot = lane // 4 + tile * GROUP
             values = packed[c, :, pl.ds(tile * LANES, LANES)]
-            inside = (slot >= 2) & (slot < depth + 2)
-            values = values + jnp.where(inside, everywhere, 0.0)
-            for k, at in enumerate((0, 1, depth + 2, depth + 3)):
+            slots = [(0, layers[0]), (depth + 2, layers[2]), (depth + 3, layers[3])]
+            for at, layer in slots + [(depth + 4, shared), (depth + 5, rows[...])]:
                 if at // GROUP == tile:
-                    values = values + columns_at(layers[k], at)
-            if (depth + 4) // GROUP == tile:
-                values = values + columns_at(base, depth + 4)
+                    values = values + columns_at(layer, at)
             x_out[c, :, pl.ds(tile * LANES, LANES)] = values
 
 
 def x_kernel(
-    counts, depth, place, packed, first, second, far_rows, rows, base, ext, edges,
+    counts, depth, place, packed, first, second, far_rows, rows, shared, beside, edges,
     strips_out, flat_out, ext_out, y_out,
 ):
     count_z, count_y, count_x = counts
@@ -160,12 +180,13 @@
     z, y, x = place[0], place[1], place[2]
     odd = x % 2 == 1
     base_tile, base_lane = (depth + 4) // GROUP, 4 * ((depth + 4) % GROUP)
+    rows_tile, rows_lane = (depth + 5) // GROUP, 4 * ((depth + 5) % GROUP)
 
     def tile_of(ref, c, tile):
         return ref[c, :, pl.ds(tile * LANES, LANES)]
 
     def row_totals(ref):
-        return tile_of(ref, 0, base_tile)[:, base_lane + 1 : base_lane + 2]
+        return tile_of(ref, 0, rows_tile)[:, rows_lane + 1 : rows_lane + 2]
 
     own_total = rows[...][:, LANES - 1 :]
     total_a, total_b = row_totals(first), row_totals(second)
@@ -195,7 +216,7 @@
             carry = jnp.where(q < 2, row_carry - left_total, row_carry)
         else:
             carry = jnp.where(q < 2, row_carry, row_carry + own_total)
-        base_y = 0.5 * (spread(merged[0][base_tile], base_lane) + carry)
+        base_y = spread(merged[0][base_tile], base_lane) + 0.5 * carry
         base_x = spread(merged[1][base_tile], base_lane)
         for tile in range(2):
             slot = lane // 4 + tile * GROUP
@@ -209,14 +230,14 @@
             strips_out[0, :, place_at] = jnp.where(inside, base_x + merged[1][tile], 0.0)
             strips_out[1, :, place_at] = jnp.where(inside, base_y - merged[0][tile], 0.0)
 
-    base_x = base[...]
-    base_y = 0.5 * (rows[...] + row_carry)
-    flat_out[0] = base_x + ext[1, 1]
-    flat_out[1] = base_y - ext[0, 1]
+    flat_x = shared[1]
+    flat_y = shared[0] + 0.5 * row_carry
+    flat_out[0] = flat_x
+    flat_out[1] = flat_y
     for k in range(4):
         inside = (z > 0) if k < 2 else (z < count_z - 1)
-        ext_out[0, k] = jnp.where(inside, base_x + ext[1, k], 0.0)
-        ext_out[1, k] = jnp.where(inside, base_y - ext[0, k], 0.0)
+        ext_out[0, k] = jnp.where(inside, flat_x + beside[1, k], 0.0)
+        ext_out[1, k] = jnp.where(inside, flat_y - beside[0, k], 0.0)
 
     slots = slot_rows(depth)
     for message in range(y_out.shape[0]):
@@ -508,7 +529,7 @@
 
 
 def call(kernel, shapes, args, scratch=(), limit=16, far_out=0, far_in=(), aliases={}):
-    vmem, far = pl.BlockSpec(memory_space=pltpu.VMEM), pl.BlockSpec(memory_space=pl.ANY)
+    vmem, far = pl.BlockSpec(memory_space=pltpu.VMEM), pl.BlockSpec(memory_space=pltpu.HBM)
     specs = [far if k in far_in else vmem for k in range(1, len(args))]
     return pl.pallas_call(
         kernel,
@@ -546,8 +567,12 @@
     place = jnp.stack([lax.axis_index(axis) for axis in ("gz", "gy", "gx")]).astype(jnp.int32)
     plane, block = (height, width), (2, height, width)
 
-    first, second, total, rows, columns = call(
-        totals_kernel, [(2, 2) + plane, (2, 2) + plane, block, plane, plane], [place, side, mag]
+    first, second, total, rows, columns, side = call(
+        totals_kernel,
+        [(2, 2) + plane, (2, 2) + plane, block, plane, plane, side.shape],
+        [place, side, mag],
+        [plane, pltpu.SemaphoreType.DMA((9,))],
+        far_in=(1, 2),
     )
     first = swap_first(first, "gz")
     second = swap_second(second, "gz") if count_z > 2 else first
@@ -567,9 +592,9 @@
         [(2, depth * height, width)],
     )
     far = len(others)
-    packed, ext, base = call(
+    packed, beside, shared = call(
         functools.partial(z_kernel, count_z, depth, far),
-        [(2, height, 2 * LANES), (2, 4) + plane, plane],
+        [(2, height, 2 * LANES), (2, 4) + plane, block],
         [place, first, second, total, columns, column_carry, rows, packed, *others],
     )
     first = swap_first(packed, "gx")
@@ -585,7 +610,7 @@
     strips, flat, ext, edge_rows = call(
         functools.partial(x_kernel, counts, depth),
         [(2, height, 4 * LANES), block, (2, 4) + plane, (messages, message_rows, width)],
-        [place, packed, first, second, far_rows, rows, base, ext, edges],
+        [place, packed, first, second, far_rows, rows, shared, beside, edges],
     )
     first = swap_first(edge_rows[0], "gy")
     second = swap_second(edge_rows[1], "gy") if count_y > 2 else first

time: 33.2 us -> 35.1 us (1.057)
  Pallas kernels: 14.1 us -> 16 us
    pallas_call x6, Pallas kernels: 14.1 us -> 16 us  [call(): pl.pallas_call(kernel, out_shape=[jax.ShapeDtypeStruct(shape, jnp.float32...]
    unnamed x6 -> x4, local copies, waits for them, and re-layouts: 2.13 us -> 2.13 us
  transfers between devices with their start and end apart: 8 -> 8, of which waited for: 3 -> 3; matrix products, arithmetic and copies ran while one was open for 0% -> 0% of each run, Pallas kernels for 20% -> 19%
where the time goes in v4:
time: 35.1 us; the launch traced here: 34.9 us
  Pallas kernels  16 us (46%)
  starting transfers between devices  11 us (31%)
  waiting for transfers between devices  5.64 us (16%)
  local copies, waits for them, and re-layouts  2.13 us (6%)
    pallas_call x6, Pallas kernels, call(): pl.pallas_call(kernel, out_shape=[jax.ShapeDtypeStruct(shape, jnp.float32...  16 us
    ppermute x8, starting transfers between devices, swap(): return lax.ppermute(part, axis, [(i, partner(i)) for i in range(count)])  11 us
    ppermute x8, waiting for transfers between devices, swap(): return lax.ppermute(part, axis, [(i, partner(i)) for i in range(count)])  5.64 us
    unnamed x4, local copies, waits for them, and re-layouts  2.13 us
  transfers between devices with their start and end apart: 8, of which 3 were waited for; matrix products, arithmetic and copies ran while one was open for 0% of the time, Pallas kernels for 19%

profile of v4, /device:TPU:0, one launch (start us, length us, event | category | flops | bytes accessed | tf_op | source)
XLA Modules:
  0.0 34.9 jit_solution(11129451196978751650)
XLA Ops:
  0.0 0.1 pad_add_fusion.place._
  0.1 0.0 copy-start
  0.1 1.4 %copy-done = f32[2,48,32,128]{3,2,1,0:T(8,128)S(1)} copy-done((f32[2,48,32,128]{3,2,1,0:T(8,128)S(1)}, f32[2,48,32,128]{3,2,1,0:T(8,128)}, u32[]{:S(2)}) %copy-start) | copy-done | bytes 1572888
  1.5 0.0 copy-start.1
  1.5 0.7 %copy-done.1 = f32[32,128]{1,0:T(8,128)S(1)} copy-done((f32[32,128]{1,0:T(8,128)S(1)}, f32[32,128]{1,0:T(8,128)}, u32[]{:S(2)}) %copy-start.1) | copy-done | bytes 16408
  2.2 3.3 %shard_map.28 = (f32[2,2,32,128]{3,2,1,0:T(8,128)S(1)}, f32[2,2,32,128]{3,2,1,0:T(8,128)S(1)}, f32[2,32,128]{2,1,0:T(8,128)S(1)}, f32[32,128]{1,0:T(8,128)S(1)},...) custom-call(s32[3]{0:T(128)S(1)} %pad_add_fusion.place._, f32[2,48,32,128]{3,2,1,0:T(8,128)S(1)} %copy-done, ...), custom_call_target="tpu_custom_call" | custom-call | tf_op jit(solution)/shard_map/pallas_call | solution.py:534
  5.5 3.1 %collective-permute-start = (f32[2,2,32,128]{3,2,1,0:T(8,128)S(1)}, f32[2,2,32,128]{3,2,1,0:T(8,128)S(1)}, u32[]{:S(2)}, u32[]{:S(2)}) collective-permute-start(f32[2,2,32,128]{3,2,1,0:T(8,128)S(1)} %get-tuple-element.25), channel_id=1, source_target_pairs={{0,8},{8,0},{16,24},{24,16},{1,9},{9,1},{17,25},{25,17},{2,10},{10... | collective-permute-start | bytes 196616 | tf_op jit(solution)/shard_map/ppermute | solution.py:24
  8.6 2.5 %collective-permute-start.1 = (f32[2,2,32,128]{3,2,1,0:T(8,128)S(1)}, f32[2,2,32,128]{3,2,1,0:T(8,128)S(1)}, u32[]{:S(2)}, u32[]{:S(2)}) collective-permute-start(f32[2,2,32,128]{3,2,1,0:T(8,128)S(1)} %get-tuple-element.26), channel_id=1, source_target_pairs={{0,24},{8,16},{16,8},{24,0},{1,25},{9,17},{17,9},{25,1},{2,26},{10... | collective-permute-start | bytes 196616 | tf_op jit(solution)/shard_map/ppermute | solution.py:24
  11.1 0.1 collective-permute-start.3
  11.2 1.5 %collective-permute-start.2 = (f32[8,128]{1,0:T(8,128)S(1)}, f32[8,128]{1,0:T(8,128)S(1)}, u32[]{:S(2)}, u32[]{:S(2)}) collective-permute-start(f32[8,128]{1,0:T(8,128)S(1)} %slice.3), channel_id=1, source_target_pairs={{0,4},{4,0},{1,5},{5,1},{2,6},{6,2},{3,7},{7,3},{8,12},{12,8},{9,1... | collective-permute-start | bytes 12296 | tf_op jit(solution)/shard_map/ppermute | solution.py:24
  12.7 1.1 %shard_map.29 = (f32[2,32,256]{2,1,0:T(8,128)S(1)}, f32[2,4,48,128]{3,2,1,0:T(8,128)S(1)}) custom-call(s32[3]{0:T(128)S(1)} %pad_add_fusion.place._, f32[2,48,32,128]{3,2,1,0:T(8,128)S(1)} %get-tuple-element.30.refs_0_.side), custom_call_target="tpu_custom_call" | custom-call | tf_op jit(solution)/shard_map/pallas_call | solution.py:534
  13.8 1.0 %collective-permute-done.2.column_carry = f32[8,128]{1,0:T(8,128)S(1)} collective-permute-done((f32[8,128]{1,0:T(8,128)S(1)}, f32[8,128]{1,0:T(8,128)S(1)}, u32[]{:S(2)}, u32[]{:S(2)}) %collective-permute-start.2) | collective-permute-done | bytes 4128 | tf_op jit(solution)/shard_map/ppermute | solution.py:24
  14.8 1.4 %collective-permute-done.3.rest_0_ = f32[2,32,128]{2,1,0:T(8,128)S(1)} collective-permute-done((f32[2,32,128]{2,1,0:T(8,128)S(1)}, f32[2,32,128]{2,1,0:T(8,128)S(1)}, u32[]{:S(2)}, u32[]{:S(2)}) %collective-permute-start.3) | collective-permute-done | bytes 32800 | tf_op jit(solution)/shard_map/ppermute | solution.py:24
  16.2 0.0 collective-permute-done.first
  16.2 0.0 collective-permute-done.1.second
  16.2 0.7 %shard_map.30 = (f32[2,32,256]{2,1,0:T(8,128)S(1)}, f32[2,4,32,128]{3,2,1,0:T(8,128)S(1)}, f32[2,32,128]{2,1,0:T(8,128)S(1)}) custom-call(s32[3]{0:T(128)S(1)} %pad_add_fusion.place._, f32[2,2,32,128]{3,2,1,0:T(8,128)S(1)} %collective-permute-done.first, f32[2,2,32,128]{3,2,1,0:T(8,128)S(1)} %collective-permute-done.1.second, ...), custom_call_target="tpu_custom_call" | custom-call | tf_op jit(solution)/shard_map/pallas_call | solution.py:534
  16.9 0.2 collective-permute-start.5
  17.1 1.5 %collective-permute-start.4 = (f32[2,32,256]{2,1,0:T(8,128)S(1)}, f32[2,32,256]{2,1,0:T(8,128)S(1)}, u32[]{:S(2)}, u32[]{:S(2)}) collective-permute-start(f32[2,32,256]{2,1,0:T(8,128)S(1)} %get-tuple-element.32.packed), channel_id=1, source_target_pairs={{0,1},{1,0},{2,3},{3,2},{4,5},{5,4},{6,7},{7,6},{8,9},{9,8},{10,11... | collective-permute-start | bytes 196616 | tf_op jit(solution)/shard_map/ppermute | solution.py:24
  18.6 0.5 %collective-permute-start.6 = (f32[32,128]{1,0:T(8,128)S(1)}, f32[32,128]{1,0:T(8,128)S(1)}, u32[]{:S(2)}, u32[]{:S(2)}) collective-permute-start(f32[32,128]{1,0:T(8,128)S(1)} %get-tuple-element.29.rows), channel_id=1, source_target_pairs={{0,2},{1,3},{2,0},{3,1},{4,6},{5,7},{6,4},{7,5},{8,10},{9,11},{10,... | collective-permute-start | bytes 49160 | tf_op jit(solution)/shard_map/ppermute | solution.py:24
  19.1 3.2 %collective-permute-done.6.far_rows = f32[32,128]{1,0:T(8,128)S(1)} collective-permute-done((f32[32,128]{1,0:T(8,128)S(1)}, f32[32,128]{1,0:T(8,128)S(1)}, u32[]{:S(2)}, u32[]{:S(2)}) %collective-permute-start.6) | collective-permute-done | bytes 16416 | tf_op jit(solution)/shard_map/ppermute | solution.py:24
  22.3 0.0 collective-permute-done.5.second
  22.3 0.0 collective-permute-done.4.first
  22.3 0.9 %shard_map.31 = (f32[2,32,512]{2,1,0:T(8,128)S(1)}, f32[2,32,128]{2,1,0:T(8,128)S(1)}, f32[2,4,32,128]{3,2,1,0:T(8,128)S(1)}, f32[1,240,128]{2,1,0:T(8,128)S(1)}) custom-call(s32[3]{0:T(128)S(1)} %pad_add_fusion.place._, f32[2,32,256]{2,1,0:T(8,128)S(1)} %get-tuple-element.32.packed, f32[2,32,256]{2,1,0:T(8,128)S(1)} %collective-permute-done.4.first, ...), custom_call_target="tpu_custom_call" | custom-call | tf_op jit(solution)/shard_map/pallas_call | solution.py:534
  23.2 1.6 %collective-permute-start.7 = (f32[240,128]{1,0:T(8,128)S(1)}, f32[240,128]{1,0:T(8,128)S(1)}, u32[]{:S(2)}, u32[]{:S(2)}) collective-permute-start(f32[240,128]{1,0:T(8,128)S(1)} %bitcast.4), channel_id=1, source_target_pairs={{0,4},{4,0},{1,5},{5,1},{2,6},{6,2},{3,7},{7,3},{8,12},{12,8},{9,1... | collective-permute-start | bytes 368648 | tf_op jit(solution)/shard_map/ppermute | solution.py:24
  24.8 5.5 %shard_map.32 = (f32[2,52,48,128]{3,2,1,0:T(8,128)S(1)}, f32[3,52,48,128]{3,2,1,0:T(8,128)S(1)}, f32[3,52,48,128]{3,2,1,0:T(8,128)S(1)}, f32[3,48,32,128]{3,2,1,0:T(8,128)}) custom-call(s32[3]{0:T(128)S(1)} %pad_add_fusion.place._, f32[2,48,32,128]{3,2,1,0:T(8,128)S(1)} %get-tuple-element.30.refs_0_.side, f32[2,32,128]{2,1,0:T(8,128)S(1)} %get-tuple-element.38.flat, ...), custom_call_target="tpu_custom_call" | custom-call | tf_op jit(solution)/shard_map/pallas_call | solution.py:534
  30.3 0.0 collective-permute-done.7.first.second
  30.3 4.6 %shard_map.33 = (f32[2,52,48,128]{3,2,1,0:T(8,128)S(1)}, f32[3,52,48,128]{3,2,1,0:T(8,128)S(1)}, f32[3,52,48,128]{3,2,1,0:T(8,128)S(1)}, f32[3,48,32,128]{3,2,1,0:T(8,128)}) custom-call(s32[3]{0:T(128)S(1)} %pad_add_fusion.place._, ...), custom_call_target="tpu_custom_call", output_to_operand_aliasing={{0}: (4, {}), {1}: (5, {}), {2}: (6, {}), {3}: (7, {})} | custom-call | tf_op jit(solution)/shard_map/pallas_call | solution.py:534
  (1 shorter events, 0.0 us)
Async XLA Ops:
  0.1 1.4 %copy-start = (f32[2,48,32,128]{3,2,1,0:T(8,128)S(1)}, f32[2,48,32,128]{3,2,1,0:T(8,128)}, u32[]{:S(2)}) copy-start(f32[2,48,32,128]{3,2,1,0:T(8,128)} %side.1) | copy-start | bytes 4718596
  1.5 0.7 %copy-start.1 = (f32[32,128]{1,0:T(8,128)S(1)}, f32[32,128]{1,0:T(8,128)}, u32[]{:S(2)}) copy-start(f32[32,128]{1,0:T(8,128)} %mag.1) | copy-start | bytes 49156
  5.5 10.7 %collective-permute-start = (f32[2,2,32,128]{3,2,1,0:T(8,128)S(1)}, f32[2,2,32,128]{3,2,1,0:T(8,128)S(1)}, u32[]{:S(2)}, u32[]{:S(2)}) collective-permute-start(f32[2,2,32,128]{3,2,1,0:T(8,128)S(1)} %get-tuple-element.25), channel_id=1, source_target_pairs={{0,8},{8,0},{16,24},{24,16},{1,9},{9,1},{17,25},{25,17},{2,10},{10... | collective-permute-start | bytes 196616 | tf_op jit(solution)/shard_map/ppermute | solution.py:24
  8.6 7.6 %collective-permute-start.1 = (f32[2,2,32,128]{3,2,1,0:T(8,128)S(1)}, f32[2,2,32,128]{3,2,1,0:T(8,128)S(1)}, u32[]{:S(2)}, u32[]{:S(2)}) collective-permute-start(f32[2,2,32,128]{3,2,1,0:T(8,128)S(1)} %get-tuple-element.26), channel_id=1, source_target_pairs={{0,24},{8,16},{16,8},{24,0},{1,25},{9,17},{17,9},{25,1},{2,26},{10... | collective-permute-start | bytes 196616 | tf_op jit(solution)/shard_map/ppermute | solution.py:24
  11.1 5.2 %collective-permute-start.3 = (f32[2,32,128]{2,1,0:T(8,128)S(1)}, f32[2,32,128]{2,1,0:T(8,128)S(1)}, u32[]{:S(2)}, u32[]{:S(2)}) collective-permute-start(f32[2,32,128]{2,1,0:T(8,128)S(1)} %get-tuple-element.27.total), channel_id=1, source_target_pairs={{0,16},{8,24},{16,0},{24,8},{1,17},{9,25},{17,1},{25,9},{2,18},{10... | collective-permute-start | bytes 98312 | tf_op jit(solution)/shard_map/ppermute | solution.py:24
  11.2 3.6 %collective-permute-start.2 = (f32[8,128]{1,0:T(8,128)S(1)}, f32[8,128]{1,0:T(8,128)S(1)}, u32[]{:S(2)}, u32[]{:S(2)}) collective-permute-start(f32[8,128]{1,0:T(8,128)S(1)} %slice.3), channel_id=1, source_target_pairs={{0,4},{4,0},{1,5},{5,1},{2,6},{6,2},{3,7},{7,3},{8,12},{12,8},{9,1... | collective-permute-start | bytes 12296 | tf_op jit(solution)/shard_map/ppermute | solution.py:24
  16.9 5.4 %collective-permute-start.5 = (f32[2,32,256]{2,1,0:T(8,128)S(1)}, f32[2,32,256]{2,1,0:T(8,128)S(1)}, u32[]{:S(2)}, u32[]{:S(2)}) collective-permute-start(f32[2,32,256]{2,1,0:T(8,128)S(1)} %get-tuple-element.32.packed), channel_id=1, source_target_pairs={{0,3},{1,2},{2,1},{3,0},{4,7},{5,6},{6,5},{7,4},{8,11},{9,10},{10,... | collective-permute-start | bytes 196616 | tf_op jit(solution)/shard_map/ppermute | solution.py:24
  17.1 5.3 %collective-permute-start.4 = (f32[2,32,256]{2,1,0:T(8,128)S(1)}, f32[2,32,256]{2,1,0:T(8,128)S(1)}, u32[]{:S(2)}, u32[]{:S(2)}) collective-permute-start(f32[2,32,256]{2,1,0:T(8,128)S(1)} %get-tuple-element.32.packed), channel_id=1, source_target_pairs={{0,1},{1,0},{2,3},{3,2},{4,5},{5,4},{6,7},{7,6},{8,9},{9,8},{10,11... | collective-permute-start | bytes 196616 | tf_op jit(solution)/shard_map/ppermute | solution.py:24
  18.6 3.7 %collective-permute-start.6 = (f32[32,128]{1,0:T(8,128)S(1)}, f32[32,128]{1,0:T(8,128)S(1)}, u32[]{:S(2)}, u32[]{:S(2)}) collective-permute-start(f32[32,128]{1,0:T(8,128)S(1)} %get-tuple-element.29.rows), channel_id=1, source_target_pairs={{0,2},{1,3},{2,0},{3,1},{4,6},{5,7},{6,4},{7,5},{8,10},{9,11},{10,... | collective-permute-start | bytes 49160 | tf_op jit(solution)/shard_map/ppermute | solution.py:24
  23.2 7.1 %collective-permute-start.7 = (f32[240,128]{1,0:T(8,128)S(1)}, f32[240,128]{1,0:T(8,128)S(1)}, u32[]{:S(2)}, u32[]{:S(2)}) collective-permute-start(f32[240,128]{1,0:T(8,128)S(1)} %bitcast.4), channel_id=1, source_target_pairs={{0,4},{4,0},{1,5},{5,1},{2,6},{6,2},{3,7},{7,3},{8,12},{12,8},{9,1... | collective-permute-start | bytes 368648 | tf_op jit(solution)/shard_map/ppermute | solution.py:24

commit v5 on v4

--- a/solution.py
+++ b/solution.py
@@ -13,6 +13,7 @@
 LANES = 128
 PAD = 8
 GROUP = LANES // 4
+LONG = pl.CostEstimate(flops=10**10, bytes_accessed=10**5, transcendentals=0)
 
 
 def near(index, count):
@@ -63,26 +64,13 @@
     return parts[0]
 
 
-def totals_kernel(
-    place, side, mag, first_out, second_out, total_out, rows_out, columns_out, held, plane, sems
-):
-    depth = side.shape[1]
-    z = place[0]
-    size = depth // 4
-    fetch_plane = pltpu.make_async_copy(mag, plane, sems.at[8])
-    fetch_plane.start()
-    fetches = []
-    for piece in range(4):
-        for c in range(2):
-            layers = pl.ds(piece * size, size)
-            fetches.append(
-                pltpu.make_async_copy(
-                    side.at[c, layers], held.at[c, layers], sems.at[piece * 2 + c]
-                )
-            )
-            fetches[-1].start()
-    fetch_plane.wait()
-    rows = columns = plane[...]
+def place_kernel(place, place_out):
+    for k in range(place.shape[0]):
+        place_out[k] = place[k]
+
+
+def plane_kernel(_, mag, rows_out, columns_out):
+    rows = columns = mag[...]
     lane, row = lane_index(rows.shape), row_index(rows.shape)
     step = 1
     while step < LANES:
@@ -95,30 +83,24 @@
         step *= 2
     columns_out[...] = columns
 
-    odd = z % 2 == 1
-    upward = odd | (z == 0)
-    low = [None, None]
-    sums = [None, None]
-    for piece in range(4):
-        for c in range(2):
-            fetches[piece * 2 + c].wait()
-            total = sums[c]
-            for layer in range(piece * size, (piece + 1) * size):
-                if layer == depth - 1:
-                    before = total
-                total = held[c, layer] if layer == 0 else total + held[c, layer]
-                if layer == 0:
-                    low0 = total
-                if layer == 1:
-                    low[c] = (low0, total)
-            sums[c] = total
-            if piece == 3:
-                low0, low1 = low[c]
-                first_out[c, 0] = jnp.where(odd, low0, before)
-                first_out[c, 1] = jnp.where(odd, low1, total)
-                second_out[c, 0] = jnp.where(upward, before, low0)
-                second_out[c, 1] = jnp.where(upward, total, low1)
-                total_out[c] = total
+
+def totals_kernel(place, side, columns, first_out, second_out, total_out, last_out):
+    depth = side.shape[1]
+    odd = place[0] % 2 == 1
+    upward = odd | (place[0] == 0)
+    for c in range(2):
+        low0 = side[c, 0]
+        low1 = low0 + side[c, 1]
+        before = low1
+        for layer in range(2, depth - 1):
+            before = before + side[c, layer]
+        total = before + side[c, depth - 1]
+        first_out[c, 0] = jnp.where(odd, low0, before)
+        first_out[c, 1] = jnp.where(odd, low1, total)
+        second_out[c, 0] = jnp.where(upward, before, low0)
+        second_out[c, 1] = jnp.where(upward, total, low1)
+        total_out[c] = total
+    last_out[...] = columns[pl.ds(columns.shape[0] - 8, 8), :]
 
 
 def pack_kernel(side, packed_out, rows_out, running):
@@ -528,7 +510,7 @@
     stepper.run(outer_tiles(height), True, out, block, sems)
 
 
-def call(kernel, shapes, args, scratch=(), limit=16, far_out=0, far_in=(), aliases={}):
+def call(kernel, shapes, args, scratch=(), limit=16, far_out=0, far_in=(), aliases={}, cost=None):
     vmem, far = pl.BlockSpec(memory_space=pltpu.VMEM), pl.BlockSpec(memory_space=pltpu.HBM)
     specs = [far if k in far_in else vmem for k in range(1, len(args))]
     return pl.pallas_call(
@@ -541,7 +523,8 @@
             for shape in scratch
         ],
         input_output_aliases=aliases,
-        compiler_params=pltpu.CompilerParams(vmem_limit_bytes=limit * 2**20),
+        cost_estimate=cost,
+        compiler_params=pltpu.CompilerParams(vmem_limit_bytes=int(limit * 2**20)),
     )(*args)
 
 
@@ -566,13 +549,20 @@
     _, depth, height, width = side.shape
     place = jnp.stack([lax.axis_index(axis) for axis in ("gz", "gy", "gx")]).astype(jnp.int32)
     plane, block = (height, width), (2, height, width)
-
-    first, second, total, rows, columns, side = call(
+    smem = pl.BlockSpec(memory_space=pltpu.SMEM)
+    place = pl.pallas_call(
+        place_kernel,
+        out_shape=jax.ShapeDtypeStruct(place.shape, jnp.int32),
+        in_specs=[smem],
+        out_specs=smem,
+        cost_estimate=LONG,
+    )(place)
+
+    rows, columns = call(plane_kernel, [plane, plane], [place, mag])
+    first, second, total, last = call(
         totals_kernel,
-        [(2, 2) + plane, (2, 2) + plane, block, plane, plane, side.shape],
-        [place, side, mag],
-        [plane, pltpu.SemaphoreType.DMA((9,))],
-        far_in=(1, 2),
+        [(2, 2) + plane, (2, 2) + plane, block, (8, width)],
+        [place, side, columns],
     )
     first = swap_first(first, "gz")
     second = swap_second(second, "gz") if count_z > 2 else first
@@ -582,7 +572,7 @@
     ]
     direct = count_y == 2 and count_x in (2, 4)
     if direct:
-        column_carry = swap_first(columns[-8:], "gy")
+        column_carry = swap_first(last, "gy")
     else:
         row_carry, column_carry = gathered_carries(rows, columns)
     packed, edges = call(

time: 35.1 us -> 34 us (0.969)
  local copies, waits for them, and re-layouts: 2.13 us -> 0.66 us
  other arithmetic: 0.08 us -> 0.66 us
    pallas_call x6 -> x7, Pallas kernels: 16 us -> 14.5 us  [call(): pl.pallas_call(kernel, out_shape=[jax.ShapeDtypeStruct(shape, jnp.float32...]
    unnamed x4 -> x6, local copies, waits for them, and re-layouts: 2.13 us -> 0.66 us
    pallas_call x0 -> x1, Pallas kernels: none -> 1.31 us  [local(): pl.pallas_call(place_kernel, out_shape=jax.ShapeDtypeStruct(place.shape,...]
    another operation x1, other arithmetic: 0.08 us -> 0.66 us  [local(): jnp.stack([lax.axis_index(axis) for axis in ('gz', 'gy', 'gx')])]
  transfers between devices with their start and end apart: 8 -> 8, of which waited for: 3 -> 3; matrix products, arithmetic and copies ran while one was open for 0% -> 0% of each run, Pallas kernels for 19% -> 20%
where the time goes in v5:
time: 34 us; the launch traced here: 33.8 us
  Pallas kernels  15.8 us (46%)
  starting transfers between devices  11 us (32%)
  waiting for transfers between devices  5.66 us (17%)
  other arithmetic  0.66 us (2%)
  local copies, waits for them, and re-layouts  0.66 us (2%)
    pallas_call x7, Pallas kernels, call(): pl.pallas_call(kernel, out_shape=[jax.ShapeDtypeStruct(shape, jnp.float32...  14.5 us
    ppermute x8, starting transfers between devices, swap(): return lax.ppermute(part, axis, [(i, partner(i)) for i in range(count)])  11 us
    ppermute x8, waiting for transfers between devices, swap(): return lax.ppermute(part, axis, [(i, partner(i)) for i in range(count)])  5.66 us
    pallas_call x1, Pallas kernels, local(): pl.pallas_call(place_kernel, out_shape=jax.ShapeDtypeStruct(place.shape,...  1.31 us
  transfers between devices with their start and end apart: 8, of which 3 were waited for; matrix products, arithmetic and copies ran while one was open for 0% of the time, Pallas kernels for 20%

profile of v5, /device:TPU:0, one launch (start us, length us, event | category | flops | bytes accessed | tf_op | source)
XLA Modules:
  0.0 33.8 jit_solution(15993131748280952425)
XLA Ops:
  0.0 0.7 %pad_add_fusion.place = s32[3]{0:T(128)} fusion(s32[1]{0:T(128)} %bitcast.2, s32[1]{0:T(128)} %bitcast.1, s32[1]{0:T(128)} %bitcast), kind=kLoop, calls=%fused_computation | loop fusion | flops 6 | bytes 24 | tf_op jit(solution)/shard_map/stack | solution.py:550
  0.7 0.0 copy-start.2
  0.7 0.0 copy-start
  0.7 1.3 %shard_map.28._.place = s32[3]{0:T(128)} custom-call(s32[3]{0:T(128)} %pad_add_fusion.place), custom_call_target="tpu_custom_call" | custom-call | flops 10000000000 | bytes 100000 | tf_op jit(solution)/shard_map/pallas_call | solution.py:553
  2.0 0.0 copy-done.2
  2.0 0.0 copy-start.1
  2.0 0.6 %copy-done.1 = s32[3]{0:T(128)S(1)} copy-done((s32[3]{0:T(128)S(1)}, s32[3]{0:T(128)}, u32[]{:S(2)}) %copy-start.1) | copy-done | bytes 36
  2.7 1.0 %shard_map.29 = (f32[32,128]{1,0:T(8,128)S(1)}, f32[32,128]{1,0:T(8,128)S(1)}) custom-call(s32[3]{0:T(128)S(1)} %copy-done.1, f32[32,128]{1,0:T(8,128)S(1)} %copy-done.2), custom_call_target="tpu_custom_call" | custom-call | tf_op jit(solution)/shard_map/pallas_call | solution.py:516
  3.7 0.0 copy-done
  3.7 0.7 %shard_map.30 = (f32[2,2,32,128]{3,2,1,0:T(8,128)S(1)}, f32[2,2,32,128]{3,2,1,0:T(8,128)S(1)}, f32[2,32,128]{2,1,0:T(8,128)S(1)}, f32[8,128]{1,0:T(8,128)S(1)}) custom-call(s32[3]{0:T(128)S(1)} %copy-done.1, f32[2,48,32,128]{3,2,1,0:T(8,128)S(1)} %copy-done, f32[32,128]{1,0:T(8,128)S(1)} %get-tuple-element.25.columns), custom_call_target="tpu_custom_call" | custom-call | tf_op jit(solution)/shard_map/pallas_call | solution.py:516
  4.3 3.1 %collective-permute-start = (f32[2,2,32,128]{3,2,1,0:T(8,128)S(1)}, f32[2,2,32,128]{3,2,1,0:T(8,128)S(1)}, u32[]{:S(2)}, u32[]{:S(2)}) collective-permute-start(f32[2,2,32,128]{3,2,1,0:T(8,128)S(1)} %get-tuple-element.26), channel_id=1, source_target_pairs={{0,8},{8,0},{16,24},{24,16},{1,9},{9,1},{17,25},{25,17},{2,10},{10... | collective-permute-start | bytes 196616 | tf_op jit(solution)/shard_map/ppermute | solution.py:25
  7.4 2.5 %collective-permute-start.1 = (f32[2,2,32,128]{3,2,1,0:T(8,128)S(1)}, f32[2,2,32,128]{3,2,1,0:T(8,128)S(1)}, u32[]{:S(2)}, u32[]{:S(2)}) collective-permute-start(f32[2,2,32,128]{3,2,1,0:T(8,128)S(1)} %get-tuple-element.27), channel_id=1, source_target_pairs={{0,24},{8,16},{16,8},{24,0},{1,25},{9,17},{17,9},{25,1},{2,26},{10... | collective-permute-start | bytes 196616 | tf_op jit(solution)/shard_map/ppermute | solution.py:25
  9.9 0.1 collective-permute-start.3
  10.0 1.5 %collective-permute-start.2 = (f32[8,128]{1,0:T(8,128)S(1)}, f32[8,128]{1,0:T(8,128)S(1)}, u32[]{:S(2)}, u32[]{:S(2)}) collective-permute-start(f32[8,128]{1,0:T(8,128)S(1)} %get-tuple-element.29), channel_id=1, source_target_pairs={{0,4},{4,0},{1,5},{5,1},{2,6},{6,2},{3,7},{7,3},{8,12},{12,8},{9,1... | collective-permute-start | bytes 12296 | tf_op jit(solution)/shard_map/ppermute | solution.py:25
  11.5 1.1 %shard_map.31 = (f32[2,32,256]{2,1,0:T(8,128)S(1)}, f32[2,4,48,128]{3,2,1,0:T(8,128)S(1)}) custom-call(s32[3]{0:T(128)S(1)} %copy-done.1, f32[2,48,32,128]{3,2,1,0:T(8,128)S(1)} %copy-done), custom_call_target="tpu_custom_call" | custom-call | tf_op jit(solution)/shard_map/pallas_call | solution.py:516
  12.6 1.0 %collective-permute-done.2.column_carry = f32[8,128]{1,0:T(8,128)S(1)} collective-permute-done((f32[8,128]{1,0:T(8,128)S(1)}, f32[8,128]{1,0:T(8,128)S(1)}, u32[]{:S(2)}, u32[]{:S(2)}) %collective-permute-start.2) | collective-permute-done | bytes 4128 | tf_op jit(solution)/shard_map/ppermute | solution.py:25
  13.6 1.4 %collective-permute-done.3.rest_0_ = f32[2,32,128]{2,1,0:T(8,128)S(1)} collective-permute-done((f32[2,32,128]{2,1,0:T(8,128)S(1)}, f32[2,32,128]{2,1,0:T(8,128)S(1)}, u32[]{:S(2)}, u32[]{:S(2)}) %collective-permute-start.3) | collective-permute-done | bytes 32800 | tf_op jit(solution)/shard_map/ppermute | solution.py:25
  15.1 0.0 collective-permute-done.first
  15.1 0.0 collective-permute-done.1.second
  15.1 0.7 %shard_map.32 = (f32[2,32,256]{2,1,0:T(8,128)S(1)}, f32[2,4,32,128]{3,2,1,0:T(8,128)S(1)}, f32[2,32,128]{2,1,0:T(8,128)S(1)}) custom-call(s32[3]{0:T(128)S(1)} %copy-done.1, f32[2,2,32,128]{3,2,1,0:T(8,128)S(1)} %collective-permute-done.first, f32[2,2,32,128]{3,2,1,0:T(8,128)S(1)} %collective-permute-done.1.second, ...), custom_call_target="tpu_custom_call" | custom-call | tf_op jit(solution)/shard_map/pallas_call | solution.py:516
  15.7 0.2 collective-permute-start.5
  15.9 1.5 %collective-permute-start.4 = (f32[2,32,256]{2,1,0:T(8,128)S(1)}, f32[2,32,256]{2,1,0:T(8,128)S(1)}, u32[]{:S(2)}, u32[]{:S(2)}) collective-permute-start(f32[2,32,256]{2,1,0:T(8,128)S(1)} %get-tuple-element.32.packed), channel_id=1, source_target_pairs={{0,1},{1,0},{2,3},{3,2},{4,5},{5,4},{6,7},{7,6},{8,9},{9,8},{10,11... | collective-permute-start | bytes 196616 | tf_op jit(solution)/shard_map/ppermute | solution.py:25
  17.4 0.5 %collective-permute-start.6 = (f32[32,128]{1,0:T(8,128)S(1)}, f32[32,128]{1,0:T(8,128)S(1)}, u32[]{:S(2)}, u32[]{:S(2)}) collective-permute-start(f32[32,128]{1,0:T(8,128)S(1)} %get-tuple-element.30.rows), channel_id=1, source_target_pairs={{0,2},{1,3},{2,0},{3,1},{4,6},{5,7},{6,4},{7,5},{8,10},{9,11},{10,... | collective-permute-start | bytes 49160 | tf_op jit(solution)/shard_map/ppermute | solution.py:25
  18.0 3.2 %collective-permute-done.6.far_rows = f32[32,128]{1,0:T(8,128)S(1)} collective-permute-done((f32[32,128]{1,0:T(8,128)S(1)}, f32[32,128]{1,0:T(8,128)S(1)}, u32[]{:S(2)}, u32[]{:S(2)}) %collective-permute-start.6) | collective-permute-done | bytes 16416 | tf_op jit(solution)/shard_map/ppermute | solution.py:25
  21.2 0.0 collective-permute-done.5.second
  21.2 0.0 collective-permute-done.4.first
  21.2 0.9 %shard_map.33 = (f32[2,32,512]{2,1,0:T(8,128)S(1)}, f32[2,32,128]{2,1,0:T(8,128)S(1)}, f32[2,4,32,128]{3,2,1,0:T(8,128)S(1)}, f32[1,240,128]{2,1,0:T(8,128)S(1)}) custom-call(s32[3]{0:T(128)S(1)} %copy-done.1, f32[2,32,256]{2,1,0:T(8,128)S(1)} %get-tuple-element.32.packed, f32[2,32,256]{2,1,0:T(8,128)S(1)} %collective-permute-done.4.first, ...), custom_call_target="tpu_custom_call" | custom-call | tf_op jit(solution)/shard_map/pallas_call | solution.py:516
  22.1 1.6 %collective-permute-start.7 = (f32[240,128]{1,0:T(8,128)S(1)}, f32[240,128]{1,0:T(8,128)S(1)}, u32[]{:S(2)}, u32[]{:S(2)}) collective-permute-start(f32[240,128]{1,0:T(8,128)S(1)} %bitcast.4), channel_id=1, source_target_pairs={{0,4},{4,0},{1,5},{5,1},{2,6},{6,2},{3,7},{7,3},{8,12},{12,8},{9,1... | collective-permute-start | bytes 368648 | tf_op jit(solution)/shard_map/ppermute | solution.py:25
  23.7 5.5 %shard_map.34 = (f32[2,52,48,128]{3,2,1,0:T(8,128)S(1)}, f32[3,52,48,128]{3,2,1,0:T(8,128)S(1)}, f32[3,52,48,128]{3,2,1,0:T(8,128)S(1)}, f32[3,48,32,128]{3,2,1,0:T(8,128)}) custom-call(s32[3]{0:T(128)S(1)} %copy-done.1, f32[2,48,32,128]{3,2,1,0:T(8,128)S(1)} %copy-done, f32[2,32,128]{2,1,0:T(8,128)S(1)} %get-tuple-element.38.flat, ...), custom_call_target="tpu_custom_call" | custom-call | tf_op jit(solution)/shard_map/pallas_call | solution.py:516
  29.2 0.0 collective-permute-done.7.first.second
  29.2 4.6 %shard_map.35 = (f32[2,52,48,128]{3,2,1,0:T(8,128)S(1)}, f32[3,52,48,128]{3,2,1,0:T(8,128)S(1)}, f32[3,52,48,128]{3,2,1,0:T(8,128)S(1)}, f32[3,48,32,128]{3,2,1,0:T(8,128)}) custom-call(s32[3]{0:T(128)S(1)} %copy-done.1, f32[2,32,512]{2,1,0:T(8,128)S(1)} %get-tuple-element.36.strips, ...), custom_call_target="tpu_custom_call", output_to_operand_aliasing={{0}: (4, {}), {1}: (5, {}), {2}: (6, {}), {3}: (7, {})} | custom-call | tf_op jit(solution)/shard_map/pallas_call | solution.py:516
Async XLA Ops:
  0.7 1.3 %copy-start.2 = (f32[32,128]{1,0:T(8,128)S(1)}, f32[32,128]{1,0:T(8,128)}, u32[]{:S(2)}) copy-start(f32[32,128]{1,0:T(8,128)} %mag.1) | copy-start | bytes 49156
  0.7 3.0 %copy-start = (f32[2,48,32,128]{3,2,1,0:T(8,128)S(1)}, f32[2,48,32,128]{3,2,1,0:T(8,128)}, u32[]{:S(2)}) copy-start(f32[2,48,32,128]{3,2,1,0:T(8,128)} %side.3) | copy-start | bytes 4718596
  2.0 0.7 %copy-start.1 = (s32[3]{0:T(128)S(1)}, s32[3]{0:T(128)}, u32[]{:S(2)}) copy-start(s32[3]{0:T(128)} %shard_map.28._.place) | copy-start | bytes 40
  4.3 10.7 %collective-permute-start = (f32[2,2,32,128]{3,2,1,0:T(8,128)S(1)}, f32[2,2,32,128]{3,2,1,0:T(8,128)S(1)}, u32[]{:S(2)}, u32[]{:S(2)}) collective-permute-start(f32[2,2,32,128]{3,2,1,0:T(8,128)S(1)} %get-tuple-element.26), channel_id=1, source_target_pairs={{0,8},{8,0},{16,24},{24,16},{1,9},{9,1},{17,25},{25,17},{2,10},{10... | collective-permute-start | bytes 196616 | tf_op jit(solution)/shard_map/ppermute | solution.py:25
  7.4 7.6 %collective-permute-start.1 = (f32[2,2,32,128]{3,2,1,0:T(8,128)S(1)}, f32[2,2,32,128]{3,2,1,0:T(8,128)S(1)}, u32[]{:S(2)}, u32[]{:S(2)}) collective-permute-start(f32[2,2,32,128]{3,2,1,0:T(8,128)S(1)} %get-tuple-element.27), channel_id=1, source_target_pairs={{0,24},{8,16},{16,8},{24,0},{1,25},{9,17},{17,9},{25,1},{2,26},{10... | collective-permute-start | bytes 196616 | tf_op jit(solution)/shard_map/ppermute | solution.py:25
  9.9 5.2 %collective-permute-start.3 = (f32[2,32,128]{2,1,0:T(8,128)S(1)}, f32[2,32,128]{2,1,0:T(8,128)S(1)}, u32[]{:S(2)}, u32[]{:S(2)}) collective-permute-start(f32[2,32,128]{2,1,0:T(8,128)S(1)} %get-tuple-element.28.total), channel_id=1, source_target_pairs={{0,16},{8,24},{16,0},{24,8},{1,17},{9,25},{17,1},{25,9},{2,18},{10... | collective-permute-start | bytes 98312 | tf_op jit(solution)/shard_map/ppermute | solution.py:25
  10.0 3.6 %collective-permute-start.2 = (f32[8,128]{1,0:T(8,128)S(1)}, f32[8,128]{1,0:T(8,128)S(1)}, u32[]{:S(2)}, u32[]{:S(2)}) collective-permute-start(f32[8,128]{1,0:T(8,128)S(1)} %get-tuple-element.29), channel_id=1, source_target_pairs={{0,4},{4,0},{1,5},{5,1},{2,6},{6,2},{3,7},{7,3},{8,12},{12,8},{9,1... | collective-permute-start | bytes 12296 | tf_op jit(solution)/shard_map/ppermute | solution.py:25
  15.7 5.4 %collective-permute-start.5 = (f32[2,32,256]{2,1,0:T(8,128)S(1)}, f32[2,32,256]{2,1,0:T(8,128)S(1)}, u32[]{:S(2)}, u32[]{:S(2)}) collective-permute-start(f32[2,32,256]{2,1,0:T(8,128)S(1)} %get-tuple-element.32.packed), channel_id=1, source_target_pairs={{0,3},{1,2},{2,1},{3,0},{4,7},{5,6},{6,5},{7,4},{8,11},{9,10},{10,... | collective-permute-start | bytes 196616 | tf_op jit(solution)/shard_map/ppermute | solution.py:25
  15.9 5.3 %collective-permute-start.4 = (f32[2,32,256]{2,1,0:T(8,128)S(1)}, f32[2,32,256]{2,1,0:T(8,128)S(1)}, u32[]{:S(2)}, u32[]{:S(2)}) collective-permute-start(f32[2,32,256]{2,1,0:T(8,128)S(1)} %get-tuple-element.32.packed), channel_id=1, source_target_pairs={{0,1},{1,0},{2,3},{3,2},{4,5},{5,4},{6,7},{7,6},{8,9},{9,8},{10,11... | collective-permute-start | bytes 196616 | tf_op jit(solution)/shard_map/ppermute | solution.py:25
  17.4 3.7 %collective-permute-start.6 = (f32[32,128]{1,0:T(8,128)S(1)}, f32[32,128]{1,0:T(8,128)S(1)}, u32[]{:S(2)}, u32[]{:S(2)}) collective-permute-start(f32[32,128]{1,0:T(8,128)S(1)} %get-tuple-element.30.rows), channel_id=1, source_target_pairs={{0,2},{1,3},{2,0},{3,1},{4,6},{5,7},{6,4},{7,5},{8,10},{9,11},{10,... | collective-permute-start | bytes 49160 | tf_op jit(solution)/shard_map/ppermute | solution.py:25
  22.1 7.1 %collective-permute-start.7 = (f32[240,128]{1,0:T(8,128)S(1)}, f32[240,128]{1,0:T(8,128)S(1)}, u32[]{:S(2)}, u32[]{:S(2)}) collective-permute-start(f32[240,128]{1,0:T(8,128)S(1)} %bitcast.4), channel_id=1, source_target_pairs={{0,4},{4,0},{1,5},{5,1},{2,6},{6,2},{3,7},{7,3},{8,12},{12,8},{9,1... | collective-permute-start | bytes 368648 | tf_op jit(solution)/shard_map/ppermute | solution.py:25

commit v6 on v5

--- a/solution.py
+++ b/solution.py
@@ -13,6 +13,7 @@
 LANES = 128
 PAD = 8
 GROUP = LANES // 4
+AXES = ("gz", "gy", "gx")
 LONG = pl.CostEstimate(flops=10**10, bytes_accessed=10**5, transcendentals=0)
 
 
@@ -64,12 +65,15 @@
     return parts[0]
 
 
-def place_kernel(place, place_out):
-    for k in range(place.shape[0]):
-        place_out[k] = place[k]
-
-
-def plane_kernel(_, mag, rows_out, columns_out):
+def place():
+    return [lax.axis_index(axis) for axis in AXES]
+
+
+def token_kernel(out):
+    out[...] = jnp.zeros_like(out)
+
+
+def plane_kernel(mag, rows_out, columns_out):
     rows = columns = mag[...]
     lane, row = lane_index(rows.shape), row_index(rows.shape)
     step = 1
@@ -84,10 +88,11 @@
     columns_out[...] = columns
 
 
-def totals_kernel(place, side, columns, first_out, second_out, total_out, last_out):
+def totals_kernel(side, columns, first_out, second_out, total_out, last_out):
     depth = side.shape[1]
-    odd = place[0] % 2 == 1
-    upward = odd | (place[0] == 0)
+    z, _, _ = place()
+    odd = z % 2 == 1
+    upward = odd | (z == 0)
     for c in range(2):
         low0 = side[c, 0]
         low1 = low0 + side[c, 1]
@@ -120,10 +125,10 @@
 
 
 def z_kernel(
-    count, depth, far, place, first, second, total, columns, column_carry, rows, packed, *rest
+    count, depth, far, first, second, total, columns, column_carry, rows, packed, *rest
 ):
     others, (x_out, ext_out, flat_out) = rest[:far], rest[far:]
-    z, y = place[0], place[1]
+    z, y, _ = place()
     odd = z % 2 == 1
     for c in range(2):
         near_a, near_b = (first[c, 0], first[c, 1]), (second[c, 0], second[c, 1])
@@ -154,12 +159,12 @@
 
 
 def x_kernel(
-    counts, depth, place, packed, first, second, far_rows, rows, shared, beside, edges,
+    counts, depth, packed, first, second, far_rows, rows, shared, beside, edges,
     strips_out, flat_out, ext_out, y_out,
 ):
     count_z, count_y, count_x = counts
     height = packed.shape[1]
-    z, y, x = place[0], place[1], place[2]
+    z, y, x = place()
     odd = x % 2 == 1
     base_tile, base_lane = (depth + 4) // GROUP, 4 * ((depth + 4) % GROUP)
     rows_tile, rows_lane = (depth + 5) // GROUP, 4 * ((depth + 5) % GROUP)
@@ -283,9 +288,9 @@
 
 
 class Stepper:
-    def __init__(self, counts, place, state, field, later, halo, depth, height):
+    def __init__(self, counts, state, field, later, halo, depth, height):
         self.counts = counts
-        self.z, self.y, self.x = place[0], place[1], place[2]
+        self.z, self.y, self.x = place()
         self.state, self.field, self.later, self.halo = state, field, later, halo
         self.depth, self.height = depth, height
         self.padded = state.shape[2]
@@ -453,7 +458,7 @@
 
 
 def inner_kernel(
-    counts, place, side, flat, ext, strips, state, field, later, out, halo, wide, block, sems
+    counts, side, flat, ext, strips, state, field, later, out, halo, wide, block, sems
 ):
     depth, height = side.shape[1], side.shape[2]
     rows = pl.ds(PAD, height)
@@ -469,18 +474,18 @@
         wide[c, rows, :] = strips[c]
         wide[c, pl.ds(0, PAD), :] = jnp.zeros((PAD, wide.shape[2]), jnp.float32)
         wide[c, pl.ds(PAD + height, PAD), :] = jnp.zeros((PAD, wide.shape[2]), jnp.float32)
-    stepper = Stepper(counts, place, state, field, later, halo, depth, height)
+    stepper = Stepper(counts, state, field, later, halo, depth, height)
     stepper.strips(wide)
     stepper.run(inner_tiles(height), False, out, block, sems)
 
 
 def outer_kernel(
-    counts, depth, place, strips, first, second, _s, _f, _l, _o,
+    counts, depth, strips, first, second, _s, _f, _l, _o,
     state, field, later, out, halo, wide, block, sems,
 ):
     _, count_y, _ = counts
     height, padded = strips.shape[1], state.shape[2]
-    y = place[1]
+    _, y, _ = place()
     slots = slot_rows(depth)
     layers = depth + 4
     odd = y % 2 == 1
@@ -505,18 +510,18 @@
                 )
     for c in range(2):
         wide[c, pl.ds(PAD, height), :] = strips[c]
-    stepper = Stepper(counts, place, state, field, later, halo, depth, height)
+    stepper = Stepper(counts, state, field, later, halo, depth, height)
     stepper.strips(wide)
     stepper.run(outer_tiles(height), True, out, block, sems)
 
 
 def call(kernel, shapes, args, scratch=(), limit=16, far_out=0, far_in=(), aliases={}, cost=None):
     vmem, far = pl.BlockSpec(memory_space=pltpu.VMEM), pl.BlockSpec(memory_space=pltpu.HBM)
-    specs = [far if k in far_in else vmem for k in range(1, len(args))]
+    specs = [far if k in far_in else vmem for k in range(len(args))]
     return pl.pallas_call(
         kernel,
         out_shape=[jax.ShapeDtypeStruct(shape, jnp.float32) for shape in shapes],
-        in_specs=[pl.BlockSpec(memory_space=pltpu.SMEM)] + specs,
+        in_specs=specs,
         out_specs=[vmem] * (len(shapes) - far_out) + [far] * far_out,
         scratch_shapes=[
             pltpu.VMEM(shape, jnp.float32) if isinstance(shape, tuple) else shape
@@ -547,22 +552,15 @@
     counts = tuple(lax.axis_size(axis) for axis in ("gz", "gy", "gx"))
     count_z, count_y, count_x = counts
     _, depth, height, width = side.shape
-    place = jnp.stack([lax.axis_index(axis) for axis in ("gz", "gy", "gx")]).astype(jnp.int32)
     plane, block = (height, width), (2, height, width)
-    smem = pl.BlockSpec(memory_space=pltpu.SMEM)
-    place = pl.pallas_call(
-        place_kernel,
-        out_shape=jax.ShapeDtypeStruct(place.shape, jnp.int32),
-        in_specs=[smem],
-        out_specs=smem,
-        cost_estimate=LONG,
-    )(place)
-
-    rows, columns = call(plane_kernel, [plane, plane], [place, mag])
+    (token,) = call(token_kernel, [(8, LANES)], [], cost=LONG)
+    rows, columns = call(
+        lambda _, *refs: plane_kernel(*refs), [plane, plane], [token, mag]
+    )
     first, second, total, last = call(
         totals_kernel,
         [(2, 2) + plane, (2, 2) + plane, block, (8, width)],
-        [place, side, columns],
+        [side, columns],
     )
     first = swap_first(first, "gz")
     second = swap_second(second, "gz") if count_z > 2 else first
@@ -576,16 +574,16 @@
     else:
         row_carry, column_carry = gathered_carries(rows, columns)
     packed, edges = call(
-        lambda _, *refs: pack_kernel(*refs),
+        pack_kernel,
         [(2, height, 2 * LANES), (2, 4, depth, width)],
-        [place, side],
+        [side],
         [(2, depth * height, width)],
     )
     far = len(others)
     packed, beside, shared = call(
         functools.partial(z_kernel, count_z, depth, far),
         [(2, height, 2 * LANES), (2, 4) + plane, block],
-        [place, first, second, total, columns, column_carry, rows, packed, *others],
+        [first, second, total, columns, column_carry, rows, packed, *others],
     )
     first = swap_first(packed, "gx")
     second = swap_second(packed, "gx") if count_x > 2 else first
@@ -600,21 +598,21 @@
     strips, flat, ext, edge_rows = call(
         functools.partial(x_kernel, counts, depth),
         [(2, height, 4 * LANES), block, (2, 4) + plane, (messages, message_rows, width)],
-        [place, packed, first, second, far_rows, rows, shared, beside, edges],
+        [packed, first, second, far_rows, rows, shared, beside, edges],
     )
     first = swap_first(edge_rows[0], "gy")
     second = swap_second(edge_rows[1], "gy") if count_y > 2 else first
-    grids = inner_steps(counts, place, side, flat, ext, strips)
-    return outer_steps(counts, depth, place, strips, first, second, grids)
-
-
-def inner_steps(counts, place, side, flat, ext, strips):
+    grids = inner_steps(counts, side, flat, ext, strips)
+    return outer_steps(counts, depth, strips, first, second, grids)
+
+
+def inner_steps(counts, side, flat, ext, strips):
     _, depth, height, width = side.shape
     grid = (depth + 4, height + 2 * PAD, width)
     return call(
         functools.partial(inner_kernel, counts),
         [(2,) + grid, (3,) + grid, (3,) + grid, (3, depth, height, width)],
-        [place, side, flat, ext, strips],
+        [side, flat, ext, strips],
         [
             (4, 2, height + 2 * PAD, LANES),
             (2, height + 2 * PAD, 4 * LANES),
@@ -625,12 +623,12 @@
     )
 
 
-def outer_steps(counts, depth, place, strips, first, second, grids):
+def outer_steps(counts, depth, strips, first, second, grids):
     height, width = strips.shape[1], first.shape[1]
     result = call(
         functools.partial(outer_kernel, counts, depth),
         [grid.shape for grid in grids],
-        [place, strips, first, second, *grids],
+        [strips, first, second, *grids],
         [
             (4, 2, height + 2 * PAD, LANES),
             (2, height + 2 * PAD, 4 * LANES),
@@ -638,8 +636,8 @@
             pltpu.SemaphoreType.DMA((6, 4)),
         ],
         far_out=1,
-        far_in=(7,),
-        aliases={4 + k: k for k in range(4)},
+        far_in=(6,),
+        aliases={3 + k: k for k in range(4)},
     )
     return result[3]
 

time: 34 us -> 28.7 us (0.84)
  Pallas kernels: 15.8 us -> 10.3 us
  other arithmetic: 0.66 us -> 0 us
  waiting for transfers between devices: 5.66 us -> 6.2 us
    pallas_call x7 -> x8, Pallas kernels: 14.5 us -> 10.3 us  [call(): pl.pallas_call(kernel, out_shape=[jax.ShapeDtypeStruct(shape, jnp.float32...]
    pallas_call x1 -> x0, Pallas kernels: 1.31 us -> none  [local(): pl.pallas_call(place_kernel, out_shape=jax.ShapeDtypeStruct(place.shape,...]
    another operation x1 -> x0, other arithmetic: 0.66 us -> none  [local(): jnp.stack([lax.axis_index(axis) for axis in ('gz', 'gy', 'gx')])]
    ppermute x8, waiting for transfers between devices: 5.66 us -> 6.2 us  [swap(): return lax.ppermute(part, axis, [(i, partner(i)) for i in range(count)])]
    unnamed x6 -> x4, local copies, waits for them, and re-layouts: 0.66 us -> 0.93 us
  transfers between devices with their start and end apart: 8 -> 8, of which waited for: 3 -> 3; matrix products, arithmetic and copies ran while one was open for 0% -> 0% of each run, Pallas kernels for 20% -> 19%
where the time goes in v6:
time: 28.7 us; the launch traced here: 28.4 us
  starting transfers between devices  11 us (38%)
  Pallas kernels  10.3 us (36%)
  waiting for transfers between devices  6.2 us (22%)
  local copies, waits for them, and re-layouts  0.93 us (3%)
    ppermute x8, starting transfers between devices, swap(): return lax.ppermute(part, axis, [(i, partner(i)) for i in range(count)])  11 us
    pallas_call x8, Pallas kernels, call(): pl.pallas_call(kernel, out_shape=[jax.ShapeDtypeStruct(shape, jnp.float32...  10.3 us
    ppermute x8, waiting for transfers between devices, swap(): return lax.ppermute(part, axis, [(i, partner(i)) for i in range(count)])  6.2 us
    unnamed x4, local copies, waits for them, and re-layouts  0.93 us
  transfers between devices with their start and end apart: 8, of which 3 were waited for; matrix products, arithmetic and copies ran while one was open for 0% of the time, Pallas kernels for 19%

profile of v6, /device:TPU:0, one launch (start us, length us, event | category | flops | bytes accessed | tf_op | source)
XLA Modules:
  0.0 28.4 jit_solution(10247210472044591144)
XLA Ops:
  0.0 0.0 copy-start.1
  0.0 0.0 copy-start
  0.0 0.7 %copy-done.1 = f32[32,128]{1,0:T(8,128)S(1)} copy-done((f32[32,128]{1,0:T(8,128)S(1)}, f32[32,128]{1,0:T(8,128)}, u32[]{:S(2)}) %copy-start.1) | copy-done | bytes 16408
  0.7 0.5 %shard_map.29 = (f32[32,128]{1,0:T(8,128)S(1)}, f32[32,128]{1,0:T(8,128)S(1)}) custom-call(f32[8,128]{1,0:T(8,128)S(1)} %shard_map.28._, f32[32,128]{1,0:T(8,128)S(1)} %copy-done.1), custom_call_target="tpu_custom_call" | custom-call | tf_op jit(solution)/shard_map/pallas_call | solution.py:521
  1.2 0.2 copy-done
  1.4 0.1 shard_map.30
  1.5 3.1 %collective-permute-start = (f32[2,2,32,128]{3,2,1,0:T(8,128)S(1)}, f32[2,2,32,128]{3,2,1,0:T(8,128)S(1)}, u32[]{:S(2)}, u32[]{:S(2)}) collective-permute-start(f32[2,2,32,128]{3,2,1,0:T(8,128)S(1)} %get-tuple-element.26), channel_id=1, source_target_pairs={{0,8},{8,0},{16,24},{24,16},{1,9},{9,1},{17,25},{25,17},{2,10},{10... | collective-permute-start | bytes 196616 | tf_op jit(solution)/shard_map/ppermute | solution.py:26
  4.6 2.5 %collective-permute-start.1 = (f32[2,2,32,128]{3,2,1,0:T(8,128)S(1)}, f32[2,2,32,128]{3,2,1,0:T(8,128)S(1)}, u32[]{:S(2)}, u32[]{:S(2)}) collective-permute-start(f32[2,2,32,128]{3,2,1,0:T(8,128)S(1)} %get-tuple-element.27), channel_id=1, source_target_pairs={{0,24},{8,16},{16,8},{24,0},{1,25},{9,17},{17,9},{25,1},{2,26},{10... | collective-permute-start | bytes 196616 | tf_op jit(solution)/shard_map/ppermute | solution.py:26
  7.1 0.1 collective-permute-start.3
  7.2 1.5 %collective-permute-start.2 = (f32[8,128]{1,0:T(8,128)S(1)}, f32[8,128]{1,0:T(8,128)S(1)}, u32[]{:S(2)}, u32[]{:S(2)}) collective-permute-start(f32[8,128]{1,0:T(8,128)S(1)} %get-tuple-element.29), channel_id=1, source_target_pairs={{0,4},{4,0},{1,5},{5,1},{2,6},{6,2},{3,7},{7,3},{8,12},{12,8},{9,1... | collective-permute-start | bytes 12296 | tf_op jit(solution)/shard_map/ppermute | solution.py:26
  8.7 0.5 %shard_map.31 = (f32[2,32,256]{2,1,0:T(8,128)S(1)}, f32[2,4,48,128]{3,2,1,0:T(8,128)S(1)}) custom-call(f32[2,48,32,128]{3,2,1,0:T(8,128)S(1)} %copy-done), custom_call_target="tpu_custom_call" | custom-call | tf_op jit(solution)/shard_map/pallas_call | solution.py:521
  9.3 1.5 %collective-permute-done.2.column_carry = f32[8,128]{1,0:T(8,128)S(1)} collective-permute-done((f32[8,128]{1,0:T(8,128)S(1)}, f32[8,128]{1,0:T(8,128)S(1)}, u32[]{:S(2)}, u32[]{:S(2)}) %collective-permute-start.2) | collective-permute-done | bytes 4128 | tf_op jit(solution)/shard_map/ppermute | solution.py:26
  10.8 1.4 %collective-permute-done.3.rest_0_ = f32[2,32,128]{2,1,0:T(8,128)S(1)} collective-permute-done((f32[2,32,128]{2,1,0:T(8,128)S(1)}, f32[2,32,128]{2,1,0:T(8,128)S(1)}, u32[]{:S(2)}, u32[]{:S(2)}) %collective-permute-start.3) | collective-permute-done | bytes 32800 | tf_op jit(solution)/shard_map/ppermute | solution.py:26
  12.3 0.0 collective-permute-done.first
  12.3 0.0 collective-permute-done.1.second
  12.3 0.1 shard_map.32
  12.4 0.2 collective-permute-start.5
  12.6 1.5 %collective-permute-start.4 = (f32[2,32,256]{2,1,0:T(8,128)S(1)}, f32[2,32,256]{2,1,0:T(8,128)S(1)}, u32[]{:S(2)}, u32[]{:S(2)}) collective-permute-start(f32[2,32,256]{2,1,0:T(8,128)S(1)} %get-tuple-element.32.packed), channel_id=1, source_target_pairs={{0,1},{1,0},{2,3},{3,2},{4,5},{5,4},{6,7},{7,6},{8,9},{9,8},{10,11... | collective-permute-start | bytes 196616 | tf_op jit(solution)/shard_map/ppermute | solution.py:26
  14.1 0.5 %collective-permute-start.6 = (f32[32,128]{1,0:T(8,128)S(1)}, f32[32,128]{1,0:T(8,128)S(1)}, u32[]{:S(2)}, u32[]{:S(2)}) collective-permute-start(f32[32,128]{1,0:T(8,128)S(1)} %get-tuple-element.30.rows), channel_id=1, source_target_pairs={{0,2},{1,3},{2,0},{3,1},{4,6},{5,7},{6,4},{7,5},{8,10},{9,11},{10,... | collective-permute-start | bytes 49160 | tf_op jit(solution)/shard_map/ppermute | solution.py:26
  14.6 3.2 %collective-permute-done.6.far_rows = f32[32,128]{1,0:T(8,128)S(1)} collective-permute-done((f32[32,128]{1,0:T(8,128)S(1)}, f32[32,128]{1,0:T(8,128)S(1)}, u32[]{:S(2)}, u32[]{:S(2)}) %collective-permute-start.6) | collective-permute-done | bytes 16416 | tf_op jit(solution)/shard_map/ppermute | solution.py:26
  17.8 0.0 collective-permute-done.5.second
  17.8 0.0 collective-permute-done.4.first
  17.8 0.4 %shard_map.33 = (f32[2,32,512]{2,1,0:T(8,128)S(1)}, f32[2,32,128]{2,1,0:T(8,128)S(1)}, f32[2,4,32,128]{3,2,1,0:T(8,128)S(1)}, f32[1,240,128]{2,1,0:T(8,128)S(1)}) custom-call(f32[2,32,256]{2,1,0:T(8,128)S(1)} %get-tuple-element.32.packed, f32[2,32,256]{2,1,0:T(8,128)S(1)} %collective-permute-done.4.first, f32[2,32,256]{2,1,0:T(8,128)S(1)} %collective-permute-done.5.second, ...), custom_call_target="tpu_custom_call" | custom-call | tf_op jit(solution)/shard_map/pallas_call | solution.py:521
  18.2 1.6 %collective-permute-start.7 = (f32[240,128]{1,0:T(8,128)S(1)}, f32[240,128]{1,0:T(8,128)S(1)}, u32[]{:S(2)}, u32[]{:S(2)}) collective-permute-start(f32[240,128]{1,0:T(8,128)S(1)} %bitcast.1), channel_id=1, source_target_pairs={{0,4},{4,0},{1,5},{5,1},{2,6},{6,2},{3,7},{7,3},{8,12},{12,8},{9,1... | collective-permute-start | bytes 368648 | tf_op jit(solution)/shard_map/ppermute | solution.py:26
  19.8 4.7 %shard_map.34 = (f32[2,52,48,128]{3,2,1,0:T(8,128)S(1)}, f32[3,52,48,128]{3,2,1,0:T(8,128)S(1)}, f32[3,52,48,128]{3,2,1,0:T(8,128)S(1)}, f32[3,48,32,128]{3,2,1,0:T(8,128)}) custom-call(f32[2,48,32,128]{3,2,1,0:T(8,128)S(1)} %copy-done, f32[2,32,128]{2,1,0:T(8,128)S(1)} %get-tuple-element.38.flat, f32[2,4,32,128]{3,2,1,0:T(8,128)S(1)} %get-tuple-element.39.ext, ...), custom_call_target="tpu_custom_call" | custom-call | tf_op jit(solution)/shard_map/pallas_call | solution.py:521
  24.5 0.0 collective-permute-done.7.first.second
  24.5 3.9 %shard_map.35 = (f32[2,52,48,128]{3,2,1,0:T(8,128)S(1)}, f32[3,52,48,128]{3,2,1,0:T(8,128)S(1)}, f32[3,52,48,128]{3,2,1,0:T(8,128)S(1)}, f32[3,48,32,128]{3,2,1,0:T(8,128)}) custom-call(f32[2,32,512]{2,1,0:T(8,128)S(1)} %get-tuple-element.36.strips, ...), custom_call_target="tpu_custom_call", output_to_operand_aliasing={{0}: (3, {}), {1}: (4, {}), {2}: (5, {}), {3}: (6, {})} | custom-call | tf_op jit(solution)/shard_map/pallas_call | solution.py:521
  (1 shorter events, 0.0 us)
Async XLA Ops:
  0.0 0.7 %copy-start.1 = (f32[32,128]{1,0:T(8,128)S(1)}, f32[32,128]{1,0:T(8,128)}, u32[]{:S(2)}) copy-start(f32[32,128]{1,0:T(8,128)} %refs_0_.1) | copy-start | bytes 49156
  0.0 1.4 %copy-start = (f32[2,48,32,128]{3,2,1,0:T(8,128)S(1)}, f32[2,48,32,128]{3,2,1,0:T(8,128)}, u32[]{:S(2)}) copy-start(f32[2,48,32,128]{3,2,1,0:T(8,128)} %side.5) | copy-start | bytes 4718596
  1.5 10.7 %collective-permute-start = (f32[2,2,32,128]{3,2,1,0:T(8,128)S(1)}, f32[2,2,32,128]{3,2,1,0:T(8,128)S(1)}, u32[]{:S(2)}, u32[]{:S(2)}) collective-permute-start(f32[2,2,32,128]{3,2,1,0:T(8,128)S(1)} %get-tuple-element.26), channel_id=1, source_target_pairs={{0,8},{8,0},{16,24},{24,16},{1,9},{9,1},{17,25},{25,17},{2,10},{10... | collective-permute-start | bytes 196616 | tf_op jit(solution)/shard_map/ppermute | solution.py:26
  4.6 7.6 %collective-permute-start.1 = (f32[2,2,32,128]{3,2,1,0:T(8,128)S(1)}, f32[2,2,32,128]{3,2,1,0:T(8,128)S(1)}, u32[]{:S(2)}, u32[]{:S(2)}) collective-permute-start(f32[2,2,32,128]{3,2,1,0:T(8,128)S(1)} %get-tuple-element.27), channel_id=1, source_target_pairs={{0,24},{8,16},{16,8},{24,0},{1,25},{9,17},{17,9},{25,1},{2,26},{10... | collective-permute-start | bytes 196616 | tf_op jit(solution)/shard_map/ppermute | solution.py:26
  7.1 5.2 %collective-permute-start.3 = (f32[2,32,128]{2,1,0:T(8,128)S(1)}, f32[2,32,128]{2,1,0:T(8,128)S(1)}, u32[]{:S(2)}, u32[]{:S(2)}) collective-permute-start(f32[2,32,128]{2,1,0:T(8,128)S(1)} %get-tuple-element.28.total), channel_id=1, source_target_pairs={{0,16},{8,24},{16,0},{24,8},{1,17},{9,25},{17,1},{25,9},{2,18},{10... | collective-permute-start | bytes 98312 | tf_op jit(solution)/shard_map/ppermute | solution.py:26
  7.2 3.6 %collective-permute-start.2 = (f32[8,128]{1,0:T(8,128)S(1)}, f32[8,128]{1,0:T(8,128)S(1)}, u32[]{:S(2)}, u32[]{:S(2)}) collective-permute-start(f32[8,128]{1,0:T(8,128)S(1)} %get-tuple-element.29), channel_id=1, source_target_pairs={{0,4},{4,0},{1,5},{5,1},{2,6},{6,2},{3,7},{7,3},{8,12},{12,8},{9,1... | collective-permute-start | bytes 12296 | tf_op jit(solution)/shard_map/ppermute | solution.py:26
  12.4 5.4 %collective-permute-start.5 = (f32[2,32,256]{2,1,0:T(8,128)S(1)}, f32[2,32,256]{2,1,0:T(8,128)S(1)}, u32[]{:S(2)}, u32[]{:S(2)}) collective-permute-start(f32[2,32,256]{2,1,0:T(8,128)S(1)} %get-tuple-element.32.packed), channel_id=1, source_target_pairs={{0,3},{1,2},{2,1},{3,0},{4,7},{5,6},{6,5},{7,4},{8,11},{9,10},{10,... | collective-permute-start | bytes 196616 | tf_op jit(solution)/shard_map/ppermute | solution.py:26
  12.6 5.3 %collective-permute-start.4 = (f32[2,32,256]{2,1,0:T(8,128)S(1)}, f32[2,32,256]{2,1,0:T(8,128)S(1)}, u32[]{:S(2)}, u32[]{:S(2)}) collective-permute-start(f32[2,32,256]{2,1,0:T(8,128)S(1)} %get-tuple-element.32.packed), channel_id=1, source_target_pairs={{0,1},{1,0},{2,3},{3,2},{4,5},{5,4},{6,7},{7,6},{8,9},{9,8},{10,11... | collective-permute-start | bytes 196616 | tf_op jit(solution)/shard_map/ppermute | solution.py:26
  14.1 3.7 %collective-permute-start.6 = (f32[32,128]{1,0:T(8,128)S(1)}, f32[32,128]{1,0:T(8,128)S(1)}, u32[]{:S(2)}, u32[]{:S(2)}) collective-permute-start(f32[32,128]{1,0:T(8,128)S(1)} %get-tuple-element.30.rows), channel_id=1, source_target_pairs={{0,2},{1,3},{2,0},{3,1},{4,6},{5,7},{6,4},{7,5},{8,10},{9,11},{10,... | collective-permute-start | bytes 49160 | tf_op jit(solution)/shard_map/ppermute | solution.py:26
  18.2 6.3 %collective-permute-start.7 = (f32[240,128]{1,0:T(8,128)S(1)}, f32[240,128]{1,0:T(8,128)S(1)}, u32[]{:S(2)}, u32[]{:S(2)}) collective-permute-start(f32[240,128]{1,0:T(8,128)S(1)} %bitcast.1), channel_id=1, source_target_pairs={{0,4},{4,0},{1,5},{5,1},{2,6},{6,2},{3,7},{7,3},{8,12},{12,8},{9,1... | collective-permute-start | bytes 368648 | tf_op jit(solution)/shard_map/ppermute | solution.py:26

commit v7 on v6

--- a/solution.py
+++ b/solution.py
@@ -125,9 +125,10 @@
 
 
 def z_kernel(
-    count, depth, far, first, second, total, columns, column_carry, rows, packed, *rest
+    count, depth, far, first, second, total, columns, column_carry, far_rows, rows, packed, *rest
 ):
-    others, (x_out, ext_out, flat_out) = rest[:far], rest[far:]
+    others, (x_out, ext_out, flat_out, far_out) = rest[:far], rest[far:]
+    far_out[...] = far_rows[...]
     z, y, _ = place()
     odd = z % 2 == 1
     for c in range(2):
@@ -571,8 +572,9 @@
     direct = count_y == 2 and count_x in (2, 4)
     if direct:
         column_carry = swap_first(last, "gy")
+        far_rows = swap(rows, "gx", lambda i: i ^ 2) if count_x == 4 else rows
     else:
-        row_carry, column_carry = gathered_carries(rows, columns)
+        far_rows, column_carry = gathered_carries(rows, columns)
     packed, edges = call(
         pack_kernel,
         [(2, height, 2 * LANES), (2, 4, depth, width)],
@@ -580,19 +582,13 @@
         [(2, depth * height, width)],
     )
     far = len(others)
-    packed, beside, shared = call(
+    packed, beside, shared, far_rows = call(
         functools.partial(z_kernel, count_z, depth, far),
-        [(2, height, 2 * LANES), (2, 4) + plane, block],
-        [first, second, total, columns, column_carry, rows, packed, *others],
+        [(2, height, 2 * LANES), (2, 4) + plane, block, plane],
+        [first, second, total, columns, column_carry, far_rows, rows, packed, *others],
     )
     first = swap_first(packed, "gx")
     second = swap_second(packed, "gx") if count_x > 2 else first
-    if not direct:
-        far_rows = row_carry
-    elif count_x == 4:
-        far_rows = swap(rows, "gx", lambda i: i ^ 2)
-    else:
-        far_rows = rows
     messages = 1 if count_y == 2 else 2
     message_rows = 4 * slot_rows(depth) + 16
     strips, flat, ext, edge_rows = call(

time: 28.7 us -> 27.8 us (0.969)
  waiting for transfers between devices: 6.2 us -> 4.39 us
  starting transfers between devices: 11 us -> 11.9 us
    ppermute x8, waiting for transfers between devices: 6.2 us -> 4.39 us  [swap(): return lax.ppermute(part, axis, [(i, partner(i)) for i in range(count)])]
    ppermute x8, starting transfers between devices: 11 us -> 11.9 us  [swap(): return lax.ppermute(part, axis, [(i, partner(i)) for i in range(count)])]
  transfers between devices with their start and end apart: 8 -> 8, of which waited for: 3 -> 2; matrix products, arithmetic and copies ran while one was open for 0% -> 0% of each run, Pallas kernels for 19% -> 19%
where the time goes in v7:
time: 27.8 us; the launch traced here: 27.5 us
  starting transfers between devices  11.9 us (43%)
  Pallas kernels  10.3 us (37%)
  waiting for transfers between devices  4.39 us (16%)
  local copies, waits for them, and re-layouts  0.93 us (3%)
    ppermute x8, starting transfers between devices, swap(): return lax.ppermute(part, axis, [(i, partner(i)) for i in range(count)])  11.9 us
    pallas_call x8, Pallas kernels, call(): pl.pallas_call(kernel, out_shape=[jax.ShapeDtypeStruct(shape, jnp.float32...  10.3 us
    ppermute x8, waiting for transfers between devices, swap(): return lax.ppermute(part, axis, [(i, partner(i)) for i in range(count)])  4.39 us
    unnamed x4, local copies, waits for them, and re-layouts  0.93 us
  transfers between devices with their start and end apart: 8, of which 2 were waited for; matrix products, arithmetic and copies ran while one was open for 0% of the time, Pallas kernels for 19%

profile of v7, /device:TPU:0, one launch (start us, length us, event | category | flops | bytes accessed | tf_op | source)
XLA Modules:
  0.0 27.5 jit_solution(2067617834117255592)
XLA Ops:
  0.0 0.0 copy-start.1
  0.0 0.0 copy-start
  0.0 0.7 %copy-done.1 = f32[32,128]{1,0:T(8,128)S(1)} copy-done((f32[32,128]{1,0:T(8,128)S(1)}, f32[32,128]{1,0:T(8,128)}, u32[]{:S(2)}) %copy-start.1) | copy-done | bytes 16408
  0.7 0.5 %shard_map.29 = (f32[32,128]{1,0:T(8,128)S(1)}, f32[32,128]{1,0:T(8,128)S(1)}) custom-call(f32[8,128]{1,0:T(8,128)S(1)} %shard_map.28._, f32[32,128]{1,0:T(8,128)S(1)} %copy-done.1), custom_call_target="tpu_custom_call" | custom-call | tf_op jit(solution)/shard_map/pallas_call | solution.py:522
  1.2 0.2 copy-done
  1.4 0.1 shard_map.30
  1.5 3.1 %collective-permute-start = (f32[2,2,32,128]{3,2,1,0:T(8,128)S(1)}, f32[2,2,32,128]{3,2,1,0:T(8,128)S(1)}, u32[]{:S(2)}, u32[]{:S(2)}) collective-permute-start(f32[2,2,32,128]{3,2,1,0:T(8,128)S(1)} %get-tuple-element.27), channel_id=1, source_target_pairs={{0,8},{8,0},{16,24},{24,16},{1,9},{9,1},{17,25},{25,17},{2,10},{10... | collective-permute-start | bytes 196616 | tf_op jit(solution)/shard_map/ppermute | solution.py:26
  4.6 2.5 %collective-permute-start.1 = (f32[2,2,32,128]{3,2,1,0:T(8,128)S(1)}, f32[2,2,32,128]{3,2,1,0:T(8,128)S(1)}, u32[]{:S(2)}, u32[]{:S(2)}) collective-permute-start(f32[2,2,32,128]{3,2,1,0:T(8,128)S(1)} %get-tuple-element.28), channel_id=1, source_target_pairs={{0,24},{8,16},{16,8},{24,0},{1,25},{9,17},{17,9},{25,1},{2,26},{10... | collective-permute-start | bytes 196616 | tf_op jit(solution)/shard_map/ppermute | solution.py:26
  7.1 0.1 collective-permute-start.4
  7.2 1.5 %collective-permute-start.3 = (f32[32,128]{1,0:T(8,128)S(1)}, f32[32,128]{1,0:T(8,128)S(1)}, u32[]{:S(2)}, u32[]{:S(2)}) collective-permute-start(f32[32,128]{1,0:T(8,128)S(1)} %get-tuple-element.31.rows), channel_id=1, source_target_pairs={{0,2},{1,3},{2,0},{3,1},{4,6},{5,7},{6,4},{7,5},{8,10},{9,11},{10,... | collective-permute-start | bytes 49160 | tf_op jit(solution)/shard_map/ppermute | solution.py:26
  8.7 1.5 %collective-permute-start.2 = (f32[8,128]{1,0:T(8,128)S(1)}, f32[8,128]{1,0:T(8,128)S(1)}, u32[]{:S(2)}, u32[]{:S(2)}) collective-permute-start(f32[8,128]{1,0:T(8,128)S(1)} %get-tuple-element.30), channel_id=1, source_target_pairs={{0,4},{4,0},{1,5},{5,1},{2,6},{6,2},{3,7},{7,3},{8,12},{12,8},{9,1... | collective-permute-start | bytes 12296 | tf_op jit(solution)/shard_map/ppermute | solution.py:26
  10.2 0.5 %shard_map.31 = (f32[2,32,256]{2,1,0:T(8,128)S(1)}, f32[2,4,48,128]{3,2,1,0:T(8,128)S(1)}) custom-call(f32[2,48,32,128]{3,2,1,0:T(8,128)S(1)} %copy-done), custom_call_target="tpu_custom_call" | custom-call | tf_op jit(solution)/shard_map/pallas_call | solution.py:522
  10.8 1.5 %collective-permute-done.2.column_carry = f32[8,128]{1,0:T(8,128)S(1)} collective-permute-done((f32[8,128]{1,0:T(8,128)S(1)}, f32[8,128]{1,0:T(8,128)S(1)}, u32[]{:S(2)}, u32[]{:S(2)}) %collective-permute-start.2) | collective-permute-done | bytes 4128 | tf_op jit(solution)/shard_map/ppermute | solution.py:26
  12.3 0.0 collective-permute-done.3.far_rows
  12.3 0.0 collective-permute-done.4.rest_0_
  12.3 0.0 collective-permute-done.first
  12.3 0.0 collective-permute-done.1.second
  12.3 0.1 shard_map.32
  12.5 0.1 collective-permute-start.6
  12.6 1.5 %collective-permute-start.5 = (f32[2,32,256]{2,1,0:T(8,128)S(1)}, f32[2,32,256]{2,1,0:T(8,128)S(1)}, u32[]{:S(2)}, u32[]{:S(2)}) collective-permute-start(f32[2,32,256]{2,1,0:T(8,128)S(1)} %get-tuple-element.33.packed), channel_id=1, source_target_pairs={{0,1},{1,0},{2,3},{3,2},{4,5},{5,4},{6,7},{7,6},{8,9},{9,8},{10,11... | collective-permute-start | bytes 196616 | tf_op jit(solution)/shard_map/ppermute | solution.py:26
  14.1 2.8 %collective-permute-done.6.second = f32[2,32,256]{2,1,0:T(8,128)S(1)} collective-permute-done((f32[2,32,256]{2,1,0:T(8,128)S(1)}, f32[2,32,256]{2,1,0:T(8,128)S(1)}, u32[]{:S(2)}, u32[]{:S(2)}) %collective-permute-start.6) | collective-permute-done | bytes 65568 | tf_op jit(solution)/shard_map/ppermute | solution.py:26
  16.9 0.0 collective-permute-done.5.first
  16.9 0.4 %shard_map.33 = (f32[2,32,512]{2,1,0:T(8,128)S(1)}, f32[2,32,128]{2,1,0:T(8,128)S(1)}, f32[2,4,32,128]{3,2,1,0:T(8,128)S(1)}, f32[1,240,128]{2,1,0:T(8,128)S(1)}) custom-call(f32[2,32,256]{2,1,0:T(8,128)S(1)} %get-tuple-element.33.packed, f32[2,32,256]{2,1,0:T(8,128)S(1)} %collective-permute-done.5.first, f32[2,32,256]{2,1,0:T(8,128)S(1)} %collective-permute-done.6.second, ...), custom_call_target="tpu_custom_call" | custom-call | tf_op jit(solution)/shard_map/pallas_call | solution.py:522
  17.3 1.6 %collective-permute-start.7 = (f32[240,128]{1,0:T(8,128)S(1)}, f32[240,128]{1,0:T(8,128)S(1)}, u32[]{:S(2)}, u32[]{:S(2)}) collective-permute-start(f32[240,128]{1,0:T(8,128)S(1)} %bitcast.1), channel_id=1, source_target_pairs={{0,4},{4,0},{1,5},{5,1},{2,6},{6,2},{3,7},{7,3},{8,12},{12,8},{9,1... | collective-permute-start | bytes 368648 | tf_op jit(solution)/shard_map/ppermute | solution.py:26
  18.9 4.7 %shard_map.34 = (f32[2,52,48,128]{3,2,1,0:T(8,128)S(1)}, f32[3,52,48,128]{3,2,1,0:T(8,128)S(1)}, f32[3,52,48,128]{3,2,1,0:T(8,128)S(1)}, f32[3,48,32,128]{3,2,1,0:T(8,128)}) custom-call(f32[2,48,32,128]{3,2,1,0:T(8,128)S(1)} %copy-done, f32[2,32,128]{2,1,0:T(8,128)S(1)} %get-tuple-element.40.flat, f32[2,4,32,128]{3,2,1,0:T(8,128)S(1)} %get-tuple-element.41.ext, ...), custom_call_target="tpu_custom_call" | custom-call | tf_op jit(solution)/shard_map/pallas_call | solution.py:522
  23.6 0.0 collective-permute-done.7.first.second
  23.6 3.9 %shard_map.35 = (f32[2,52,48,128]{3,2,1,0:T(8,128)S(1)}, f32[3,52,48,128]{3,2,1,0:T(8,128)S(1)}, f32[3,52,48,128]{3,2,1,0:T(8,128)S(1)}, f32[3,48,32,128]{3,2,1,0:T(8,128)}) custom-call(f32[2,32,512]{2,1,0:T(8,128)S(1)} %get-tuple-element.38.strips, ...), custom_call_target="tpu_custom_call", output_to_operand_aliasing={{0}: (3, {}), {1}: (4, {}), {2}: (5, {}), {3}: (6, {})} | custom-call | tf_op jit(solution)/shard_map/pallas_call | solution.py:522
  (1 shorter events, 0.0 us)
Async XLA Ops:
  0.0 0.7 %copy-start.1 = (f32[32,128]{1,0:T(8,128)S(1)}, f32[32,128]{1,0:T(8,128)}, u32[]{:S(2)}) copy-start(f32[32,128]{1,0:T(8,128)} %refs_0_.1) | copy-start | bytes 49156
  0.0 1.4 %copy-start = (f32[2,48,32,128]{3,2,1,0:T(8,128)S(1)}, f32[2,48,32,128]{3,2,1,0:T(8,128)}, u32[]{:S(2)}) copy-start(f32[2,48,32,128]{3,2,1,0:T(8,128)} %side.5) | copy-start | bytes 4718596
  1.5 10.8 %collective-permute-start = (f32[2,2,32,128]{3,2,1,0:T(8,128)S(1)}, f32[2,2,32,128]{3,2,1,0:T(8,128)S(1)}, u32[]{:S(2)}, u32[]{:S(2)}) collective-permute-start(f32[2,2,32,128]{3,2,1,0:T(8,128)S(1)} %get-tuple-element.27), channel_id=1, source_target_pairs={{0,8},{8,0},{16,24},{24,16},{1,9},{9,1},{17,25},{25,17},{2,10},{10... | collective-permute-start | bytes 196616 | tf_op jit(solution)/shard_map/ppermute | solution.py:26
  4.6 7.7 %collective-permute-start.1 = (f32[2,2,32,128]{3,2,1,0:T(8,128)S(1)}, f32[2,2,32,128]{3,2,1,0:T(8,128)S(1)}, u32[]{:S(2)}, u32[]{:S(2)}) collective-permute-start(f32[2,2,32,128]{3,2,1,0:T(8,128)S(1)} %get-tuple-element.28), channel_id=1, source_target_pairs={{0,24},{8,16},{16,8},{24,0},{1,25},{9,17},{17,9},{25,1},{2,26},{10... | collective-permute-start | bytes 196616 | tf_op jit(solution)/shard_map/ppermute | solution.py:26
  7.1 5.2 %collective-permute-start.4 = (f32[2,32,128]{2,1,0:T(8,128)S(1)}, f32[2,32,128]{2,1,0:T(8,128)S(1)}, u32[]{:S(2)}, u32[]{:S(2)}) collective-permute-start(f32[2,32,128]{2,1,0:T(8,128)S(1)} %get-tuple-element.29.total), channel_id=1, source_target_pairs={{0,16},{8,24},{16,0},{24,8},{1,17},{9,25},{17,1},{25,9},{2,18},{10... | collective-permute-start | bytes 98312 | tf_op jit(solution)/shard_map/ppermute | solution.py:26
  7.2 5.1 %collective-permute-start.3 = (f32[32,128]{1,0:T(8,128)S(1)}, f32[32,128]{1,0:T(8,128)S(1)}, u32[]{:S(2)}, u32[]{:S(2)}) collective-permute-start(f32[32,128]{1,0:T(8,128)S(1)} %get-tuple-element.31.rows), channel_id=1, source_target_pairs={{0,2},{1,3},{2,0},{3,1},{4,6},{5,7},{6,4},{7,5},{8,10},{9,11},{10,... | collective-permute-start | bytes 49160 | tf_op jit(solution)/shard_map/ppermute | solution.py:26
  8.7 3.6 %collective-permute-start.2 = (f32[8,128]{1,0:T(8,128)S(1)}, f32[8,128]{1,0:T(8,128)S(1)}, u32[]{:S(2)}, u32[]{:S(2)}) collective-permute-start(f32[8,128]{1,0:T(8,128)S(1)} %get-tuple-element.30), channel_id=1, source_target_pairs={{0,4},{4,0},{1,5},{5,1},{2,6},{6,2},{3,7},{7,3},{8,12},{12,8},{9,1... | collective-permute-start | bytes 12296 | tf_op jit(solution)/shard_map/ppermute | solution.py:26
  12.5 4.4 %collective-permute-start.6 = (f32[2,32,256]{2,1,0:T(8,128)S(1)}, f32[2,32,256]{2,1,0:T(8,128)S(1)}, u32[]{:S(2)}, u32[]{:S(2)}) collective-permute-start(f32[2,32,256]{2,1,0:T(8,128)S(1)} %get-tuple-element.33.packed), channel_id=1, source_target_pairs={{0,3},{1,2},{2,1},{3,0},{4,7},{5,6},{6,5},{7,4},{8,11},{9,10},{10,... | collective-permute-start | bytes 196616 | tf_op jit(solution)/shard_map/ppermute | solution.py:26
  12.6 4.3 %collective-permute-start.5 = (f32[2,32,256]{2,1,0:T(8,128)S(1)}, f32[2,32,256]{2,1,0:T(8,128)S(1)}, u32[]{:S(2)}, u32[]{:S(2)}) collective-permute-start(f32[2,32,256]{2,1,0:T(8,128)S(1)} %get-tuple-element.33.packed), channel_id=1, source_target_pairs={{0,1},{1,0},{2,3},{3,2},{4,5},{5,4},{6,7},{7,6},{8,9},{9,8},{10,11... | collective-permute-start | bytes 196616 | tf_op jit(solution)/shard_map/ppermute | solution.py:26
  17.3 6.3 %collective-permute-start.7 = (f32[240,128]{1,0:T(8,128)S(1)}, f32[240,128]{1,0:T(8,128)S(1)}, u32[]{:S(2)}, u32[]{:S(2)}) collective-permute-start(f32[240,128]{1,0:T(8,128)S(1)} %bitcast.1), channel_id=1, source_target_pairs={{0,4},{4,0},{1,5},{5,1},{2,6},{6,2},{3,7},{7,3},{8,12},{12,8},{9,1... | collective-permute-start | bytes 368648 | tf_op jit(solution)/shard_map/ppermute | solution.py:26

commit v8 on v7

--- a/solution.py
+++ b/solution.py
@@ -409,7 +409,7 @@
                     flat_later = self.later.at[c].reshape((depth + 4) * self.padded, LANES)
                     flat_later[pl.ds(row, depth + 4, stride=self.padded), :] = line
 
-    def run(self, tiles, rows, out, block, sems, pieces=6):
+    def run(self, tiles, rows, out, block, sems):
         depth = self.depth
         for layer in range(depth + 3):
             for r in tiles[0]:
@@ -421,28 +421,25 @@
         for layer in range(1, depth + 2):
             for r in tiles[2]:
                 self.second_field(layer, r)
+        for layer in range(depth):
+            for k, r in enumerate(tiles[3]):
+                for c, value in enumerate(self.second_push(layer + 2, r)):
+                    block[c, layer, pl.ds(8 * k, 8), :] = value
         copies = []
-        size = depth // pieces
-        for piece in range(pieces):
-            layers = pl.ds(piece * size, size)
-            for layer in range(piece * size, (piece + 1) * size):
-                for k, r in enumerate(tiles[3]):
-                    for c, value in enumerate(self.second_push(layer + 2, r)):
-                        block[c, layer, pl.ds(8 * k, 8), :] = value
-            k = 0
-            while k < len(tiles[3]):
-                run = 1
-                while k + run < len(tiles[3]) and tiles[3][k + run] == tiles[3][k] + 8 * run:
-                    run += 1
-                copies.append(
-                    pltpu.make_async_copy(
-                        block.at[:, layers, pl.ds(8 * k, 8 * run), :],
-                        out.at[:, layers, pl.ds(tiles[3][k] - PAD, 8 * run), :],
-                        sems.at[piece, k],
-                    )
+        k = 0
+        while k < len(tiles[3]):
+            run = 1
+            while k + run < len(tiles[3]) and tiles[3][k + run] == tiles[3][k] + 8 * run:
+                run += 1
+            copies.append(
+                pltpu.make_async_copy(
+                    block.at[:, :, pl.ds(8 * k, 8 * run), :],
+                    out.at[:, :, pl.ds(tiles[3][k] - PAD, 8 * run), :],
+                    sems.at[len(copies)],
                 )
-                copies[-1].start()
-                k += run
+            )
+            copies[-1].start()
+            k += run
         for copy in copies:
             copy.wait()
 
@@ -613,7 +610,7 @@
             (4, 2, height + 2 * PAD, LANES),
             (2, height + 2 * PAD, 4 * LANES),
             (3, depth, height - 16, width),
-            pltpu.SemaphoreType.DMA((6, 4)),
+            pltpu.SemaphoreType.DMA((height // 8,)),
         ],
         far_out=1,
     )
@@ -629,7 +626,7 @@
             (4, 2, height + 2 * PAD, LANES),
             (2, height + 2 * PAD, 4 * LANES),
             (3, depth, 16, width),
-            pltpu.SemaphoreType.DMA((6, 4)),
+            pltpu.SemaphoreType.DMA((height // 8,)),
         ],
         far_out=1,
         far_in=(6,),

time: 27.8 us -> 26.9 us (0.968)
  Pallas kernels: 10.3 us -> 9.41 us
    pallas_call x8, Pallas kernels: 10.3 us -> 9.41 us  [call(): pl.pallas_call(kernel, out_shape=[jax.ShapeDtypeStruct(shape, jnp.float32...]
  transfers between devices with their start and end apart: 8 -> 8, of which waited for: 2 -> 2; matrix products, arithmetic and copies ran while one was open for 0% -> 0% of each run, Pallas kernels for 19% -> 18%
where the time goes in v8:
time: 26.9 us; the launch traced here: 26.7 us
  starting transfers between devices  11.9 us (44%)
  Pallas kernels  9.41 us (35%)
  waiting for transfers between devices  4.39 us (16%)
  local copies, waits for them, and re-layouts  0.93 us (3%)
    ppermute x8, starting transfers between devices, swap(): return lax.ppermute(part, axis, [(i, partner(i)) for i in range(count)])  11.9 us
    pallas_call x8, Pallas kernels, call(): pl.pallas_call(kernel, out_shape=[jax.ShapeDtypeStruct(shape, jnp.float32...  9.41 us
    ppermute x8, waiting for transfers between devices, swap(): return lax.ppermute(part, axis, [(i, partner(i)) for i in range(count)])  4.39 us
    unnamed x4, local copies, waits for them, and re-layouts  0.93 us
  transfers between devices with their start and end apart: 8, of which 2 were waited for; matrix products, arithmetic and copies ran while one was open for 0% of the time, Pallas kernels for 18%

profile of v8, /device:TPU:0, one launch (start us, length us, event | category | flops | bytes accessed | tf_op | source)
XLA Modules:
  0.0 26.7 jit_solution(17576080743366268390)
XLA Ops:
  0.0 0.0 copy-start.1
  0.0 0.0 copy-start
  0.0 0.7 %copy-done.1 = f32[32,128]{1,0:T(8,128)S(1)} copy-done((f32[32,128]{1,0:T(8,128)S(1)}, f32[32,128]{1,0:T(8,128)}, u32[]{:S(2)}) %copy-start.1) | copy-done | bytes 16408
  0.7 0.5 %shard_map.29 = (f32[32,128]{1,0:T(8,128)S(1)}, f32[32,128]{1,0:T(8,128)S(1)}) custom-call(f32[8,128]{1,0:T(8,128)S(1)} %shard_map.28._, f32[32,128]{1,0:T(8,128)S(1)} %copy-done.1), custom_call_target="tpu_custom_call" | custom-call | tf_op jit(solution)/shard_map/pallas_call | solution.py:519
  1.2 0.2 copy-done
  1.4 0.1 shard_map.30
  1.5 3.1 %collective-permute-start = (f32[2,2,32,128]{3,2,1,0:T(8,128)S(1)}, f32[2,2,32,128]{3,2,1,0:T(8,128)S(1)}, u32[]{:S(2)}, u32[]{:S(2)}) collective-permute-start(f32[2,2,32,128]{3,2,1,0:T(8,128)S(1)} %get-tuple-element.27), channel_id=1, source_target_pairs={{0,8},{8,0},{16,24},{24,16},{1,9},{9,1},{17,25},{25,17},{2,10},{10... | collective-permute-start | bytes 196616 | tf_op jit(solution)/shard_map/ppermute | solution.py:26
  4.6 2.5 %collective-permute-start.1 = (f32[2,2,32,128]{3,2,1,0:T(8,128)S(1)}, f32[2,2,32,128]{3,2,1,0:T(8,128)S(1)}, u32[]{:S(2)}, u32[]{:S(2)}) collective-permute-start(f32[2,2,32,128]{3,2,1,0:T(8,128)S(1)} %get-tuple-element.28), channel_id=1, source_target_pairs={{0,24},{8,16},{16,8},{24,0},{1,25},{9,17},{17,9},{25,1},{2,26},{10... | collective-permute-start | bytes 196616 | tf_op jit(solution)/shard_map/ppermute | solution.py:26
  7.1 0.1 collective-permute-start.4
  7.2 1.5 %collective-permute-start.3 = (f32[32,128]{1,0:T(8,128)S(1)}, f32[32,128]{1,0:T(8,128)S(1)}, u32[]{:S(2)}, u32[]{:S(2)}) collective-permute-start(f32[32,128]{1,0:T(8,128)S(1)} %get-tuple-element.31.rows), channel_id=1, source_target_pairs={{0,2},{1,3},{2,0},{3,1},{4,6},{5,7},{6,4},{7,5},{8,10},{9,11},{10,... | collective-permute-start | bytes 49160 | tf_op jit(solution)/shard_map/ppermute | solution.py:26
  8.7 1.5 %collective-permute-start.2 = (f32[8,128]{1,0:T(8,128)S(1)}, f32[8,128]{1,0:T(8,128)S(1)}, u32[]{:S(2)}, u32[]{:S(2)}) collective-permute-start(f32[8,128]{1,0:T(8,128)S(1)} %get-tuple-element.30), channel_id=1, source_target_pairs={{0,4},{4,0},{1,5},{5,1},{2,6},{6,2},{3,7},{7,3},{8,12},{12,8},{9,1... | collective-permute-start | bytes 12296 | tf_op jit(solution)/shard_map/ppermute | solution.py:26
  10.2 0.5 %shard_map.31 = (f32[2,32,256]{2,1,0:T(8,128)S(1)}, f32[2,4,48,128]{3,2,1,0:T(8,128)S(1)}) custom-call(f32[2,48,32,128]{3,2,1,0:T(8,128)S(1)} %copy-done), custom_call_target="tpu_custom_call" | custom-call | tf_op jit(solution)/shard_map/pallas_call | solution.py:519
  10.8 1.5 %collective-permute-done.2.column_carry = f32[8,128]{1,0:T(8,128)S(1)} collective-permute-done((f32[8,128]{1,0:T(8,128)S(1)}, f32[8,128]{1,0:T(8,128)S(1)}, u32[]{:S(2)}, u32[]{:S(2)}) %collective-permute-start.2) | collective-permute-done | bytes 4128 | tf_op jit(solution)/shard_map/ppermute | solution.py:26
  12.3 0.0 collective-permute-done.3.far_rows
  12.3 0.0 collective-permute-done.4.rest_0_
  12.3 0.0 collective-permute-done.first
  12.3 0.0 collective-permute-done.1.second
  12.3 0.1 shard_map.32
  12.5 0.1 collective-permute-start.6
  12.6 1.5 %collective-permute-start.5 = (f32[2,32,256]{2,1,0:T(8,128)S(1)}, f32[2,32,256]{2,1,0:T(8,128)S(1)}, u32[]{:S(2)}, u32[]{:S(2)}) collective-permute-start(f32[2,32,256]{2,1,0:T(8,128)S(1)} %get-tuple-element.33.packed), channel_id=1, source_target_pairs={{0,1},{1,0},{2,3},{3,2},{4,5},{5,4},{6,7},{7,6},{8,9},{9,8},{10,11... | collective-permute-start | bytes 196616 | tf_op jit(solution)/shard_map/ppermute | solution.py:26
  14.1 2.8 %collective-permute-done.6.second = f32[2,32,256]{2,1,0:T(8,128)S(1)} collective-permute-done((f32[2,32,256]{2,1,0:T(8,128)S(1)}, f32[2,32,256]{2,1,0:T(8,128)S(1)}, u32[]{:S(2)}, u32[]{:S(2)}) %collective-permute-start.6) | collective-permute-done | bytes 65568 | tf_op jit(solution)/shard_map/ppermute | solution.py:26
  16.9 0.0 collective-permute-done.5.first
  16.9 0.4 %shard_map.33 = (f32[2,32,512]{2,1,0:T(8,128)S(1)}, f32[2,32,128]{2,1,0:T(8,128)S(1)}, f32[2,4,32,128]{3,2,1,0:T(8,128)S(1)}, f32[1,240,128]{2,1,0:T(8,128)S(1)}) custom-call(f32[2,32,256]{2,1,0:T(8,128)S(1)} %get-tuple-element.33.packed, f32[2,32,256]{2,1,0:T(8,128)S(1)} %collective-permute-done.5.first, f32[2,32,256]{2,1,0:T(8,128)S(1)} %collective-permute-done.6.second, ...), custom_call_target="tpu_custom_call" | custom-call | tf_op jit(solution)/shard_map/pallas_call | solution.py:519
  17.3 1.6 %collective-permute-start.7 = (f32[240,128]{1,0:T(8,128)S(1)}, f32[240,128]{1,0:T(8,128)S(1)}, u32[]{:S(2)}, u32[]{:S(2)}) collective-permute-start(f32[240,128]{1,0:T(8,128)S(1)} %bitcast.1), channel_id=1, source_target_pairs={{0,4},{4,0},{1,5},{5,1},{2,6},{6,2},{3,7},{7,3},{8,12},{12,8},{9,1... | collective-permute-start | bytes 368648 | tf_op jit(solution)/shard_map/ppermute | solution.py:26
  18.9 4.3 %shard_map.34 = (f32[2,52,48,128]{3,2,1,0:T(8,128)S(1)}, f32[3,52,48,128]{3,2,1,0:T(8,128)S(1)}, f32[3,52,48,128]{3,2,1,0:T(8,128)S(1)}, f32[3,48,32,128]{3,2,1,0:T(8,128)}) custom-call(f32[2,48,32,128]{3,2,1,0:T(8,128)S(1)} %copy-done, f32[2,32,128]{2,1,0:T(8,128)S(1)} %get-tuple-element.40.flat, f32[2,4,32,128]{3,2,1,0:T(8,128)S(1)} %get-tuple-element.41.ext, ...), custom_call_target="tpu_custom_call" | custom-call | tf_op jit(solution)/shard_map/pallas_call | solution.py:519
  23.2 0.0 collective-permute-done.7.first.second
  23.2 3.5 %shard_map.35 = (f32[2,52,48,128]{3,2,1,0:T(8,128)S(1)}, f32[3,52,48,128]{3,2,1,0:T(8,128)S(1)}, f32[3,52,48,128]{3,2,1,0:T(8,128)S(1)}, f32[3,48,32,128]{3,2,1,0:T(8,128)}) custom-call(f32[2,32,512]{2,1,0:T(8,128)S(1)} %get-tuple-element.38.strips, ...), custom_call_target="tpu_custom_call", output_to_operand_aliasing={{0}: (3, {}), {1}: (4, {}), {2}: (5, {}), {3}: (6, {})} | custom-call | tf_op jit(solution)/shard_map/pallas_call | solution.py:519
  (1 shorter events, 0.0 us)
Async XLA Ops:
  0.0 0.7 %copy-start.1 = (f32[32,128]{1,0:T(8,128)S(1)}, f32[32,128]{1,0:T(8,128)}, u32[]{:S(2)}) copy-start(f32[32,128]{1,0:T(8,128)} %refs_0_.1) | copy-start | bytes 49156
  0.0 1.4 %copy-start = (f32[2,48,32,128]{3,2,1,0:T(8,128)S(1)}, f32[2,48,32,128]{3,2,1,0:T(8,128)}, u32[]{:S(2)}) copy-start(f32[2,48,32,128]{3,2,1,0:T(8,128)} %side.5) | copy-start | bytes 4718596
  1.5 10.8 %collective-permute-start = (f32[2,2,32,128]{3,2,1,0:T(8,128)S(1)}, f32[2,2,32,128]{3,2,1,0:T(8,128)S(1)}, u32[]{:S(2)}, u32[]{:S(2)}) collective-permute-start(f32[2,2,32,128]{3,2,1,0:T(8,128)S(1)} %get-tuple-element.27), channel_id=1, source_target_pairs={{0,8},{8,0},{16,24},{24,16},{1,9},{9,1},{17,25},{25,17},{2,10},{10... | collective-permute-start | bytes 196616 | tf_op jit(solution)/shard_map/ppermute | solution.py:26
  4.6 7.7 %collective-permute-start.1 = (f32[2,2,32,128]{3,2,1,0:T(8,128)S(1)}, f32[2,2,32,128]{3,2,1,0:T(8,128)S(1)}, u32[]{:S(2)}, u32[]{:S(2)}) collective-permute-start(f32[2,2,32,128]{3,2,1,0:T(8,128)S(1)} %get-tuple-element.28), channel_id=1, source_target_pairs={{0,24},{8,16},{16,8},{24,0},{1,25},{9,17},{17,9},{25,1},{2,26},{10... | collective-permute-start | bytes 196616 | tf_op jit(solution)/shard_map/ppermute | solution.py:26
  7.1 5.2 %collective-permute-start.4 = (f32[2,32,128]{2,1,0:T(8,128)S(1)}, f32[2,32,128]{2,1,0:T(8,128)S(1)}, u32[]{:S(2)}, u32[]{:S(2)}) collective-permute-start(f32[2,32,128]{2,1,0:T(8,128)S(1)} %get-tuple-element.29.total), channel_id=1, source_target_pairs={{0,16},{8,24},{16,0},{24,8},{1,17},{9,25},{17,1},{25,9},{2,18},{10... | collective-permute-start | bytes 98312 | tf_op jit(solution)/shard_map/ppermute | solution.py:26
  7.2 5.1 %collective-permute-start.3 = (f32[32,128]{1,0:T(8,128)S(1)}, f32[32,128]{1,0:T(8,128)S(1)}, u32[]{:S(2)}, u32[]{:S(2)}) collective-permute-start(f32[32,128]{1,0:T(8,128)S(1)} %get-tuple-element.31.rows), channel_id=1, source_target_pairs={{0,2},{1,3},{2,0},{3,1},{4,6},{5,7},{6,4},{7,5},{8,10},{9,11},{10,... | collective-permute-start | bytes 49160 | tf_op jit(solution)/shard_map/ppermute | solution.py:26
  8.7 3.6 %collective-permute-start.2 = (f32[8,128]{1,0:T(8,128)S(1)}, f32[8,128]{1,0:T(8,128)S(1)}, u32[]{:S(2)}, u32[]{:S(2)}) collective-permute-start(f32[8,128]{1,0:T(8,128)S(1)} %get-tuple-element.30), channel_id=1, source_target_pairs={{0,4},{4,0},{1,5},{5,1},{2,6},{6,2},{3,7},{7,3},{8,12},{12,8},{9,1... | collective-permute-start | bytes 12296 | tf_op jit(solution)/shard_map/ppermute | solution.py:26
  12.5 4.4 %collective-permute-start.6 = (f32[2,32,256]{2,1,0:T(8,128)S(1)}, f32[2,32,256]{2,1,0:T(8,128)S(1)}, u32[]{:S(2)}, u32[]{:S(2)}) collective-permute-start(f32[2,32,256]{2,1,0:T(8,128)S(1)} %get-tuple-element.33.packed), channel_id=1, source_target_pairs={{0,3},{1,2},{2,1},{3,0},{4,7},{5,6},{6,5},{7,4},{8,11},{9,10},{10,... | collective-permute-start | bytes 196616 | tf_op jit(solution)/shard_map/ppermute | solution.py:26
  12.6 4.3 %collective-permute-start.5 = (f32[2,32,256]{2,1,0:T(8,128)S(1)}, f32[2,32,256]{2,1,0:T(8,128)S(1)}, u32[]{:S(2)}, u32[]{:S(2)}) collective-permute-start(f32[2,32,256]{2,1,0:T(8,128)S(1)} %get-tuple-element.33.packed), channel_id=1, source_target_pairs={{0,1},{1,0},{2,3},{3,2},{4,5},{5,4},{6,7},{7,6},{8,9},{9,8},{10,11... | collective-permute-start | bytes 196616 | tf_op jit(solution)/shard_map/ppermute | solution.py:26
  17.3 5.9 %collective-permute-start.7 = (f32[240,128]{1,0:T(8,128)S(1)}, f32[240,128]{1,0:T(8,128)S(1)}, u32[]{:S(2)}, u32[]{:S(2)}) collective-permute-start(f32[240,128]{1,0:T(8,128)S(1)} %bitcast.1), channel_id=1, source_target_pairs={{0,4},{4,0},{1,5},{5,1},{2,6},{6,2},{3,7},{7,3},{8,12},{12,8},{9,1... | collective-permute-start | bytes 368648 | tf_op jit(solution)/shard_map/ppermute | solution.py:26

commit v9 on v8

--- a/solution.py
+++ b/solution.py
@@ -143,7 +143,7 @@
         if c == 0:
             shared = 0.5 * rows[...] - carry
         else:
-            before = jnp.where(y > 0, column_carry[7:8, :], 0.0)
+            before = jnp.where(y > 0, column_carry[...][7:8, :], 0.0)
             shared = carry - 0.5 * (columns[...] + before)
         layers = (low[0] - low[1], None, total[c] + high[0], total[c] + high[1])
         flat_out[c] = shared
@@ -230,25 +230,26 @@
     slots = slot_rows(depth)
     for message in range(y_out.shape[0]):
         downward = (y % 2 == 1) if message == 0 else (y % 2 == 0)
+
+        def edge_row(values, r):
+            return jnp.where(downward, values[r : r + 1], values[height - 2 + r : height - 1 + r])
+
         for c in range(2):
             for r in range(2):
                 start = (c * 2 + r) * slots
-                low, high = pl.ds(r, 1), pl.ds(height - 2 + r, 1)
-                flat = jnp.where(downward, flat_out[c, low, :], flat_out[c, high, :])
+                flat = edge_row(flat_out[c], r)
                 edge = jnp.where(downward, edges[1 - c, r], edges[1 - c, 2 + r])
                 edge = edge if c == 0 else -edge
                 y_out[message, pl.ds(start + 2, depth), :] = flat + edge
                 for k, at in enumerate((0, 1, depth + 2, depth + 3)):
-                    y_out[message, pl.ds(start + at, 1), :] = jnp.where(
-                        downward, ext_out[c, k, low, :], ext_out[c, k, high, :]
-                    )
+                    y_out[message, pl.ds(start + at, 1), :] = edge_row(ext_out[c, k], r)
             for tile in range(4):
                 start = 4 * slots + (c * 4 + tile) * 2
                 lanes = pl.ds(tile * LANES, LANES)
                 y_out[message, pl.ds(start, 2), :] = jnp.where(
                     downward,
-                    strips_out[c, pl.ds(0, 2), lanes],
-                    strips_out[c, pl.ds(height - 2, 2), lanes],
+                    strips_out[c, pl.ds(0, 8), lanes][:2],
+                    strips_out[c, pl.ds(height - 8, 8), lanes][6:],
                 )
 
 
@@ -406,7 +407,7 @@
             @pl.when(jnp.logical_not(exists))
             def _():
                 for c in range(3):
-                    flat_later = self.later.at[c].reshape((depth + 4) * self.padded, LANES)
+                    flat_later = self.later.at[c].reshape(self.later.shape[1] * self.padded, LANES)
                     flat_later[pl.ds(row, depth + 4, stride=self.padded), :] = line
 
     def run(self, tiles, rows, out, block, sems):
@@ -497,7 +498,7 @@
             return jnp.where(exists, value, 0.0)
 
         for c in range(2):
-            flat_state = state.at[c].reshape(layers * padded, LANES)
+            flat_state = state.at[c].reshape(state.shape[1] * padded, LANES)
             for r in range(2):
                 flat_state[pl.ds(row + r, layers, stride=padded), :] = received(
                     pl.ds((c * 2 + r) * slots, layers)
@@ -587,7 +588,7 @@
     first = swap_first(packed, "gx")
     second = swap_second(packed, "gx") if count_x > 2 else first
     messages = 1 if count_y == 2 else 2
-    message_rows = 4 * slot_rows(depth) + 16
+    message_rows = 4 * slot_rows(depth) + 24
     strips, flat, ext, edge_rows = call(
         functools.partial(x_kernel, counts, depth),
         [(2, height, 4 * LANES), block, (2, 4) + plane, (messages, message_rows, width)],
@@ -601,7 +602,7 @@
 
 def inner_steps(counts, side, flat, ext, strips):
     _, depth, height, width = side.shape
-    grid = (depth + 4, height + 2 * PAD, width)
+    grid = (slot_rows(depth), height + 2 * PAD, width)
     return call(
         functools.partial(inner_kernel, counts),
         [(2,) + grid, (3,) + grid, (3,) + grid, (3, depth, height, width)],

time: 26.9 us -> 26.9 us (level)
  no operation moved by 1% of the time
where the time goes in v9:
time: 26.9 us; the launch traced here: 26.7 us
  starting transfers between devices  11.9 us (44%)
  Pallas kernels  9.4 us (35%)
  waiting for transfers between devices  4.39 us (16%)
  local copies, waits for them, and re-layouts  0.93 us (3%)
    ppermute x8, starting transfers between devices, swap(): return lax.ppermute(part, axis, [(i, partner(i)) for i in range(count)])  11.9 us
    pallas_call x8, Pallas kernels, call(): pl.pallas_call(kernel, out_shape=[jax.ShapeDtypeStruct(shape, jnp.float32...  9.4 us
    ppermute x8, waiting for transfers between devices, swap(): return lax.ppermute(part, axis, [(i, partner(i)) for i in range(count)])  4.39 us
    unnamed x4, local copies, waits for them, and re-layouts  0.93 us
  transfers between devices with their start and end apart: 8, of which 2 were waited for; matrix products, arithmetic and copies ran while one was open for 0% of the time, Pallas kernels for 18%

profile of v9, /device:TPU:0, one launch (start us, length us, event | category | flops | bytes accessed | tf_op | source)
XLA Modules:
  0.0 26.7 jit_solution(393366124517793503)
XLA Ops:
  0.0 0.0 copy-start.1
  0.0 0.0 copy-start
  0.0 0.7 %copy-done.1 = f32[32,128]{1,0:T(8,128)S(1)} copy-done((f32[32,128]{1,0:T(8,128)S(1)}, f32[32,128]{1,0:T(8,128)}, u32[]{:S(2)}) %copy-start.1) | copy-done | bytes 16408
  0.7 0.5 %shard_map.29 = (f32[32,128]{1,0:T(8,128)S(1)}, f32[32,128]{1,0:T(8,128)S(1)}) custom-call(f32[8,128]{1,0:T(8,128)S(1)} %shard_map.28._, f32[32,128]{1,0:T(8,128)S(1)} %copy-done.1), custom_call_target="tpu_custom_call" | custom-call | tf_op jit(solution)/shard_map/pallas_call | solution.py:520
  1.2 0.2 copy-done
  1.4 0.1 shard_map.30
  1.5 3.1 %collective-permute-start = (f32[2,2,32,128]{3,2,1,0:T(8,128)S(1)}, f32[2,2,32,128]{3,2,1,0:T(8,128)S(1)}, u32[]{:S(2)}, u32[]{:S(2)}) collective-permute-start(f32[2,2,32,128]{3,2,1,0:T(8,128)S(1)} %get-tuple-element.27), channel_id=1, source_target_pairs={{0,8},{8,0},{16,24},{24,16},{1,9},{9,1},{17,25},{25,17},{2,10},{10... | collective-permute-start | bytes 196616 | tf_op jit(solution)/shard_map/ppermute | solution.py:26
  4.6 2.5 %collective-permute-start.1 = (f32[2,2,32,128]{3,2,1,0:T(8,128)S(1)}, f32[2,2,32,128]{3,2,1,0:T(8,128)S(1)}, u32[]{:S(2)}, u32[]{:S(2)}) collective-permute-start(f32[2,2,32,128]{3,2,1,0:T(8,128)S(1)} %get-tuple-element.28), channel_id=1, source_target_pairs={{0,24},{8,16},{16,8},{24,0},{1,25},{9,17},{17,9},{25,1},{2,26},{10... | collective-permute-start | bytes 196616 | tf_op jit(solution)/shard_map/ppermute | solution.py:26
  7.1 0.1 collective-permute-start.4
  7.2 1.5 %collective-permute-start.3 = (f32[32,128]{1,0:T(8,128)S(1)}, f32[32,128]{1,0:T(8,128)S(1)}, u32[]{:S(2)}, u32[]{:S(2)}) collective-permute-start(f32[32,128]{1,0:T(8,128)S(1)} %get-tuple-element.31.rows), channel_id=1, source_target_pairs={{0,2},{1,3},{2,0},{3,1},{4,6},{5,7},{6,4},{7,5},{8,10},{9,11},{10,... | collective-permute-start | bytes 49160 | tf_op jit(solution)/shard_map/ppermute | solution.py:26
  8.7 1.5 %collective-permute-start.2 = (f32[8,128]{1,0:T(8,128)S(1)}, f32[8,128]{1,0:T(8,128)S(1)}, u32[]{:S(2)}, u32[]{:S(2)}) collective-permute-start(f32[8,128]{1,0:T(8,128)S(1)} %get-tuple-element.30), channel_id=1, source_target_pairs={{0,4},{4,0},{1,5},{5,1},{2,6},{6,2},{3,7},{7,3},{8,12},{12,8},{9,1... | collective-permute-start | bytes 12296 | tf_op jit(solution)/shard_map/ppermute | solution.py:26
  10.2 0.5 %shard_map.31 = (f32[2,32,256]{2,1,0:T(8,128)S(1)}, f32[2,4,48,128]{3,2,1,0:T(8,128)S(1)}) custom-call(f32[2,48,32,128]{3,2,1,0:T(8,128)S(1)} %copy-done), custom_call_target="tpu_custom_call" | custom-call | tf_op jit(solution)/shard_map/pallas_call | solution.py:520
  10.8 1.5 %collective-permute-done.2.column_carry = f32[8,128]{1,0:T(8,128)S(1)} collective-permute-done((f32[8,128]{1,0:T(8,128)S(1)}, f32[8,128]{1,0:T(8,128)S(1)}, u32[]{:S(2)}, u32[]{:S(2)}) %collective-permute-start.2) | collective-permute-done | bytes 4128 | tf_op jit(solution)/shard_map/ppermute | solution.py:26
  12.3 0.0 collective-permute-done.3.far_rows
  12.3 0.0 collective-permute-done.4.rest_0_
  12.3 0.0 collective-permute-done.first
  12.3 0.0 collective-permute-done.1.second
  12.3 0.1 shard_map.32
  12.5 0.1 collective-permute-start.6
  12.6 1.5 %collective-permute-start.5 = (f32[2,32,256]{2,1,0:T(8,128)S(1)}, f32[2,32,256]{2,1,0:T(8,128)S(1)}, u32[]{:S(2)}, u32[]{:S(2)}) collective-permute-start(f32[2,32,256]{2,1,0:T(8,128)S(1)} %get-tuple-element.33.packed), channel_id=1, source_target_pairs={{0,1},{1,0},{2,3},{3,2},{4,5},{5,4},{6,7},{7,6},{8,9},{9,8},{10,11... | collective-permute-start | bytes 196616 | tf_op jit(solution)/shard_map/ppermute | solution.py:26
  14.1 2.8 %collective-permute-done.6.second = f32[2,32,256]{2,1,0:T(8,128)S(1)} collective-permute-done((f32[2,32,256]{2,1,0:T(8,128)S(1)}, f32[2,32,256]{2,1,0:T(8,128)S(1)}, u32[]{:S(2)}, u32[]{:S(2)}) %collective-permute-start.6) | collective-permute-done | bytes 65568 | tf_op jit(solution)/shard_map/ppermute | solution.py:26
  16.9 0.0 collective-permute-done.5.first
  16.9 0.4 %shard_map.33 = (f32[2,32,512]{2,1,0:T(8,128)S(1)}, f32[2,32,128]{2,1,0:T(8,128)S(1)}, f32[2,4,32,128]{3,2,1,0:T(8,128)S(1)}, f32[1,248,128]{2,1,0:T(8,128)S(1)}) custom-call(f32[2,32,256]{2,1,0:T(8,128)S(1)} %get-tuple-element.33.packed, f32[2,32,256]{2,1,0:T(8,128)S(1)} %collective-permute-done.5.first, f32[2,32,256]{2,1,0:T(8,128)S(1)} %collective-permute-done.6.second, ...), custom_call_target="tpu_custom_call" | custom-call | tf_op jit(solution)/shard_map/pallas_call | solution.py:520
  17.3 1.6 %collective-permute-start.7 = (f32[248,128]{1,0:T(8,128)S(1)}, f32[248,128]{1,0:T(8,128)S(1)}, u32[]{:S(2)}, u32[]{:S(2)}) collective-permute-start(f32[248,128]{1,0:T(8,128)S(1)} %bitcast.1), channel_id=1, source_target_pairs={{0,4},{4,0},{1,5},{5,1},{2,6},{6,2},{3,7},{7,3},{8,12},{12,8},{9,1... | collective-permute-start | bytes 380936 | tf_op jit(solution)/shard_map/ppermute | solution.py:26
  18.9 4.3 %shard_map.34 = (f32[2,56,48,128]{3,2,1,0:T(8,128)S(1)}, f32[3,56,48,128]{3,2,1,0:T(8,128)S(1)}, f32[3,56,48,128]{3,2,1,0:T(8,128)S(1)}, f32[3,48,32,128]{3,2,1,0:T(8,128)}) custom-call(f32[2,48,32,128]{3,2,1,0:T(8,128)S(1)} %copy-done, f32[2,32,128]{2,1,0:T(8,128)S(1)} %get-tuple-element.40.flat, f32[2,4,32,128]{3,2,1,0:T(8,128)S(1)} %get-tuple-element.41.ext, ...), custom_call_target="tpu_custom_call" | custom-call | tf_op jit(solution)/shard_map/pallas_call | solution.py:520
  23.2 0.0 collective-permute-done.7.first.second
  23.2 3.5 %shard_map.35 = (f32[2,56,48,128]{3,2,1,0:T(8,128)S(1)}, f32[3,56,48,128]{3,2,1,0:T(8,128)S(1)}, f32[3,56,48,128]{3,2,1,0:T(8,128)S(1)}, f32[3,48,32,128]{3,2,1,0:T(8,128)}) custom-call(f32[2,32,512]{2,1,0:T(8,128)S(1)} %get-tuple-element.38.strips, ...), custom_call_target="tpu_custom_call", output_to_operand_aliasing={{0}: (3, {}), {1}: (4, {}), {2}: (5, {}), {3}: (6, {})} | custom-call | tf_op jit(solution)/shard_map/pallas_call | solution.py:520
  (1 shorter events, 0.0 us)
Async XLA Ops:
  0.0 0.7 %copy-start.1 = (f32[32,128]{1,0:T(8,128)S(1)}, f32[32,128]{1,0:T(8,128)}, u32[]{:S(2)}) copy-start(f32[32,128]{1,0:T(8,128)} %refs_0_.1) | copy-start | bytes 49156
  0.0 1.4 %copy-start = (f32[2,48,32,128]{3,2,1,0:T(8,128)S(1)}, f32[2,48,32,128]{3,2,1,0:T(8,128)}, u32[]{:S(2)}) copy-start(f32[2,48,32,128]{3,2,1,0:T(8,128)} %side.5) | copy-start | bytes 4718596
  1.5 10.8 %collective-permute-start = (f32[2,2,32,128]{3,2,1,0:T(8,128)S(1)}, f32[2,2,32,128]{3,2,1,0:T(8,128)S(1)}, u32[]{:S(2)}, u32[]{:S(2)}) collective-permute-start(f32[2,2,32,128]{3,2,1,0:T(8,128)S(1)} %get-tuple-element.27), channel_id=1, source_target_pairs={{0,8},{8,0},{16,24},{24,16},{1,9},{9,1},{17,25},{25,17},{2,10},{10... | collective-permute-start | bytes 196616 | tf_op jit(solution)/shard_map/ppermute | solution.py:26
  4.6 7.7 %collective-permute-start.1 = (f32[2,2,32,128]{3,2,1,0:T(8,128)S(1)}, f32[2,2,32,128]{3,2,1,0:T(8,128)S(1)}, u32[]{:S(2)}, u32[]{:S(2)}) collective-permute-start(f32[2,2,32,128]{3,2,1,0:T(8,128)S(1)} %get-tuple-element.28), channel_id=1, source_target_pairs={{0,24},{8,16},{16,8},{24,0},{1,25},{9,17},{17,9},{25,1},{2,26},{10... | collective-permute-start | bytes 196616 | tf_op jit(solution)/shard_map/ppermute | solution.py:26
  7.1 5.2 %collective-permute-start.4 = (f32[2,32,128]{2,1,0:T(8,128)S(1)}, f32[2,32,128]{2,1,0:T(8,128)S(1)}, u32[]{:S(2)}, u32[]{:S(2)}) collective-permute-start(f32[2,32,128]{2,1,0:T(8,128)S(1)} %get-tuple-element.29.total), channel_id=1, source_target_pairs={{0,16},{8,24},{16,0},{24,8},{1,17},{9,25},{17,1},{25,9},{2,18},{10... | collective-permute-start | bytes 98312 | tf_op jit(solution)/shard_map/ppermute | solution.py:26
  7.2 5.1 %collective-permute-start.3 = (f32[32,128]{1,0:T(8,128)S(1)}, f32[32,128]{1,0:T(8,128)S(1)}, u32[]{:S(2)}, u32[]{:S(2)}) collective-permute-start(f32[32,128]{1,0:T(8,128)S(1)} %get-tuple-element.31.rows), channel_id=1, source_target_pairs={{0,2},{1,3},{2,0},{3,1},{4,6},{5,7},{6,4},{7,5},{8,10},{9,11},{10,... | collective-permute-start | bytes 49160 | tf_op jit(solution)/shard_map/ppermute | solution.py:26
  8.7 3.6 %collective-permute-start.2 = (f32[8,128]{1,0:T(8,128)S(1)}, f32[8,128]{1,0:T(8,128)S(1)}, u32[]{:S(2)}, u32[]{:S(2)}) collective-permute-start(f32[8,128]{1,0:T(8,128)S(1)} %get-tuple-element.30), channel_id=1, source_target_pairs={{0,4},{4,0},{1,5},{5,1},{2,6},{6,2},{3,7},{7,3},{8,12},{12,8},{9,1... | collective-permute-start | bytes 12296 | tf_op jit(solution)/shard_map/ppermute | solution.py:26
  12.5 4.4 %collective-permute-start.6 = (f32[2,32,256]{2,1,0:T(8,128)S(1)}, f32[2,32,256]{2,1,0:T(8,128)S(1)}, u32[]{:S(2)}, u32[]{:S(2)}) collective-permute-start(f32[2,32,256]{2,1,0:T(8,128)S(1)} %get-tuple-element.33.packed), channel_id=1, source_target_pairs={{0,3},{1,2},{2,1},{3,0},{4,7},{5,6},{6,5},{7,4},{8,11},{9,10},{10,... | collective-permute-start | bytes 196616 | tf_op jit(solution)/shard_map/ppermute | solution.py:26
  12.6 4.3 %collective-permute-start.5 = (f32[2,32,256]{2,1,0:T(8,128)S(1)}, f32[2,32,256]{2,1,0:T(8,128)S(1)}, u32[]{:S(2)}, u32[]{:S(2)}) collective-permute-start(f32[2,32,256]{2,1,0:T(8,128)S(1)} %get-tuple-element.33.packed), channel_id=1, source_target_pairs={{0,1},{1,0},{2,3},{3,2},{4,5},{5,4},{6,7},{7,6},{8,9},{9,8},{10,11... | collective-permute-start | bytes 196616 | tf_op jit(solution)/shard_map/ppermute | solution.py:26
  17.3 5.9 %collective-permute-start.7 = (f32[248,128]{1,0:T(8,128)S(1)}, f32[248,128]{1,0:T(8,128)S(1)}, u32[]{:S(2)}, u32[]{:S(2)}) collective-permute-start(f32[248,128]{1,0:T(8,128)S(1)} %bitcast.1), channel_id=1, source_target_pairs={{0,4},{4,0},{1,5},{5,1},{2,6},{6,2},{3,7},{7,3},{8,12},{12,8},{9,1... | collective-permute-start | bytes 380936 | tf_op jit(solution)/shard_map/ppermute | solution.py:26
